TPU v7x, 1024 devices: a whole 4x8x16 slice. The times are simulated.
1024 devices in a mesh: group: 16 (over z), local: 64 (over y, x, core).
Axes of the slice: x: 4, y: 8, z: 16, core: 2. Of those that a mesh axis runs over, the one named last changes fastest.
Arguments:
- grad_out: bfloat16 [2048, 7168], P('group', 'local'), may hold values from -4 to 4
- routes: int32 [2048, 8], P('group'), may hold values from 0 to 127, as said below
- slots: int32 [2048, 8], P('group'), may hold values from 0 to 15, as said below
- gates: bfloat16 [2048, 8], P('group'), may hold values from 0.049804688 to 0.59765625
- w_down: bfloat16 [1024, 1024, 896], P(('group', 'local')), may hold values from -0.1875 to 0.1875
- saved_gate: bfloat16 [1024, 256, 128], P(('group', 'local')), may hold values from -5 to 5
- saved_up: bfloat16 [1024, 256, 128], P(('group', 'local')), may hold values from -5 to 5
Outputs:
- grad_gate_pre: bfloat16 [1024, 256, 128], P(('group', 'local'))
- grad_up_pre: bfloat16 [1024, 256, 128], P(('group', 'local'))
- grad_gates: float32 [2048, 8], P('group')
Inputs may be any that keep to these rules, and one draw needn't show every extreme that they name: `routes`: each row names 8 different experts that lie in at most 4 groups of 8 consecutive experts. Among the tokens of one group index, no expert is named more than 16 times, and one expert is named exactly 16 times by the tokens of every group index. For one group index and one expert, the slots of the routes that name it are distinct and run from 0 without gaps.
All inputs are finite; a program needn't handle non-finite values.
Results may differ from a plain program's by a relative error of at most 0.0014.
Values may be sent and summed in bfloat16 or wider, within the bound.
No kernel may reach another device: no remote copies, remote signals or barrier semaphores. Data moves between devices by JAX's collectives and lax.ppermute only.
A program may use at most 32 MiB of HBM per device.

v0:
```python
import jax
import jax.numpy as jnp
from jax import lax
from jax.sharding import PartitionSpec as P

EXP_GRP = 8


def swapped(shard, axis, bit):
    return lax.ppermute(shard, axis, [(i, i ^ 1 << bit) for i in range(lax.axis_size(axis))])


def shards(grad_out, routes, slots, gates, w_down, saved_gate, saved_up):
    group_count = lax.axis_size("group")
    local_count = lax.axis_size("local")
    shard_count = local_count // EXP_GRP
    shard_bits = shard_count.bit_length() - 1
    expert_bits = EXP_GRP.bit_length() - 1
    tok_count, col_width = grad_out.shape
    route_count = routes.shape[1]
    capacity = saved_gate.shape[1]
    slot_count = capacity // group_count
    hidden_share = saved_gate.shape[2]
    local_index = lax.axis_index("local")
    expert_index = local_index % EXP_GRP
    shard_index = local_index // EXP_GRP
    group_slots = EXP_GRP * slot_count
    total_slots = group_count * group_slots
    flat_target = (routes // EXP_GRP * group_slots + routes % EXP_GRP * slot_count + slots).reshape(
        -1
    )
    token_ids = jnp.repeat(jnp.arange(tok_count, dtype=jnp.int32), route_count)
    source = jnp.full((total_slots,), tok_count, jnp.int32).at[flat_target].set(token_ids)
    slot_gate = jnp.zeros((total_slots,), jnp.bfloat16).at[flat_target].set(gates.reshape(-1))
    padded = jnp.concatenate([grad_out, jnp.zeros((1, col_width), grad_out.dtype)], axis=0)
    send_rows = padded[source].reshape(group_count, group_slots, col_width)
    send_gates = slot_gate.reshape(group_count, group_slots)
    recv_rows, recv_gates = (
        lax.all_to_all(send_rows, "group", split_axis=0, concat_axis=0, tiled=True),
        lax.all_to_all(send_gates, "group", split_axis=0, concat_axis=0, tiled=True),
    )
    group_rows = jnp.transpose(
        recv_rows.reshape(group_count, EXP_GRP, slot_count, col_width), (1, 0, 2, 3)
    )
    own_gates = lax.dynamic_slice_in_dim(
        recv_gates.reshape(group_count, EXP_GRP, slot_count), expert_index, 1, 1
    )
    expert_gates = own_gates.reshape(capacity).astype(jnp.float32)
    pieces = group_rows.reshape((2,) * expert_bits + (capacity, col_width))
    for bit_level in range(expert_bits):
        axis_pos = expert_bits - 1 - bit_level
        own_bit = expert_index >> bit_level & 1
        kept_half = lax.dynamic_slice_in_dim(pieces, own_bit, 1, axis_pos)
        given_half = lax.dynamic_slice_in_dim(pieces, 1 - own_bit, 1, axis_pos)
        received_half = swapped(given_half, "local", bit_level)
        pieces = jnp.where(
            own_bit == 0,
            jnp.concatenate([kept_half, received_half], axis_pos),
            jnp.concatenate([received_half, kept_half], axis_pos),
        )
    expert_rows = jnp.transpose(pieces.reshape(EXP_GRP, capacity, col_width), (1, 0, 2)).reshape(
        capacity, EXP_GRP * col_width
    )
    weight_view = w_down[0].reshape(shard_count, hidden_share, w_down.shape[2])
    partial_value = jnp.einsum(
        "cd,shd->sch", expert_rows, weight_view, preferred_element_type=jnp.float32
    )
    halves = partial_value.reshape((2,) * shard_bits + (capacity, hidden_share))
    bit_order = list(reversed(range(shard_bits)))
    for bit_level in bit_order:
        axis_pos = shard_bits - 1 - bit_level
        own_bit = shard_index >> bit_level & 1
        kept_half = lax.dynamic_slice_in_dim(halves, own_bit, 1, axis_pos)
        given_half = lax.dynamic_slice_in_dim(halves, 1 - own_bit, 1, axis_pos)
        halves = kept_half + swapped(given_half, "local", bit_level + expert_bits)
    hidden_grad = halves.reshape(capacity, hidden_share)
    gate_pre = saved_gate[0].astype(jnp.float32)
    up_pre = saved_up[0].astype(jnp.float32)
    sigmoid_gate = jax.nn.sigmoid(gate_pre)
    hidden = gate_pre * sigmoid_gate * up_pre
    route_part = jnp.sum(hidden_grad * hidden, axis=1)
    scaled = expert_gates[:, None] * hidden_grad
    grad_up = (scaled * gate_pre * sigmoid_gate).astype(jnp.bfloat16)
    grad_gate = (scaled * up_pre * sigmoid_gate * (1.0 + gate_pre * (1.0 - sigmoid_gate))).astype(
        jnp.bfloat16
    )
    expert_rows_ids = jnp.arange(EXP_GRP, dtype=jnp.int32)
    table = jnp.where(expert_rows_ids[:, None] == expert_index, route_part[None, :], 0.0)
    terms = lax.psum(table, "local")
    home_terms = lax.all_to_all(
        terms.reshape(EXP_GRP, group_count, slot_count),
        "group",
        split_axis=1,
        concat_axis=1,
        tiled=True,
    )
    flat_index = (
        routes % EXP_GRP * (group_count * slot_count) + routes // EXP_GRP * slot_count + slots
    )
    grad_gates = home_terms.reshape(-1)[flat_index]
    return (grad_gate[None], grad_up[None], grad_gates)


def solution(mesh):
    return jax.shard_map(
        shards,
        mesh=mesh,
        in_specs=(
            P("group", "local"),
            P("group", None),
            P("group", None),
            P("group", None),
            P(("group", "local"), None, None),
            P(("group", "local"), None, None),
            P(("group", "local"), None, None),
        ),
        out_specs=(
            P(("group", "local"), None, None),
            P(("group", "local"), None, None),
            P("group", None),
        ),
        check_vma=False,
    )
```

profile of v0, /device:TPU:1, one launch (start us, length us, event | category | flops | bytes accessed | tf_op | source)
XLA Modules:
  0.0 417.9 jit_solution(7542819363368851388)
XLA Ops:
  0.6 1.0 copy.48
  1.6 0.7 compare_select_fusion.2
  2.7 4.3 %scatter_custom_fusion.1 = s32[2048]{0:T(1024)S(1)} fusion(s32[1024]{0:T(1024)S(1)} %bitcast.67, s32[1024]{0:T(1024)S(1)} %reshape.181, s32[]{:T(128)} %constant.74.clone.1), kind=kCustom, calls=%fused_computation.44 | custom fusion | bytes 8196 | tf_op jit(solution)/shard_map/scatter | solution.py:33
  7.0 6.2 %gather_fusion = bf16[2048,112]{1,0:T(8,128)(2,1)S(1)} fusion(bf16[129,112]{1,0:T(8,128)(2,1)S(1)} %concatenate.21, s32[2048]{0:T(1024)S(1)} %fusion.17), kind=kCustom, calls=%fused_computation | custom fusion | bytes 925696 | tf_op jit(solution)/shard_map/gather | solution.py:36
  13.2 1.0 copy.49
  14.2 19.4 %all-to-all-start.1 = ((bf16[16,128,112]{1,2,0:T(8,128)(2,1)}), bf16[16,128,112]{1,2,0:T(8,128)(2,1)S(1)}, u32[]{:S(2)}, u32[]{:S(2)}) async-start(bf16[16,128,112]{1,2,0:T(8,128)(2,1)} %copy.49), calls=%async_computation.1 | async-start | bytes 917504 | tf_op jit(solution)/shard_map/all_to_all | solution.py:39
  33.7 20.8 %all-to-all-done.1 = bf16[16,128,112]{1,2,0:T(8,128)(2,1)S(1)} async-done(((bf16[16,128,112]{1,2,0:T(8,128)(2,1)}), bf16[16,128,112]{1,2,0:T(8,128)(2,1)S(1)}, u32[]{:S(2)}, u32[]{:S(2)}) %all-to-all-start.1) | async-done | bytes 458784 | tf_op jit(solution)/shard_map/all_to_all | solution.py:39
  54.9 8.8 %collective-permute-start = (bf16[2,2,1,256,112]{4,3,2,1,0:T(8,128)(2,1)S(1)}, bf16[2,2,1,256,112]{4,3,2,1,0:T(8,128)(2,1)S(1)}, u32[]{:S(2)}, u32[]{:S(2)}) collective-permute-start(bf16[2,2,1,256,112]{4,3,2,1,0:T(8,128)(2,1)S(1)} %get-tuple-element.24), channel_id=1, source_target_pairs={{0,1},{1,0},{2,3},{3,2},{4,5},{5,4},{6,7},{7,6},{8,9},{9,8},{10,11... | collective-permute-start | bytes 688136 | tf_op jit(solution)/shard_map/ppermute | solution.py:10
  63.7 1.1 collective-permute-done
  65.0 3.1 collective-permute-start.1
  68.2 6.3 %collective-permute-done.1 = bf16[2,1,2,256,112]{4,3,2,1,0:T(8,128)(2,1)S(1)} collective-permute-done((bf16[2,1,2,256,112]{4,3,2,1,0:T(8,128)(2,1)S(1)}, bf16[2,1,2,256,112]{4,3,2,1,0:T(8,128)(2,1)S(1)}, u32[]{:S(2)}, u32[]{:S(2)}) %collective-permute-start.1) | collective-permute-done | bytes 229408 | tf_op jit(solution)/shard_map/ppermute | solution.py:10
  74.7 4.7 %collective-permute-start.2 = (bf16[1,2,2,256,112]{4,3,2,1,0:T(8,128)(2,1)S(1)}, bf16[1,2,2,256,112]{4,3,2,1,0:T(8,128)(2,1)S(1)}, u32[]{:S(2)}, u32[]{:S(2)}) collective-permute-start(bf16[1,2,2,256,112]{4,3,2,1,0:T(8,128)(2,1)S(1)} %get-tuple-element.20), channel_id=1, source_target_pairs={{0,4},{1,5},{2,6},{3,7},{4,0},{5,1},{6,2},{7,3},{8,12},{9,13},{10,... | collective-permute-start | bytes 688136 | tf_op jit(solution)/shard_map/ppermute | solution.py:10
  79.4 5.3 %collective-permute-done.2 = bf16[1,2,2,256,112]{4,3,2,1,0:T(8,128)(2,1)S(1)} collective-permute-done((bf16[1,2,2,256,112]{4,3,2,1,0:T(8,128)(2,1)S(1)}, bf16[1,2,2,256,112]{4,3,2,1,0:T(8,128)(2,1)S(1)}, u32[]{:S(2)}, u32[]{:S(2)}) %collective-permute-start.2) | collective-permute-done | bytes 229408 | tf_op jit(solution)/shard_map/ppermute | solution.py:10
  85.1 0.7 fusion.24
  85.9 1.0 copy.63
  86.9 7.6 %collective-permute-start.3 = (f32[1,2,2,256,128]{4,3,2,1,0:T(8,128)}, f32[1,2,2,256,128]{4,3,2,1,0:T(8,128)S(1)}, u32[]{:S(2)}, u32[]{:S(2)}) collective-permute-start(f32[1,2,2,256,128]{4,3,2,1,0:T(8,128)} %copy.63), channel_id=1, source_target_pairs={{0,32},{1,33},{2,34},{3,35},{4,36},{5,37},{6,38},{7,39},{8,40},{9,... | collective-permute-start | bytes 1572872 | tf_op jit(solution)/shard_map/ppermute | solution.py:10
  94.7 13.5 %collective-permute-done.3 = f32[1,2,2,256,128]{4,3,2,1,0:T(8,128)S(1)} collective-permute-done((f32[1,2,2,256,128]{4,3,2,1,0:T(8,128)}, f32[1,2,2,256,128]{4,3,2,1,0:T(8,128)S(1)}, u32[]{:S(2)}, u32[]{:S(2)}) %collective-permute-start.3) | collective-permute-done | bytes 524320 | tf_op jit(solution)/shard_map/ppermute | solution.py:10
  108.3 14.1 %collective-permute-start.4 = (f32[1,1,2,256,128]{4,3,2,1,0:T(8,128)S(1)}, f32[1,1,2,256,128]{4,3,2,1,0:T(8,128)S(1)}, u32[]{:S(2)}, u32[]{:S(2)}) collective-permute-start(f32[1,1,2,256,128]{4,3,2,1,0:T(8,128)S(1)} %constant_dynamic-slice_fusion.1), channel_id=1, source_target_pairs={{0,16},{1,17},{2,18},{3,19},{4,20},{5,21},{6,22},{7,23},{8,24},{9,... | collective-permute-start | bytes 786440 | tf_op jit(solution)/shard_map/ppermute | solution.py:10
  122.6 7.6 %scatter_custom_fusion = bf16[2048]{0:T(1024)(128)(2,1)S(1)} fusion(s32[1024]{0:T(1024)S(1)} %bitcast.68, bf16[1024]{0:T(1024)(128)(2,1)S(1)} %reshape.173, bf16[]{:T(256)} %constant.68.clone.1), kind=kCustom, calls=%fused_computation.61 | custom fusion | bytes 4098 | tf_op jit(solution)/shard_map/scatter | solution.py:34
  130.2 0.6 copy.47
  130.8 5.5 %all-to-all-start = ((bf16[16,1,128]{2,1,0:T(2,128)(2,1)}), bf16[16,1,128]{2,1,0:T(2,128)(2,1)S(1)}, u32[]{:S(2)}, u32[]{:S(2)}) async-start(bf16[16,1,128]{2,1,0:T(2,128)(2,1)} %copy.47), calls=%async_computation | async-start | bytes 16384 | tf_op jit(solution)/shard_map/all_to_all | solution.py:40
  136.6 1.9 collective-permute-start.5
  138.6 9.0 %all-to-all-done = bf16[16,1,128]{2,1,0:T(2,128)(2,1)S(1)} async-done(((bf16[16,1,128]{2,1,0:T(2,128)(2,1)}), bf16[16,1,128]{2,1,0:T(2,128)(2,1)S(1)}, u32[]{:S(2)}, u32[]{:S(2)}) %all-to-all-start) | async-done | bytes 4128 | tf_op jit(solution)/shard_map/all_to_all | solution.py:40
  148.1 243.5 %psum.7 = f32[8,16,16]{2,1,0:T(8,128)S(1)} all-reduce(f32[8,16,16]{2,1,0:T(8,128)S(1)} %reshape.148), channel_id=1, replica_groups=mesh['group'=16,'local'=64] {'local'}, use_global_device_ids=true, to_apply=%region_3.4 | all-reduce | flops 2048 | bytes 16384 | tf_op jit(solution)/shard_map/psum | solution.py:89
  391.7 0.7 reshape.201
  392.4 6.0 %all-to-all-start.2 = ((f32[16,1,128]{2,1,0:T(1,128)}), f32[16,1,128]{2,1,0:T(1,128)S(1)}, u32[]{:S(2)}, u32[]{:S(2)}) async-start(f32[16,1,128]{2,1,0:T(1,128)} %reshape.201), calls=%async_computation.2 | async-start | bytes 16384 | tf_op jit(solution)/shard_map/all_to_all | solution.py:90
  398.4 0.8 fusion.16
  399.1 10.5 %all-to-all-done.2 = f32[16,1,128]{2,1,0:T(1,128)S(1)} async-done(((f32[16,1,128]{2,1,0:T(1,128)}), f32[16,1,128]{2,1,0:T(1,128)S(1)}, u32[]{:S(2)}, u32[]{:S(2)}) %all-to-all-start.2) | async-done | bytes 8224 | tf_op jit(solution)/shard_map/all_to_all | solution.py:90
  409.6 0.5 broadcast.121
  410.1 0.7 reduce.5
  411.0 6.1 %gather_fusion.1 = f32[1024]{0:T(1024)S(1)} fusion(f32[2048]{0:T(1024)S(1)} %reshape.149, s32[1024]{0:T(1024)S(1)} %broadcast_clamp_fusion), kind=kCustom, calls=%fused_computation.1 | custom fusion | bytes 12288 | tf_op jit(solution)/shard_map/gather | solution.py:100
  417.2 0.7 copy.59
  (50 shorter events, 3.2 us)
Async XLA Ops:
  0.6 84.4 %copy-start = (bf16[1,1024,896]{2,1,0:T(8,128)(2,1)S(1)}, bf16[1,1024,896]{2,1,0:T(8,128)(2,1)}, u32[]{:S(2)}) copy-start(bf16[1,1024,896]{2,1,0:T(8,128)(2,1)} %param.11) | copy-start | bytes 5505028
  14.2 40.3 %all-to-all-start.1 = ((bf16[16,128,112]{1,2,0:T(8,128)(2,1)}), bf16[16,128,112]{1,2,0:T(8,128)(2,1)S(1)}, u32[]{:S(2)}, u32[]{:S(2)}) async-start(bf16[16,128,112]{1,2,0:T(8,128)(2,1)} %copy.49), calls=%async_computation.1 | async-start | bytes 917504 | tf_op jit(solution)/shard_map/all_to_all | solution.py:39
  54.9 9.9 %collective-permute-start = (bf16[2,2,1,256,112]{4,3,2,1,0:T(8,128)(2,1)S(1)}, bf16[2,2,1,256,112]{4,3,2,1,0:T(8,128)(2,1)S(1)}, u32[]{:S(2)}, u32[]{:S(2)}) collective-permute-start(bf16[2,2,1,256,112]{4,3,2,1,0:T(8,128)(2,1)S(1)} %get-tuple-element.24), channel_id=1, source_target_pairs={{0,1},{1,0},{2,3},{3,2},{4,5},{5,4},{6,7},{7,6},{8,9},{9,8},{10,11... | collective-permute-start | bytes 688136 | tf_op jit(solution)/shard_map/ppermute | solution.py:10
  65.0 9.4 %collective-permute-start.1 = (bf16[2,1,2,256,112]{4,3,2,1,0:T(8,128)(2,1)S(1)}, bf16[2,1,2,256,112]{4,3,2,1,0:T(8,128)(2,1)S(1)}, u32[]{:S(2)}, u32[]{:S(2)}) collective-permute-start(bf16[2,1,2,256,112]{4,3,2,1,0:T(8,128)(2,1)S(1)} %get-tuple-element.22), channel_id=1, source_target_pairs={{0,2},{1,3},{2,0},{3,1},{4,6},{5,7},{6,4},{7,5},{8,10},{9,11},{10,... | collective-permute-start | bytes 688136 | tf_op jit(solution)/shard_map/ppermute | solution.py:10
  74.7 10.0 %collective-permute-start.2 = (bf16[1,2,2,256,112]{4,3,2,1,0:T(8,128)(2,1)S(1)}, bf16[1,2,2,256,112]{4,3,2,1,0:T(8,128)(2,1)S(1)}, u32[]{:S(2)}, u32[]{:S(2)}) collective-permute-start(bf16[1,2,2,256,112]{4,3,2,1,0:T(8,128)(2,1)S(1)} %get-tuple-element.20), channel_id=1, source_target_pairs={{0,4},{1,5},{2,6},{3,7},{4,0},{5,1},{6,2},{7,3},{8,12},{9,13},{10,... | collective-permute-start | bytes 688136 | tf_op jit(solution)/shard_map/ppermute | solution.py:10
  86.9 35.5 %copy-start.3 = (bf16[128,8]{0,1:T(8,128)(2,1)S(1)}, bf16[128,8]{0,1:T(8,128)(2,1)}, u32[]{:S(2)}) copy-start(bf16[128,8]{0,1:T(8,128)(2,1)} %param.10) | copy-start | bytes 6148
  86.9 21.3 %collective-permute-start.3 = (f32[1,2,2,256,128]{4,3,2,1,0:T(8,128)}, f32[1,2,2,256,128]{4,3,2,1,0:T(8,128)S(1)}, u32[]{:S(2)}, u32[]{:S(2)}) collective-permute-start(f32[1,2,2,256,128]{4,3,2,1,0:T(8,128)} %copy.63), channel_id=1, source_target_pairs={{0,32},{1,33},{2,34},{3,35},{4,36},{5,37},{6,38},{7,39},{8,40},{9,... | collective-permute-start | bytes 1572872 | tf_op jit(solution)/shard_map/ppermute | solution.py:10
  94.7 53.2 %copy-start.1 = (bf16[1,256,128]{2,1,0:T(8,128)(2,1)S(1)}, bf16[1,256,128]{2,1,0:T(8,128)(2,1)}, u32[]{:S(2)}) copy-start(bf16[1,256,128]{2,1,0:T(8,128)(2,1)} %param.12) | copy-start | bytes 196612
  94.7 53.1 %copy-start.2 = (bf16[1,256,128]{2,1,0:T(8,128)(2,1)S(1)}, bf16[1,256,128]{2,1,0:T(8,128)(2,1)}, u32[]{:S(2)}) copy-start(bf16[1,256,128]{2,1,0:T(8,128)(2,1)} %param.13) | copy-start | bytes 196612
  108.3 28.3 %collective-permute-start.4 = (f32[1,1,2,256,128]{4,3,2,1,0:T(8,128)S(1)}, f32[1,1,2,256,128]{4,3,2,1,0:T(8,128)S(1)}, u32[]{:S(2)}, u32[]{:S(2)}) collective-permute-start(f32[1,1,2,256,128]{4,3,2,1,0:T(8,128)S(1)} %constant_dynamic-slice_fusion.1), channel_id=1, source_target_pairs={{0,16},{1,17},{2,18},{3,19},{4,20},{5,21},{6,22},{7,23},{8,24},{9,... | collective-permute-start | bytes 786440 | tf_op jit(solution)/shard_map/ppermute | solution.py:10
  130.8 16.8 %all-to-all-start = ((bf16[16,1,128]{2,1,0:T(2,128)(2,1)}), bf16[16,1,128]{2,1,0:T(2,128)(2,1)S(1)}, u32[]{:S(2)}, u32[]{:S(2)}) async-start(bf16[16,1,128]{2,1,0:T(2,128)(2,1)} %copy.47), calls=%async_computation | async-start | bytes 16384 | tf_op jit(solution)/shard_map/all_to_all | solution.py:40
  136.6 11.2 %collective-permute-start.5 = (f32[1,1,1,256,128]{4,3,2,1,0:T(8,128)S(1)}, f32[1,1,1,256,128]{4,3,2,1,0:T(8,128)S(1)}, u32[]{:S(2)}, u32[]{:S(2)}) collective-permute-start(f32[1,1,1,256,128]{4,3,2,1,0:T(8,128)S(1)} %constant_dynamic-slice_fusion), channel_id=1, source_target_pairs={{0,8},{1,9},{2,10},{3,11},{4,12},{5,13},{6,14},{7,15},{8,0},{9,1},... | collective-permute-start | bytes 393224 | tf_op jit(solution)/shard_map/ppermute | solution.py:10
  392.4 17.2 %all-to-all-start.2 = ((f32[16,1,128]{2,1,0:T(1,128)}), f32[16,1,128]{2,1,0:T(1,128)S(1)}, u32[]{:S(2)}, u32[]{:S(2)}) async-start(f32[16,1,128]{2,1,0:T(1,128)} %reshape.201), calls=%async_computation.2 | async-start | bytes 16384 | tf_op jit(solution)/shard_map/all_to_all | solution.py:90
where the time goes:
time: 422 us; the launch traced here: 418 us
  blocking collectives  244 us (58%)
  starting transfers between devices  71 us (17%)
  waiting for transfers between devices  66.5 us (16%)
  local copies, waits for them, and re-layouts  31.9 us (8%)
    psum x1, blocking collectives, shards(): terms = lax.psum(table, 'local')  244 us
    ppermute x6, starting transfers between devices, swapped(): lax.ppermute(shard, axis, [(i, i ^ 1 << bit) for i in range(lax.axis_size...  40.1 us
    ppermute x6, waiting for transfers between devices, swapped(): lax.ppermute(shard, axis, [(i, i ^ 1 << bit) for i in range(lax.axis_size...  26.2 us
    all_to_all x1, waiting for transfers between devices, shards(): lax.all_to_all(send_rows, 'group', split_axis=0, concat_axis=0, tiled=True)  20.8 us
    all_to_all x1, starting transfers between devices, shards(): lax.all_to_all(send_rows, 'group', split_axis=0, concat_axis=0, tiled=True)  19.4 us
    all_to_all x1, waiting for transfers between devices, shards(): lax.all_to_all(terms.reshape(EXP_GRP, group_count, slot_count), 'group',...  10.5 us
    all_to_all x1, waiting for transfers between devices, shards(): lax.all_to_all(send_gates, 'group', split_axis=0, concat_axis=0, tiled=True)  8.99 us
  transfers between devices with their start and end apart: 9, of which 7 were waited for; matrix products, arithmetic and copies ran while one was open for 2% of the time, Pallas kernels for 0%

commit v1 on v0

v1 whole, which is shorter than its diff:
```python
import jax
import jax.numpy as jnp
from jax import lax
from jax.experimental import pallas as pl
from jax.experimental.pallas import tpu as pltpu
from jax.sharding import Mesh, PartitionSpec as P

EXP_GRP = 8
NT = (((1,), (1,)), ((), ()))
F32 = jnp.float32
BF16 = jnp.bfloat16


def lanes(shape):
    return lax.broadcasted_iota(jnp.int32, shape, len(shape) - 1)


def rows(shape):
    return lax.broadcasted_iota(jnp.int32, shape, 0)


def dispatch_kernel(where_ref, tokens_ref, routes_ref, slots_ref, gates_ref, out_ref, gate_ref):
    groups, _, lane_count = out_ref.shape
    tok_count = tokens_ref.shape[1]
    slot_count = 16
    capacity = groups * slot_count
    expert = where_ref[0]
    routes = routes_ref[...]
    place = jnp.where(
        routes % EXP_GRP == expert, routes // EXP_GRP * slot_count + slots_ref[...], -1
    )
    row_ids = rows((capacity, tok_count))
    pick = jnp.zeros((capacity, tok_count), F32)
    gate = jnp.zeros((capacity, tok_count), F32)
    for k in range(routes.shape[0]):
        hit = row_ids == place[k : k + 1, :]
        pick = jnp.where(hit, 1.0, pick)
        gate = jnp.where(hit, gates_ref[k : k + 1, :], gate)
    pick = pick.astype(BF16)
    for b in range(tokens_ref.shape[0] // lane_count):
        block = lax.dot_general(
            pick,
            tokens_ref[b * lane_count : (b + 1) * lane_count, :],
            NT,
            preferred_element_type=F32,
        )
        out_ref[:, b * slot_count : (b + 1) * slot_count, :] = block.astype(BF16).reshape(
            groups, slot_count, lane_count
        )
    gate_ref[...] = jnp.broadcast_to(
        jnp.sum(gate, axis=1, keepdims=True), (capacity, lane_count)
    )


def hidden_kernel(gate_ref, up_ref, out_ref):
    gate_pre = gate_ref[...].astype(F32)
    out_ref[...] = gate_pre * jax.nn.sigmoid(gate_pre) * up_ref[...].astype(F32)


def matmul_kernel(where_ref, rows_ref, w_ref, hidden_ref, gate_ref, give_ref, *outs):
    keep_refs, term_ref = outs[:-1], outs[-1]
    groups, _, lane_count = rows_ref.shape
    slot_count = 16
    capacity = groups * slot_count
    group, shard = where_ref[0], where_ref[1]
    own, quad = shard % 2, shard // 2
    blocks = w_ref.shape[1] // lane_count
    x = jnp.concatenate(
        [
            rows_ref[:, b * slot_count : (b + 1) * slot_count, :].reshape(capacity, lane_count)
            for b in range(blocks)
        ],
        axis=1,
    )
    terms = jnp.zeros((capacity, lane_count), F32)
    for d in range(4):
        for mine in (0, 1):
            target = (quad + d) % 4 * 2 + (own if mine else 1 - own)
            part = lax.dot_general(
                x,
                w_ref[pl.ds(pl.multiple_of(target * lane_count, lane_count), lane_count), :],
                NT,
                preferred_element_type=F32,
            )
            terms += part * hidden_ref[target]
            if mine:
                keep_refs[d][...] = part
            else:
                give_ref[d] = part
    total = jnp.sum(terms, axis=1, keepdims=True)
    row_ids, lane_ids = rows((capacity, lane_count)), lanes((capacity, lane_count))
    hit = lane_ids == group % 8 * slot_count + row_ids % slot_count
    pads = jnp.zeros((groups, 6, lane_count), F32)
    term = jnp.sum(
        jnp.where(hit, total, 0.0).reshape(groups, slot_count, lane_count), axis=1, keepdims=True
    )
    gate = jnp.sum(
        jnp.where(hit, gate_ref[...], 0.0).reshape(groups, slot_count, lane_count),
        axis=1,
        keepdims=True,
    )
    term_ref[...] = jnp.concatenate([term, gate, pads], axis=1)


def output_kernel(h0, h1, h2, h3, home_ref, gate_pre_ref, up_pre_ref, grad_gate_ref, grad_up_ref):
    hidden_grad = h0[...] + h1[...] + h2[...] + h3[...]
    capacity, lane_count = hidden_grad.shape
    groups = home_ref.shape[0]
    gates = jnp.broadcast_to(
        home_ref[:, 1:2, :], (groups, capacity // groups, lane_count)
    ).reshape(capacity, lane_count)
    hit = lanes((capacity, lane_count)) == rows((capacity, lane_count)) % lane_count
    gate = jnp.sum(jnp.where(hit, gates, 0.0), axis=1, keepdims=True)
    gate_pre = gate_pre_ref[...].astype(F32)
    up_pre = up_pre_ref[...].astype(F32)
    sigmoid_gate = jax.nn.sigmoid(gate_pre)
    scaled = gate * hidden_grad
    grad_up_ref[...] = (scaled * gate_pre * sigmoid_gate).astype(BF16)
    grad_gate_ref[...] = (
        scaled * up_pre * sigmoid_gate * (1.0 + gate_pre * (1.0 - sigmoid_gate))
    ).astype(BF16)


def collect_kernel(terms_ref, routes_ref, slots_ref, out_ref):
    shards, experts, halves, lane_count = terms_ref.shape
    tok_count, route_count = routes_ref.shape
    table = terms_ref[0]
    for s in range(1, shards):
        table += terms_ref[s]
    routes = routes_ref[...]
    place = routes // EXP_GRP * 16 + slots_ref[...]
    expert = routes % EXP_GRP
    out = jnp.zeros((tok_count, route_count), F32)
    route_ids = lanes((tok_count, route_count))
    expert_ids = lanes((tok_count, experts))
    for k in range(route_count):
        picked = jnp.zeros((tok_count, experts), F32)
        for h in range(halves):
            hit = lanes((tok_count, lane_count)) + h * lane_count == place[:, k : k + 1]
            picked += lax.dot_general(
                jnp.where(hit, 1.0, 0.0),
                table[:, h, :],
                NT,
                preferred_element_type=F32,
                precision=lax.Precision.HIGHEST,
            )
        column = jnp.sum(
            jnp.where(expert_ids == expert[:, k : k + 1], picked, 0.0), axis=1, keepdims=True
        )
        out = jnp.where(route_ids == k, column, out)
    out_ref[...] = out


VMEM = pl.BlockSpec(memory_space=pltpu.VMEM)
SMEM = pl.BlockSpec(memory_space=pltpu.SMEM)


def call(kernel, specs, out_shape, *args):
    outs = jax.tree.map(lambda _: VMEM, out_shape)
    return pl.pallas_call(
        kernel,
        in_specs=specs,
        out_specs=outs,
        out_shape=out_shape,
        compiler_params=pltpu.CompilerParams(vmem_limit_bytes=24 << 20),
    )(*args)


def shards(grad_out, routes, slots, gates, w_down, saved_gate, saved_up):
    groups = lax.axis_size("group")
    shard_count = lax.axis_size("y")
    capacity, lane_count = saved_gate.shape[1:]
    tok_count, col_width = grad_out.shape
    width = w_down.shape[2]
    group, shard, expert = (lax.axis_index(a) for a in ("group", "y", "xc"))
    where = jnp.stack([group, shard]).astype(jnp.int32)

    token_view = jnp.broadcast_to(grad_out.T[None], (EXP_GRP, col_width, tok_count))
    token_view = lax.all_to_all(token_view, "xc", 0, 0, tiled=True).reshape(width, tok_count)
    slot_rows = jax.ShapeDtypeStruct((groups, width // lane_count * 16, lane_count), BF16)
    column = jax.ShapeDtypeStruct((capacity, lane_count), F32)
    send, gate_rows = call(
        dispatch_kernel,
        [SMEM] + [VMEM] * 4,
        (slot_rows, column),
        expert.astype(jnp.int32)[None],
        token_view,
        routes.T,
        slots.T,
        gates.T.astype(F32),
    )

    pre = jnp.concatenate([saved_gate, saved_up], axis=0)
    send, pre = lax.optimization_barrier((send, pre))
    expert_rows = lax.all_to_all(send, "group", 0, 0, tiled=True)
    every_pre = lax.all_gather(pre, "y")
    full = jax.ShapeDtypeStruct((shard_count, capacity, lane_count), F32)
    hidden = call(hidden_kernel, [VMEM] * 2, full, every_pre[:, 0], every_pre[:, 1])

    give, k0, k1, k2, k3, terms = call(
        matmul_kernel,
        [SMEM] + [VMEM] * 4,
        (
            jax.ShapeDtypeStruct((4, capacity, lane_count), F32),
            column,
            column,
            column,
            column,
            jax.ShapeDtypeStruct((groups, 8, lane_count), F32),
        ),
        where,
        expert_rows,
        w_down[0],
        hidden,
        gate_rows,
    )

    got = lax.ppermute(give, "y", [(i, i ^ 1) for i in range(shard_count)])
    home = lax.all_to_all(terms, "group", 0, 0, tiled=True)
    parts = [k + got[d] for d, k in enumerate((k0, k1, k2, k3))]
    for d in (2, 1, 3):
        parts[d] = lax.ppermute(
            parts[d], "y", [(i, (i + 2 * d) % shard_count) for i in range(shard_count)]
        )
    own_terms = jnp.sum(home[:, 0, :].reshape(2, groups // 2, lane_count), axis=1)
    every_term = lax.all_to_all(
        jnp.broadcast_to(own_terms[None], (shard_count * EXP_GRP, 2, lane_count)),
        ("y", "xc"),
        0,
        0,
        tiled=True,
    ).reshape(shard_count, EXP_GRP, 2, lane_count)
    out = jax.ShapeDtypeStruct((capacity, lane_count), BF16)
    grad_gate, grad_up = call(
        output_kernel, [VMEM] * 7, (out, out), *parts, home, saved_gate[0], saved_up[0]
    )
    grad_gates = call(
        collect_kernel,
        [VMEM] * 3,
        jax.ShapeDtypeStruct(routes.shape, F32),
        every_term,
        routes,
        slots,
    )
    return (grad_gate[None], grad_up[None], grad_gates)


def solution(mesh):
    fine = Mesh(mesh.devices.reshape(mesh.shape["group"], -1, EXP_GRP), ("group", "y", "xc"))
    local, device = ("y", "xc"), ("group", "y", "xc")
    return jax.shard_map(
        shards,
        mesh=fine,
        in_specs=(
            P("group", local),
            P("group", None),
            P("group", None),
            P("group", None),
            P(device, None, None),
            P(device, None, None),
            P(device, None, None),
        ),
        out_specs=(P(device, None, None), P(device, None, None), P("group", None)),
        check_vma=False,
    )
```

time: 422 us -> 150 us (0.36)
  blocking collectives: 244 us -> 24.1 us
  local copies, waits for them, and re-layouts: 31.9 us -> 5.96 us
  waiting for transfers between devices: 66.5 us -> 43.1 us
  starting transfers between devices: 71 us -> 54.7 us
  between operations: 1.09 us -> 14.2 us
  Pallas kernels: 0 us -> 5.12 us
    psum x1 -> x0, blocking collectives: 244 us -> none  [shards(): terms = lax.psum(table, 'local')]
    all_gather x0 -> x1, waiting for transfers between devices: none -> 29.3 us  [shards(): every_pre = lax.all_gather(pre, 'y')]
    all_to_all x3, waiting for transfers between devices: 40.3 us -> 13.9 us  [the longest x1 9.87 us: shards(): lax.all_to_all(jnp.broadcast_to(own_terms[None], (shard_count * EXP_GRP,...]
    ppermute x6 -> x4, waiting for transfers between devices: 26.2 us -> 0.01 us  [the longest x3 0.01 us: shards(): lax.ppermute(parts[d], 'y', [(i, (i + 2 * d) % shard_count) for i in rang...]
    ppermute x6 -> x4, starting transfers between devices: 40.1 us -> 15.3 us  [the longest x3 11.8 us: shards(): lax.ppermute(parts[d], 'y', [(i, (i + 2 * d) % shard_count) for i in rang...]
    all_to_all x0 -> x1, blocking collectives: none -> 24.1 us  [shards(): home = lax.all_to_all(terms, 'group', 0, 0, tiled=True)]
    gather x3 -> x0, local copies, waits for them, and re-layouts: 12.4 us -> none  [the longest x2 6.23 us: shards(): grad_gates = home_terms.reshape(-1)[flat_index]]
    scatter x2 -> x0, local copies, waits for them, and re-layouts: 11.9 us -> none  [the longest x1 7.59 us: shards(): jnp.zeros((total_slots,), jnp.bfloat16).at[flat_target]]
  transfers between devices with their start and end apart: 9 -> 8, of which waited for: 7 -> 3; matrix products, arithmetic and copies ran while one was open for 2% -> 4% of each run, Pallas kernels for 0% -> 1%
where the time goes in v1:
time: 150 us
  starting transfers between devices  54.7 us (36%)
  waiting for transfers between devices  43.1 us (29%)
  blocking collectives  24.1 us (16%)
  between operations  14.2 us (9%)
  local copies, waits for them, and re-layouts  5.96 us (4%)
  Pallas kernels  5.12 us (3%)
  other arithmetic  2.4 us (2%)
    all_gather x1, waiting for transfers between devices, shards(): every_pre = lax.all_gather(pre, 'y')  29.3 us
    all_to_all x1, blocking collectives, shards(): home = lax.all_to_all(terms, 'group', 0, 0, tiled=True)  24.1 us
    all_to_all x1, starting transfers between devices, shards(): lax.all_to_all(token_view, 'xc', 0, 0, tiled=True).reshape(width, tok_count)  17.5 us
    all_to_all x1, starting transfers between devices, shards(): lax.all_to_all(jnp.broadcast_to(own_terms[None], (shard_count * EXP_GRP,...  15.1 us
    ppermute x3, starting transfers between devices, shards(): lax.ppermute(parts[d], 'y', [(i, (i + 2 * d) % shard_count) for i in rang...  11.8 us
    all_to_all x1, waiting for transfers between devices, shards(): lax.all_to_all(jnp.broadcast_to(own_terms[None], (shard_count * EXP_GRP,...  9.87 us
    all_to_all x1, starting transfers between devices, shards(): expert_rows = lax.all_to_all(send, 'group', 0, 0, tiled=True)  6.92 us
    pallas_call x5, Pallas kernels, call(): pl.pallas_call(kernel, in_specs=specs, out_specs=outs, out_shape=out_shap...  5.12 us
  transfers between devices with their start and end apart: 8, of which 3 were waited for; matrix products, arithmetic and copies ran while one was open for 4% of the time, Pallas kernels for 1%

profile of v1, /device:TPU:1, one launch (start us, length us, event | category | flops | bytes accessed | tf_op | source)
XLA Modules:
  0.0 149.6 jit_solution(7840135458843841167)
XLA Ops:
  7.2 1.5 broadcast_in_dim.22
  8.6 17.5 %all-to-all-start = ((bf16[8,112,128]{2,1,0:T(8,128)(2,1)}), bf16[8,112,128]{2,1,0:T(8,128)(2,1)S(1)}, u32[]{:S(2)}, u32[]{:S(2)}) async-start(bf16[8,112,128]{2,1,0:T(8,128)(2,1)} %broadcast_in_dim.22), calls=%async_computation | async-start | bytes 458752 | tf_op jit(solution)/shard_map/all_to_all | solution.py:179
  26.1 1.5 %pad_maximum_fusion = bf16[2,256,128]{2,1,0:T(8,128)(2,1)} fusion(bf16[1,256,128]{2,1,0:T(8,128)(2,1)} %param.13, bf16[1,256,128]{2,1,0:T(8,128)(2,1)} %param.12), kind=kLoop, calls=%fused_computation.10 | loop fusion | flops 65536 | bytes 262144 | tf_op jit(solution)/shard_map/concatenate | solution.py:193
  27.6 0.7 convert_bitcast_fusion.gates_ref
  28.3 4.0 %all-to-all-done = bf16[8,112,128]{2,1,0:T(8,128)(2,1)S(1)} async-done(((bf16[8,112,128]{2,1,0:T(8,128)(2,1)}), bf16[8,112,128]{2,1,0:T(8,128)(2,1)S(1)}, u32[]{:S(2)}, u32[]{:S(2)}) %all-to-all-start) | async-done | bytes 229408 | tf_op jit(solution)/shard_map/all_to_all | solution.py:179
  32.3 0.7 copy-done.3
  33.0 0.7 copy-done.5
  33.7 1.2 shard_map.94
  34.9 0.0 all-gather.3.cloned.1.call-update
  34.9 6.9 %all-to-all-start.1 = ((bf16[16,112,128]{2,1,0:T(8,128)(2,1)}), bf16[16,112,128]{2,1,0:T(8,128)(2,1)S(1)}, u32[]{:S(2)}, u32[]{:S(2)}) async-start(bf16[16,112,128]{2,1,0:T(8,128)(2,1)} %get-tuple-element.16), calls=%async_computation.1 | async-start | bytes 917504 | tf_op jit(solution)/shard_map/all_to_all | solution.py:195
  41.8 0.1 pad_add_fusion.where_ref
  41.9 29.3 %all-gather.3.cloned.1.call-done = bf16[16,256,128]{2,1,0:T(8,128)(2,1)} async-done(((bf16[2,256,128]{2,1,0:T(8,128)(2,1)}), bf16[16,256,128]{2,1,0:T(8,128)(2,1)}) %all-gather.3.cloned.1.call-update) | async-done | bytes 1048592 | tf_op jit(solution)/shard_map/all_gather | solution.py:196
  71.2 1.4 slice_bitcast_fusion
  72.6 0.2 shard_map.95.hidden_ref
  72.8 0.1 copy-done
  73.0 1.8 %shard_map.96 = (f32[4,256,128]{2,1,0:T(8,128)S(1)}, f32[256,128]{1,0:T(8,128)S(1)}, f32[256,128]{1,0:T(8,128)S(1)}, f32[256,128]{1,0:T(8,128)S(1)}, f32[256,128]{1,0:T(8,128)S(1)}, /*index=5*/f32[16,8,128]{2,1,0:T(8,128)S(1)}) custom-call(s32[2]{0:T(128)S(1)} %pad_add_fusion.where_ref, bf16[16,112,128]{2,1,0:T(8,128)(2,1)S(1)} %all-to-all-done.1.rows_ref, ...), custom_call_target="tpu_custom_call" | custom-call | tf_op jit(solution)/shard_map/pallas_call | solution.py:160
  74.7 0.0 copy-start.4
  74.7 0.0 copy-start.6
  74.8 3.4 %collective-permute-start = (f32[4,256,128]{2,1,0:T(8,128)S(1)}, f32[4,256,128]{2,1,0:T(8,128)S(1)}, u32[]{:S(2)}, u32[]{:S(2)}) collective-permute-start(f32[4,256,128]{2,1,0:T(8,128)S(1)} %get-tuple-element.20), channel_id=1, source_target_pairs={{0,8},{8,0},{16,24},{24,16},{32,40},{40,32},{48,56},{56,48},{1,9},... | collective-permute-start | bytes 1572872 | tf_op jit(solution)/shard_map/ppermute | solution.py:218
  78.2 24.1 %all_to_all.20.home_ref = f32[16,8,128]{2,1,0:T(8,128)S(1)} all-to-all(f32[16,8,128]{2,1,0:T(8,128)S(1)} %get-tuple-element.24), channel_id=1, replica_groups=mesh['group'=16,'y'=8,'xc'=8] {'group'}, dimensions={0} | all-to-all | bytes 131072 | tf_op jit(solution)/shard_map/all_to_all | solution.py:219
  102.3 0.1 fusion
  102.4 3.4 %collective-permute-start.1 = (f32[256,128]{1,0:T(8,128)S(1)}, f32[256,128]{1,0:T(8,128)S(1)}, u32[]{:S(2)}, u32[]{:S(2)}) collective-permute-start(f32[256,128]{1,0:T(8,128)S(1)} %get-tuple-element.40), channel_id=1, source_target_pairs={{0,16},{8,24},{16,32},{24,40},{32,48},{40,56},{48,0},{56,8},{1,17}... | collective-permute-start | bytes 393224 | tf_op jit(solution)/shard_map/ppermute | solution.py:222
  105.8 4.5 %collective-permute-start.2 = (f32[256,128]{1,0:T(8,128)S(1)}, f32[256,128]{1,0:T(8,128)S(1)}, u32[]{:S(2)}, u32[]{:S(2)}) collective-permute-start(f32[256,128]{1,0:T(8,128)S(1)} %get-tuple-element.39), channel_id=1, source_target_pairs={{0,32},{8,40},{16,48},{24,56},{32,0},{40,8},{48,16},{56,24},{1,33}... | collective-permute-start | bytes 393224 | tf_op jit(solution)/shard_map/ppermute | solution.py:222
  110.3 4.0 %collective-permute-start.3 = (f32[256,128]{1,0:T(8,128)S(1)}, f32[256,128]{1,0:T(8,128)S(1)}, u32[]{:S(2)}, u32[]{:S(2)}) collective-permute-start(f32[256,128]{1,0:T(8,128)S(1)} %get-tuple-element.38), channel_id=1, source_target_pairs={{0,48},{8,56},{16,0},{24,8},{32,16},{40,24},{48,32},{56,40},{1,49}... | collective-permute-start | bytes 393224 | tf_op jit(solution)/shard_map/ppermute | solution.py:222
  114.3 0.7 broadcast_in_dim.25
  115.0 15.1 %all-to-all-start.3 = ((f32[64,2,128]{2,1,0:T(2,128)}), f32[64,2,128]{2,1,0:T(2,128)S(1)}, u32[]{:S(2)}, u32[]{:S(2)}) async-start(f32[64,2,128]{2,1,0:T(2,128)} %broadcast_in_dim.25), calls=%async_computation.3 | async-start | bytes 131072 | tf_op jit(solution)/shard_map/all_to_all | solution.py:226
  130.0 0.1 copy.20.routes_ref
  130.1 0.1 copy.21.slots_ref
  130.2 9.9 %all-to-all-done.3 = f32[64,2,128]{2,1,0:T(2,128)S(1)} async-done(((f32[64,2,128]{2,1,0:T(2,128)}), f32[64,2,128]{2,1,0:T(2,128)S(1)}, u32[]{:S(2)}, u32[]{:S(2)}) %all-to-all-start.3) | async-done | bytes 65568 | tf_op jit(solution)/shard_map/all_to_all | solution.py:226
  140.1 1.2 shard_map.98
  141.3 0.7 copy.22
  142.0 0.8 shard_map.97
  (17 shorter events, 0.1 us)
Async XLA Ops:
  8.6 23.7 %all-to-all-start = ((bf16[8,112,128]{2,1,0:T(8,128)(2,1)}), bf16[8,112,128]{2,1,0:T(8,128)(2,1)S(1)}, u32[]{:S(2)}, u32[]{:S(2)}) async-start(bf16[8,112,128]{2,1,0:T(8,128)(2,1)} %broadcast_in_dim.22), calls=%async_computation | async-start | bytes 458752 | tf_op jit(solution)/shard_map/all_to_all | solution.py:179
  26.1 45.1 %all-gather.3.cloned.1.call-start = ((), (), s32[]{:S(2)}) async-start(), calls=%async_computation.4 | async-start | bytes 1179648 | tf_op jit(solution)/shard_map/all_gather | solution.py:196
  32.3 0.7 copy-start.3
  33.0 0.7 copy-start.5
  34.9 37.9 %all-to-all-start.1 = ((bf16[16,112,128]{2,1,0:T(8,128)(2,1)}), bf16[16,112,128]{2,1,0:T(8,128)(2,1)S(1)}, u32[]{:S(2)}, u32[]{:S(2)}) async-start(bf16[16,112,128]{2,1,0:T(8,128)(2,1)} %get-tuple-element.16), calls=%async_computation.1 | async-start | bytes 917504 | tf_op jit(solution)/shard_map/all_to_all | solution.py:195
  71.2 1.8 %copy-start = (bf16[1,1024,896]{2,1,0:T(8,128)(2,1)S(1)}, bf16[1,1024,896]{2,1,0:T(8,128)(2,1)}, u32[]{:S(2)}) copy-start(bf16[1,1024,896]{2,1,0:T(8,128)(2,1)} %param.11) | copy-start | bytes 5505028
  74.7 55.3 %copy-start.4 = (s32[128,8]{0,1:T(8,128)S(1)}, s32[128,8]{0,1:T(8,128)}, u32[]{:S(2)}) copy-start(s32[128,8]{0,1:T(8,128)} %param.8) | copy-start | bytes 12292
  74.7 55.4 %copy-start.6 = (s32[128,8]{0,1:T(8,128)S(1)}, s32[128,8]{0,1:T(8,128)}, u32[]{:S(2)}) copy-start(s32[128,8]{0,1:T(8,128)} %param.9) | copy-start | bytes 12292
  74.8 67.2 %copy-start.1 = (bf16[1,256,128]{2,1,0:T(8,128)(2,1)S(1)}, bf16[1,256,128]{2,1,0:T(8,128)(2,1)}, u32[]{:S(2)}) copy-start(bf16[1,256,128]{2,1,0:T(8,128)(2,1)} %param.13) | copy-start | bytes 196612
  74.8 67.2 %copy-start.2 = (bf16[1,256,128]{2,1,0:T(8,128)(2,1)S(1)}, bf16[1,256,128]{2,1,0:T(8,128)(2,1)}, u32[]{:S(2)}) copy-start(bf16[1,256,128]{2,1,0:T(8,128)(2,1)} %param.12) | copy-start | bytes 196612
  74.8 27.6 %collective-permute-start = (f32[4,256,128]{2,1,0:T(8,128)S(1)}, f32[4,256,128]{2,1,0:T(8,128)S(1)}, u32[]{:S(2)}, u32[]{:S(2)}) collective-permute-start(f32[4,256,128]{2,1,0:T(8,128)S(1)} %get-tuple-element.20), channel_id=1, source_target_pairs={{0,8},{8,0},{16,24},{24,16},{32,40},{40,32},{48,56},{56,48},{1,9},... | collective-permute-start | bytes 1572872 | tf_op jit(solution)/shard_map/ppermute | solution.py:218
  102.4 39.5 %collective-permute-start.1 = (f32[256,128]{1,0:T(8,128)S(1)}, f32[256,128]{1,0:T(8,128)S(1)}, u32[]{:S(2)}, u32[]{:S(2)}) collective-permute-start(f32[256,128]{1,0:T(8,128)S(1)} %get-tuple-element.40), channel_id=1, source_target_pairs={{0,16},{8,24},{16,32},{24,40},{32,48},{40,56},{48,0},{56,8},{1,17}... | collective-permute-start | bytes 393224 | tf_op jit(solution)/shard_map/ppermute | solution.py:222
  105.8 36.2 %collective-permute-start.2 = (f32[256,128]{1,0:T(8,128)S(1)}, f32[256,128]{1,0:T(8,128)S(1)}, u32[]{:S(2)}, u32[]{:S(2)}) collective-permute-start(f32[256,128]{1,0:T(8,128)S(1)} %get-tuple-element.39), channel_id=1, source_target_pairs={{0,32},{8,40},{16,48},{24,56},{32,0},{40,8},{48,16},{56,24},{1,33}... | collective-permute-start | bytes 393224 | tf_op jit(solution)/shard_map/ppermute | solution.py:222
  110.3 31.7 %collective-permute-start.3 = (f32[256,128]{1,0:T(8,128)S(1)}, f32[256,128]{1,0:T(8,128)S(1)}, u32[]{:S(2)}, u32[]{:S(2)}) collective-permute-start(f32[256,128]{1,0:T(8,128)S(1)} %get-tuple-element.38), channel_id=1, source_target_pairs={{0,48},{8,56},{16,0},{24,8},{32,16},{40,24},{48,32},{56,40},{1,49}... | collective-permute-start | bytes 393224 | tf_op jit(solution)/shard_map/ppermute | solution.py:222
  115.0 25.1 %all-to-all-start.3 = ((f32[64,2,128]{2,1,0:T(2,128)}), f32[64,2,128]{2,1,0:T(2,128)S(1)}, u32[]{:S(2)}, u32[]{:S(2)}) async-start(f32[64,2,128]{2,1,0:T(2,128)} %broadcast_in_dim.25), calls=%async_computation.3 | async-start | bytes 131072 | tf_op jit(solution)/shard_map/all_to_all | solution.py:226
Sparse Core Ops, SparseCore 0:
  35.0 36.0 all-gather.2

commit v2 on v0

v2 whole, which is shorter than its diff:
```python
import jax
import jax.numpy as jnp
from jax import lax
from jax.experimental import pallas as pl
from jax.experimental.pallas import tpu as pltpu
from jax.sharding import Mesh, PartitionSpec as P

EXP_GRP = 8
SLOTS = 16
PAD = 8
NT = (((1,), (1,)), ((), ()))
TN = (((0,), (0,)), ((), ()))
F32 = jnp.float32
BF16 = jnp.bfloat16


def lanes(shape):
    return lax.broadcasted_iota(jnp.int32, shape, len(shape) - 1)


def rows(shape):
    return lax.broadcasted_iota(jnp.int32, shape, 0)


def dispatch_kernel(tokens_ref, routes_ref, slots_ref, gates_ref, out_ref):
    col_width, tok_count = tokens_ref.shape
    lane_count = out_ref.shape[2]
    place = routes_ref[...] * SLOTS + slots_ref[...]
    gates = gates_ref[...].astype(F32)
    spare = (lane_count - col_width, tok_count)
    features = jnp.concatenate([tokens_ref[...], jnp.zeros(spare, BF16)], axis=0)
    marks = jnp.where(rows((lane_count, tok_count)) == col_width, 1.0, 0.0).astype(BF16)
    source = jnp.concatenate([features, marks], axis=1)
    chunk = 256
    for start in range(0, out_ref.shape[0] * SLOTS, chunk):
        row_ids = rows((chunk, tok_count)) + start
        pick = jnp.zeros((chunk, tok_count), F32)
        gate = jnp.zeros((chunk, tok_count), F32)
        for k in range(place.shape[0]):
            hit = row_ids == place[k : k + 1, :]
            pick = jnp.where(hit, 1.0, pick)
            gate = jnp.where(hit, gates[k : k + 1, :], gate)
        both = jnp.concatenate([pick.astype(BF16), gate.astype(BF16)], axis=1)
        block = lax.dot_general(both, source, NT, preferred_element_type=F32)
        out_ref[start // SLOTS : (start + chunk) // SLOTS] = block.astype(BF16).reshape(
            chunk // SLOTS, SLOTS, lane_count
        )


def hidden_kernel(gate_ref, up_ref, out_ref):
    gate_pre = gate_ref[...].astype(F32)
    out_ref[...] = gate_pre * jax.nn.sigmoid(gate_pre) * up_ref[...].astype(F32)


def matmul_kernel(shard_ref, rows_ref, w_ref, *refs):
    hidden_refs, (part_ref, gate_ref) = refs[:-2], refs[-2:]
    groups, parts, _, lane_count = rows_ref.shape
    capacity = groups * SLOTS
    col_width = w_ref.shape[1] // parts
    shard = shard_ref[0]
    count = part_ref.shape[0]
    blocks = [rows_ref[:, e].reshape(capacity, lane_count) for e in range(parts)]
    x = jnp.concatenate([b[:, :col_width] for b in blocks], axis=1)
    terms = jnp.zeros((capacity, lane_count), F32)
    for j in range(count):
        target = (shard + j) % count
        first = pl.multiple_of(target * lane_count, lane_count)
        part = lax.dot_general(
            x, w_ref[pl.ds(first, lane_count), :], NT, preferred_element_type=F32
        )
        terms += part * hidden_refs[j][...]
        part_ref[target, :capacity] = part
    total = jnp.sum(terms, axis=1, keepdims=True)
    hit = lanes((capacity, lane_count)) == rows((capacity, lane_count)) % lane_count
    halves = capacity // lane_count
    line = jnp.sum(jnp.where(hit, total, 0.0).reshape(halves, lane_count, lane_count), axis=1)
    line = jnp.concatenate([line, jnp.zeros((PAD - halves, lane_count), F32)], axis=0)
    for j in range(count):
        part_ref[j, capacity:] = line
    gate = jnp.where(lanes((capacity, lane_count)) == col_width, blocks[0].astype(F32), 0.0)
    gate_ref[...] = jnp.broadcast_to(
        jnp.sum(gate, axis=1, keepdims=True), (capacity, lane_count)
    )


def terms_kernel(part_ref, out_ref):
    total = part_ref[0]
    for s in range(1, part_ref.shape[0]):
        total += part_ref[s]
    devices, _, lane_count = out_ref.shape
    half = devices // 2
    out_ref[:half] = jnp.broadcast_to(total[0:1, :][None], (half, 1, lane_count))
    out_ref[half:] = jnp.broadcast_to(total[1:2, :][None], (half, 1, lane_count))


def output_kernel(part_ref, gate_ref, gate_pre_ref, up_pre_ref, grad_gate_ref, grad_up_ref):
    capacity = gate_ref.shape[0]
    hidden_grad = part_ref[0, :capacity]
    for s in range(1, part_ref.shape[0]):
        hidden_grad += part_ref[s, :capacity]
    gate_pre = gate_pre_ref[...].astype(F32)
    up_pre = up_pre_ref[...].astype(F32)
    sigmoid_gate = jax.nn.sigmoid(gate_pre)
    scaled = gate_ref[...] * hidden_grad
    grad_up_ref[...] = (scaled * gate_pre * sigmoid_gate).astype(BF16)
    grad_gate_ref[...] = (
        scaled * up_pre * sigmoid_gate * (1.0 + gate_pre * (1.0 - sigmoid_gate))
    ).astype(BF16)


def collect_kernel(group_ref, terms_ref, routes_ref, slots_ref, out_ref):
    experts, _, lane_count = terms_ref.shape
    route_count, tok_count = routes_ref.shape
    table = terms_ref[:, 0, :]
    offset = group_ref[0] % (lane_count // SLOTS) * SLOTS
    for k in range(route_count):
        hit = rows((experts, tok_count)) == routes_ref[k : k + 1, :]
        picked = lax.dot_general(
            table,
            jnp.where(hit, 1.0, 0.0),
            TN,
            preferred_element_type=F32,
            precision=lax.Precision.HIGHEST,
        )
        own = rows((lane_count, tok_count)) == slots_ref[k : k + 1, :] + offset
        out_ref[k : k + 1, :] = jnp.sum(jnp.where(own, picked, 0.0), axis=0, keepdims=True)


VMEM = pl.BlockSpec(memory_space=pltpu.VMEM)
SMEM = pl.BlockSpec(memory_space=pltpu.SMEM)


def call(kernel, specs, out_shape, *args):
    return pl.pallas_call(
        kernel,
        in_specs=specs,
        out_specs=jax.tree.map(lambda _: VMEM, out_shape),
        out_shape=out_shape,
        compiler_params=pltpu.CompilerParams(vmem_limit_bytes=24 << 20),
    )(*args)


def shards(grad_out, routes, slots, gates, w_down, saved_gate, saved_up):
    shape = jax.ShapeDtypeStruct
    groups, shard_count, parts = (lax.axis_size(a) for a in ("group", "y", "xc"))
    capacity, lane_count = saved_gate.shape[1:]
    group = lax.axis_index("group").astype(jnp.int32)[None]
    shard = lax.axis_index("y").astype(jnp.int32)[None]
    column = shape((capacity, lane_count), F32)

    send = call(
        dispatch_kernel,
        [VMEM] * 4,
        shape((groups * parts, SLOTS, lane_count), BF16),
        grad_out.T,
        routes.T,
        slots.T,
        gates.T,
    )
    send, gate_pre, up_pre = lax.optimization_barrier((send, saved_gate[0], saved_up[0]))
    expert_rows = lax.all_to_all(send, ("group", "xc"), 0, 0, tiled=True)

    hidden = call(hidden_kernel, [VMEM] * 2, column, gate_pre, up_pre)
    others = {
        j: lax.ppermute(
            hidden, "y", [(i, (i - j) % shard_count) for i in range(shard_count)]
        )
        for j in range(1, shard_count)
    }
    part, gate_rows = call(
        matmul_kernel,
        [SMEM] + [VMEM] * (2 + shard_count),
        (shape((shard_count, capacity + PAD, lane_count), F32), column),
        shard,
        expert_rows.reshape(groups, parts, SLOTS, lane_count),
        w_down[0],
        hidden,
        *(others[j] for j in range(1, shard_count)),
    )

    part = lax.all_to_all(part, "y", 0, 0, tiled=True)
    tail = pl.BlockSpec((shard_count, PAD, lane_count), lambda i: (0, capacity // PAD, 0))
    term_rows = pl.pallas_call(
        terms_kernel,
        grid=(1,),
        in_specs=[tail],
        out_specs=pl.BlockSpec((groups * parts, 1, lane_count), lambda i: (0, 0, 0)),
        out_shape=shape((groups * parts, 1, lane_count), F32),
    )(part)
    home_terms = lax.all_to_all(term_rows, ("group", "xc"), 0, 0, tiled=True)
    out = shape((capacity, lane_count), BF16)
    grad_gate, grad_up = call(
        output_kernel, [VMEM] * 4, (out, out), part, gate_rows, saved_gate[0], saved_up[0]
    )
    grad_gates = call(
        collect_kernel,
        [SMEM] + [VMEM] * 3,
        shape(routes.shape[::-1], F32),
        group,
        home_terms,
        routes.T,
        slots.T,
    )
    return (grad_gate[None], grad_up[None], grad_gates.T)


def solution(mesh):
    fine = Mesh(mesh.devices.reshape(mesh.shape["group"], -1, EXP_GRP), ("group", "y", "xc"))
    local, device = ("y", "xc"), ("group", "y", "xc")
    return jax.shard_map(
        shards,
        mesh=fine,
        in_specs=(
            P("group", local),
            P("group", None),
            P("group", None),
            P("group", None),
            P(device, None, None),
            P(device, None, None),
            P(device, None, None),
        ),
        out_specs=(P(device, None, None), P(device, None, None), P("group", None)),
        check_vma=False,
    )
```

time: 422 us -> 141 us (0.33)
  blocking collectives: 244 us -> 32.4 us
  waiting for transfers between devices: 66.5 us -> 26 us
  local copies, waits for them, and re-layouts: 31.9 us -> 4.63 us
  Pallas kernels: 0 us -> 6.85 us
    psum x1 -> x0, blocking collectives: 244 us -> none  [shards(): terms = lax.psum(table, 'local')]
    all_to_all x0 -> x1, blocking collectives: none -> 32.4 us  [shards(): part = lax.all_to_all(part, 'y', 0, 0, tiled=True)]
    all_to_all x3 -> x2, waiting for transfers between devices: 40.3 us -> 14 us  [the longest x1 14 us: shards(): home_terms = lax.all_to_all(term_rows, ('group', 'xc'), 0, 0, tiled=True)]
    ppermute x6 -> x7, waiting for transfers between devices: 26.2 us -> 12 us  [shards(): lax.ppermute(hidden, 'y', [(i, (i - j) % shard_count) for i in range(shar...]
    gather x3 -> x0, local copies, waits for them, and re-layouts: 12.4 us -> none  [the longest x2 6.23 us: shards(): grad_gates = home_terms.reshape(-1)[flat_index]]
    scatter x2 -> x0, local copies, waits for them, and re-layouts: 11.9 us -> none  [the longest x1 7.59 us: shards(): jnp.zeros((total_slots,), jnp.bfloat16).at[flat_target]]
    ppermute x6 -> x7, starting transfers between devices: 40.1 us -> 28.4 us  [shards(): lax.ppermute(hidden, 'y', [(i, (i - j) % shard_count) for i in range(shar...]
    all_to_all x3 -> x2, starting transfers between devices: 30.9 us -> 41.6 us  [the longest x1 24.1 us: shards(): expert_rows = lax.all_to_all(send, ('group', 'xc'), 0, 0, tiled=True)]
  transfers between devices with their start and end apart: 9 -> 9, of which waited for: 7 -> 4; matrix products, arithmetic and copies ran while one was open for 2% -> 0% of each run, Pallas kernels for 0% -> 1%
where the time goes in v2:
time: 141 us
  starting transfers between devices  70 us (50%)
  blocking collectives  32.4 us (23%)
  waiting for transfers between devices  26 us (18%)
  Pallas kernels  6.85 us (5%)
  local copies, waits for them, and re-layouts  4.63 us (3%)
    all_to_all x1, blocking collectives, shards(): part = lax.all_to_all(part, 'y', 0, 0, tiled=True)  32.4 us
    ppermute x7, starting transfers between devices, shards(): lax.ppermute(hidden, 'y', [(i, (i - j) % shard_count) for i in range(shar...  28.4 us
    all_to_all x1, starting transfers between devices, shards(): expert_rows = lax.all_to_all(send, ('group', 'xc'), 0, 0, tiled=True)  24.1 us
    all_to_all x1, starting transfers between devices, shards(): home_terms = lax.all_to_all(term_rows, ('group', 'xc'), 0, 0, tiled=True)  17.6 us
    all_to_all x1, waiting for transfers between devices, shards(): home_terms = lax.all_to_all(term_rows, ('group', 'xc'), 0, 0, tiled=True)  14 us
    ppermute x7, waiting for transfers between devices, shards(): lax.ppermute(hidden, 'y', [(i, (i - j) % shard_count) for i in range(shar...  12 us
    pallas_call x5, Pallas kernels, call(): pl.pallas_call(kernel, in_specs=specs, out_specs=jax.tree.map(lambda _: V...  5.32 us
    unnamed x24, local copies, waits for them, and re-layouts  4.63 us
  transfers between devices with their start and end apart: 9, of which 4 were waited for; matrix products, arithmetic and copies ran while one was open for 0% of the time, Pallas kernels for 1%

profile of v2, /device:TPU:1, one launch (start us, length us, event | category | flops | bytes accessed | tf_op | source)
XLA Modules:
  0.0 140.8 jit_solution(4653846265329166874)
XLA Ops:
  0.7 0.9 copy-done.6
  1.5 0.7 copy-done.7
  2.2 0.7 copy-done.9
  2.9 0.7 copy-done.11
  3.6 2.0 %shard_map.94 = bf16[128,16,128]{2,1,0:T(8,128)(2,1)} custom-call(bf16[112,128]{1,0:T(8,128)(2,1)S(1)} %bitcast.19, s32[8,128]{1,0:T(8,128)S(1)} %bitcast.20, s32[8,128]{1,0:T(8,128)S(1)} %bitcast.22, bf16[8,128]{1,0:T(8,128)(2,1)S(1)} %bitcast.24), custom_call_target="tpu_custom_call" | custom-call | tf_op jit(solution)/shard_map/pallas_call | solution.py:134
  5.6 24.1 %all-to-all-start = ((bf16[128,16,128]{2,1,0:T(8,128)(2,1)}), bf16[128,16,128]{2,1,0:T(8,128)(2,1)S(1)}, u32[]{:S(2)}, u32[]{:S(2)}) async-start(bf16[128,16,128]{2,1,0:T(8,128)(2,1)} %shard_map.94), calls=%async_computation | async-start | bytes 1048576 | tf_op jit(solution)/shard_map/all_to_all | solution.py:161
  29.7 0.0 copy-start.2
  29.7 0.8 copy-done.2
  30.5 0.8 copy-done.4
  31.4 3.2 %collective-permute-start.6 = (f32[256,128]{1,0:T(8,128)S(1)}, f32[256,128]{1,0:T(8,128)S(1)}, u32[]{:S(2)}, u32[]{:S(2)}) collective-permute-start(f32[256,128]{1,0:T(8,128)S(1)} %shard_map.95.refs_0_), channel_id=1, source_target_pairs={{0,8},{8,16},{16,24},{24,32},{32,40},{40,48},{48,56},{56,0},{1,9},... | collective-permute-start | bytes 393224 | tf_op jit(solution)/shard_map/ppermute | solution.py:165
  34.6 4.2 %collective-permute-start.5 = (f32[256,128]{1,0:T(8,128)S(1)}, f32[256,128]{1,0:T(8,128)S(1)}, u32[]{:S(2)}, u32[]{:S(2)}) collective-permute-start(f32[256,128]{1,0:T(8,128)S(1)} %shard_map.95.refs_0_), channel_id=1, source_target_pairs={{0,16},{8,24},{16,32},{24,40},{32,48},{40,56},{48,0},{56,8},{1,17}... | collective-permute-start | bytes 393224 | tf_op jit(solution)/shard_map/ppermute | solution.py:165
  38.8 4.6 %collective-permute-start.4 = (f32[256,128]{1,0:T(8,128)S(1)}, f32[256,128]{1,0:T(8,128)S(1)}, u32[]{:S(2)}, u32[]{:S(2)}) collective-permute-start(f32[256,128]{1,0:T(8,128)S(1)} %shard_map.95.refs_0_), channel_id=1, source_target_pairs={{0,24},{8,32},{16,40},{24,48},{32,56},{40,0},{48,8},{56,16},{1,25}... | collective-permute-start | bytes 393224 | tf_op jit(solution)/shard_map/ppermute | solution.py:165
  43.5 3.5 %collective-permute-start.3 = (f32[256,128]{1,0:T(8,128)S(1)}, f32[256,128]{1,0:T(8,128)S(1)}, u32[]{:S(2)}, u32[]{:S(2)}) collective-permute-start(f32[256,128]{1,0:T(8,128)S(1)} %shard_map.95.refs_0_), channel_id=1, source_target_pairs={{0,32},{8,40},{16,48},{24,56},{32,0},{40,8},{48,16},{56,24},{1,33}... | collective-permute-start | bytes 393224 | tf_op jit(solution)/shard_map/ppermute | solution.py:165
  47.0 4.9 %collective-permute-start.2 = (f32[256,128]{1,0:T(8,128)S(1)}, f32[256,128]{1,0:T(8,128)S(1)}, u32[]{:S(2)}, u32[]{:S(2)}) collective-permute-start(f32[256,128]{1,0:T(8,128)S(1)} %shard_map.95.refs_0_), channel_id=1, source_target_pairs={{0,40},{8,48},{16,56},{24,0},{32,8},{40,16},{48,24},{56,32},{1,41}... | collective-permute-start | bytes 393224 | tf_op jit(solution)/shard_map/ppermute | solution.py:165
  51.9 0.0 collective-permute-done.6.refs_7_
  51.9 5.0 %collective-permute-start.1 = (f32[256,128]{1,0:T(8,128)S(1)}, f32[256,128]{1,0:T(8,128)S(1)}, u32[]{:S(2)}, u32[]{:S(2)}) collective-permute-start(f32[256,128]{1,0:T(8,128)S(1)} %shard_map.95.refs_0_), channel_id=1, source_target_pairs={{0,48},{8,56},{16,0},{24,8},{32,16},{40,24},{48,32},{56,40},{1,49}... | collective-permute-start | bytes 393224 | tf_op jit(solution)/shard_map/ppermute | solution.py:165
  56.9 0.0 collective-permute-done.5.refs_6_
  56.9 3.0 %collective-permute-start = (f32[256,128]{1,0:T(8,128)S(1)}, f32[256,128]{1,0:T(8,128)S(1)}, u32[]{:S(2)}, u32[]{:S(2)}) collective-permute-start(f32[256,128]{1,0:T(8,128)S(1)} %shard_map.95.refs_0_), channel_id=1, source_target_pairs={{0,56},{8,0},{16,8},{24,16},{32,24},{40,32},{48,40},{56,48},{1,57}... | collective-permute-start | bytes 393224 | tf_op jit(solution)/shard_map/ppermute | solution.py:165
  59.9 0.0 collective-permute-done.4.refs_5_
  59.9 0.0 collective-permute-done.3.refs_4_
  59.9 5.2 %collective-permute-done.2.refs_3_ = f32[256,128]{1,0:T(8,128)S(1)} collective-permute-done((f32[256,128]{1,0:T(8,128)S(1)}, f32[256,128]{1,0:T(8,128)S(1)}, u32[]{:S(2)}, u32[]{:S(2)}) %collective-permute-start.2) | collective-permute-done | bytes 131104 | tf_op jit(solution)/shard_map/ppermute | solution.py:165
  65.1 5.4 %collective-permute-done.1.refs_2_ = f32[256,128]{1,0:T(8,128)S(1)} collective-permute-done((f32[256,128]{1,0:T(8,128)S(1)}, f32[256,128]{1,0:T(8,128)S(1)}, u32[]{:S(2)}, u32[]{:S(2)}) %collective-permute-start.1) | collective-permute-done | bytes 131104 | tf_op jit(solution)/shard_map/ppermute | solution.py:165
  70.5 1.4 %collective-permute-done.refs_1_ = f32[256,128]{1,0:T(8,128)S(1)} collective-permute-done((f32[256,128]{1,0:T(8,128)S(1)}, f32[256,128]{1,0:T(8,128)S(1)}, u32[]{:S(2)}, u32[]{:S(2)}) %collective-permute-start) | collective-permute-done | bytes 131104 | tf_op jit(solution)/shard_map/ppermute | solution.py:165
  71.9 0.0 all-to-all-done
  71.9 1.3 shard_map.96
  73.2 32.4 %all_to_all.15.part_ref = f32[8,264,128]{2,1,0:T(8,128)} all-to-all(f32[8,264,128]{2,1,0:T(8,128)S(1)} %get-tuple-element.13), channel_id=1, replica_groups=mesh['group'=16,'y'=8,'xc'=8] {'y'}, dimensions={0} | all-to-all | bytes 2162688 | tf_op jit(solution)/shard_map/all_to_all | solution.py:181
  105.6 0.0 copy-start.10
  105.6 1.5 %shard_map.98 = f32[128,1,128]{2,1,0:T(1,128)} custom-call(f32[8,264,128]{2,1,0:T(8,128)} %all_to_all.15.part_ref), custom_call_target="tpu_custom_call" | custom-call | tf_op jit(solution)/shard_map/pallas_call | solution.py:183
  107.1 17.6 %all-to-all-start.2 = ((f32[128,1,128]{2,1,0:T(1,128)}), f32[128,1,128]{2,1,0:T(1,128)S(1)}, u32[]{:S(2)}, u32[]{:S(2)}) async-start(f32[128,1,128]{2,1,0:T(1,128)} %shard_map.98), calls=%async_computation.2 | async-start | bytes 131072 | tf_op jit(solution)/shard_map/all_to_all | solution.py:190
  124.7 0.7 shard_map.97
  125.5 14.0 %all-to-all-done.2.terms_ref = f32[128,1,128]{2,1,0:T(1,128)S(1)} async-done(((f32[128,1,128]{2,1,0:T(1,128)}), f32[128,1,128]{2,1,0:T(1,128)S(1)}, u32[]{:S(2)}, u32[]{:S(2)}) %all-to-all-start.2) | async-done | bytes 65568 | tf_op jit(solution)/shard_map/all_to_all | solution.py:190
  139.5 1.3 shard_map.99
  (17 shorter events, 0.1 us)
Async XLA Ops:
  0.6 71.3 %copy-start.1 = (bf16[1,1024,896]{2,1,0:T(8,128)(2,1)S(1)}, bf16[1,1024,896]{2,1,0:T(8,128)(2,1)}, u32[]{:S(2)}) copy-start(bf16[1,1024,896]{2,1,0:T(8,128)(2,1)} %param.11) | copy-start | bytes 5505028
  0.6 0.9 copy-start.6
  1.5 0.7 copy-start.7
  2.2 0.7 copy-start.9
  2.9 0.7 copy-start.11
  5.6 66.3 %all-to-all-start = ((bf16[128,16,128]{2,1,0:T(8,128)(2,1)}), bf16[128,16,128]{2,1,0:T(8,128)(2,1)S(1)}, u32[]{:S(2)}, u32[]{:S(2)}) async-start(bf16[128,16,128]{2,1,0:T(8,128)(2,1)} %shard_map.94), calls=%async_computation | async-start | bytes 1048576 | tf_op jit(solution)/shard_map/all_to_all | solution.py:161
  29.7 0.8 copy-start.2
  30.5 0.8 copy-start.4
  31.4 20.5 %collective-permute-start.6 = (f32[256,128]{1,0:T(8,128)S(1)}, f32[256,128]{1,0:T(8,128)S(1)}, u32[]{:S(2)}, u32[]{:S(2)}) collective-permute-start(f32[256,128]{1,0:T(8,128)S(1)} %shard_map.95.refs_0_), channel_id=1, source_target_pairs={{0,8},{8,16},{16,24},{24,32},{32,40},{40,48},{48,56},{56,0},{1,9},... | collective-permute-start | bytes 393224 | tf_op jit(solution)/shard_map/ppermute | solution.py:165
  34.6 22.3 %collective-permute-start.5 = (f32[256,128]{1,0:T(8,128)S(1)}, f32[256,128]{1,0:T(8,128)S(1)}, u32[]{:S(2)}, u32[]{:S(2)}) collective-permute-start(f32[256,128]{1,0:T(8,128)S(1)} %shard_map.95.refs_0_), channel_id=1, source_target_pairs={{0,16},{8,24},{16,32},{24,40},{32,48},{40,56},{48,0},{56,8},{1,17}... | collective-permute-start | bytes 393224 | tf_op jit(solution)/shard_map/ppermute | solution.py:165
  38.8 21.1 %collective-permute-start.4 = (f32[256,128]{1,0:T(8,128)S(1)}, f32[256,128]{1,0:T(8,128)S(1)}, u32[]{:S(2)}, u32[]{:S(2)}) collective-permute-start(f32[256,128]{1,0:T(8,128)S(1)} %shard_map.95.refs_0_), channel_id=1, source_target_pairs={{0,24},{8,32},{16,40},{24,48},{32,56},{40,0},{48,8},{56,16},{1,25}... | collective-permute-start | bytes 393224 | tf_op jit(solution)/shard_map/ppermute | solution.py:165
  43.5 16.4 %collective-permute-start.3 = (f32[256,128]{1,0:T(8,128)S(1)}, f32[256,128]{1,0:T(8,128)S(1)}, u32[]{:S(2)}, u32[]{:S(2)}) collective-permute-start(f32[256,128]{1,0:T(8,128)S(1)} %shard_map.95.refs_0_), channel_id=1, source_target_pairs={{0,32},{8,40},{16,48},{24,56},{32,0},{40,8},{48,16},{56,24},{1,33}... | collective-permute-start | bytes 393224 | tf_op jit(solution)/shard_map/ppermute | solution.py:165
  47.0 18.1 %collective-permute-start.2 = (f32[256,128]{1,0:T(8,128)S(1)}, f32[256,128]{1,0:T(8,128)S(1)}, u32[]{:S(2)}, u32[]{:S(2)}) collective-permute-start(f32[256,128]{1,0:T(8,128)S(1)} %shard_map.95.refs_0_), channel_id=1, source_target_pairs={{0,40},{8,48},{16,56},{24,0},{32,8},{40,16},{48,24},{56,32},{1,41}... | collective-permute-start | bytes 393224 | tf_op jit(solution)/shard_map/ppermute | solution.py:165
  51.9 18.6 %collective-permute-start.1 = (f32[256,128]{1,0:T(8,128)S(1)}, f32[256,128]{1,0:T(8,128)S(1)}, u32[]{:S(2)}, u32[]{:S(2)}) collective-permute-start(f32[256,128]{1,0:T(8,128)S(1)} %shard_map.95.refs_0_), channel_id=1, source_target_pairs={{0,48},{8,56},{16,0},{24,8},{32,16},{40,24},{48,32},{56,40},{1,49}... | collective-permute-start | bytes 393224 | tf_op jit(solution)/shard_map/ppermute | solution.py:165
  56.9 15.0 %collective-permute-start = (f32[256,128]{1,0:T(8,128)S(1)}, f32[256,128]{1,0:T(8,128)S(1)}, u32[]{:S(2)}, u32[]{:S(2)}) collective-permute-start(f32[256,128]{1,0:T(8,128)S(1)} %shard_map.95.refs_0_), channel_id=1, source_target_pairs={{0,56},{8,0},{16,8},{24,16},{32,24},{40,32},{48,40},{56,48},{1,57}... | collective-permute-start | bytes 393224 | tf_op jit(solution)/shard_map/ppermute | solution.py:165
  105.6 19.1 %copy-start = (f32[8,264,128]{2,1,0:T(8,128)S(1)}, f32[8,264,128]{2,1,0:T(8,128)}, u32[]{:S(2)}) copy-start(f32[8,264,128]{2,1,0:T(8,128)} %all_to_all.15.part_ref) | copy-start | bytes 3244036
  105.6 19.1 %copy-start.3 = (bf16[1,256,128]{2,1,0:T(8,128)(2,1)S(1)}, bf16[1,256,128]{2,1,0:T(8,128)(2,1)}, u32[]{:S(2)}) copy-start(bf16[1,256,128]{2,1,0:T(8,128)(2,1)} %param.12) | copy-start | bytes 196612
  105.6 19.1 %copy-start.5 = (bf16[1,256,128]{2,1,0:T(8,128)(2,1)S(1)}, bf16[1,256,128]{2,1,0:T(8,128)(2,1)}, u32[]{:S(2)}) copy-start(bf16[1,256,128]{2,1,0:T(8,128)(2,1)} %param.13) | copy-start | bytes 196612
  105.6 33.9 %copy-start.8 = (s32[128,8]{0,1:T(8,128)S(1)}, s32[128,8]{0,1:T(8,128)}, u32[]{:S(2)}) copy-start(s32[128,8]{0,1:T(8,128)} %param.8) | copy-start | bytes 12292
  105.6 33.9 %copy-start.10 = (s32[128,8]{0,1:T(8,128)S(1)}, s32[128,8]{0,1:T(8,128)}, u32[]{:S(2)}) copy-start(s32[128,8]{0,1:T(8,128)} %param.9) | copy-start | bytes 12292
  107.1 32.4 %all-to-all-start.2 = ((f32[128,1,128]{2,1,0:T(1,128)}), f32[128,1,128]{2,1,0:T(1,128)S(1)}, u32[]{:S(2)}, u32[]{:S(2)}) async-start(f32[128,1,128]{2,1,0:T(1,128)} %shard_map.98), calls=%async_computation.2 | async-start | bytes 131072 | tf_op jit(solution)/shard_map/all_to_all | solution.py:190

commit v3 on v2

v3 whole, which is shorter than its diff:
```python
import jax
import jax.numpy as jnp
from jax import lax
from jax.experimental import pallas as pl
from jax.experimental.pallas import tpu as pltpu
from jax.sharding import Mesh, PartitionSpec as P

EXP_GRP = 8
SLOTS = 16
NT = (((1,), (1,)), ((), ()))
F32 = jnp.float32
BF16 = jnp.bfloat16


def lanes(shape):
    return lax.broadcasted_iota(jnp.int32, shape, len(shape) - 1)


def rows(shape):
    return lax.broadcasted_iota(jnp.int32, shape, 0)


def dispatch_kernel(tokens_ref, routes_ref, slots_ref, gates_ref, out_ref):
    col_width, tok_count = tokens_ref.shape
    lane_count = out_ref.shape[2]
    place = routes_ref[...] * SLOTS + slots_ref[...]
    gates = gates_ref[...].astype(F32)
    spare = (lane_count - col_width, tok_count)
    features = jnp.concatenate([tokens_ref[...], jnp.zeros(spare, BF16)], axis=0)
    marks = jnp.where(rows((lane_count, tok_count)) == col_width, 1.0, 0.0).astype(BF16)
    source = jnp.concatenate([features, marks], axis=1)
    chunk = 256
    for start in range(0, out_ref.shape[0] * SLOTS, chunk):
        row_ids = rows((chunk, tok_count)) + start
        pick = jnp.zeros((chunk, tok_count), F32)
        gate = jnp.zeros((chunk, tok_count), F32)
        for k in range(place.shape[0]):
            hit = row_ids == place[k : k + 1, :]
            pick = jnp.where(hit, 1.0, pick)
            gate = jnp.where(hit, gates[k : k + 1, :], gate)
        both = jnp.concatenate([pick.astype(BF16), gate.astype(BF16)], axis=1)
        block = lax.dot_general(both, source, NT, preferred_element_type=F32)
        out_ref[start // SLOTS : (start + chunk) // SLOTS] = block.astype(BF16).reshape(
            chunk // SLOTS, SLOTS, lane_count
        )


def hidden_kernel(gate_ref, up_ref, out_ref):
    gate_pre = gate_ref[...].astype(F32)
    out_ref[...] = gate_pre * jax.nn.sigmoid(gate_pre) * up_ref[...].astype(F32)


def matmul_kernel(where_ref, rows_ref, w_ref, same_ref, other_ref, give_ref, *outs):
    keep_refs, (term_ref, gate_ref) = outs[:-2], outs[-2:]
    groups, parts, _, lane_count = rows_ref.shape
    capacity = groups * SLOTS
    col_width = w_ref.shape[1] // parts
    group, shard = where_ref[0], where_ref[1]
    own, quad = shard % 2, shard // 2
    quads = give_ref.shape[0]
    blocks = [rows_ref[:, e].reshape(capacity, lane_count) for e in range(parts)]
    x = jnp.concatenate([b[:, :col_width] for b in blocks], axis=1)
    terms = jnp.zeros((capacity, lane_count), F32)
    for d in range(quads):
        target = (quad + d) % quads
        for mine, hidden_ref in ((0, other_ref), (1, same_ref)):
            unit = target * 2 + (own if mine else 1 - own)
            first = pl.multiple_of(unit * lane_count, lane_count)
            part = lax.dot_general(
                x, w_ref[pl.ds(first, lane_count), :], NT, preferred_element_type=F32
            )
            terms += part * hidden_ref[target]
            if mine:
                keep_refs[d][...] = part
            else:
                give_ref[d] = part
    total = jnp.sum(terms, axis=1, keepdims=True)
    row_ids, lane_ids = rows((capacity, lane_count)), lanes((capacity, lane_count))
    hit = lane_ids == group % (lane_count // SLOTS) * SLOTS + row_ids % SLOTS
    term_ref[...] = jnp.sum(
        jnp.where(hit, total, 0.0).reshape(groups, SLOTS, lane_count), axis=1, keepdims=True
    )
    gate = jnp.where(lane_ids == col_width, blocks[0].astype(F32), 0.0)
    gate_ref[...] = jnp.broadcast_to(
        jnp.sum(gate, axis=1, keepdims=True), (capacity, lane_count)
    )


def spread_kernel(home_ref, out_ref):
    groups, _, lane_count = home_ref.shape
    half = groups // 2
    home = jnp.sum(home_ref[...].reshape(2, half, lane_count), axis=1)
    out_ref[...] = jnp.broadcast_to(home[None], out_ref.shape)


def output_kernel(h0, h1, h2, h3, gate_ref, gate_pre_ref, up_pre_ref, grad_gate_ref, grad_up_ref):
    hidden_grad = h0[...] + h1[...] + h2[...] + h3[...]
    gate_pre = gate_pre_ref[...].astype(F32)
    up_pre = up_pre_ref[...].astype(F32)
    sigmoid_gate = jax.nn.sigmoid(gate_pre)
    scaled = gate_ref[...] * hidden_grad
    grad_up_ref[...] = (scaled * gate_pre * sigmoid_gate).astype(BF16)
    grad_gate_ref[...] = (
        scaled * up_pre * sigmoid_gate * (1.0 + gate_pre * (1.0 - sigmoid_gate))
    ).astype(BF16)


def collect_kernel(terms_ref, routes_ref, slots_ref, out_ref):
    shard_count, experts, halves, lane_count = terms_ref.shape
    route_count, tok_count = routes_ref.shape
    table = terms_ref[0]
    for s in range(1, shard_count):
        table += terms_ref[s]
    routes = routes_ref[...]
    place = routes // EXP_GRP * SLOTS + slots_ref[...]
    for k in range(route_count):
        picked = jnp.zeros((experts, tok_count), F32)
        for h in range(halves):
            hit = rows((lane_count, tok_count)) + h * lane_count == place[k : k + 1, :]
            picked += jnp.dot(
                table[:, h, :],
                jnp.where(hit, 1.0, 0.0),
                preferred_element_type=F32,
                precision=lax.Precision.HIGHEST,
            )
        own = rows((experts, tok_count)) == routes[k : k + 1, :] % EXP_GRP
        out_ref[k : k + 1, :] = jnp.sum(jnp.where(own, picked, 0.0), axis=0, keepdims=True)


VMEM = pl.BlockSpec(memory_space=pltpu.VMEM)
SMEM = pl.BlockSpec(memory_space=pltpu.SMEM)


def call(kernel, specs, out_shape, *args):
    return pl.pallas_call(
        kernel,
        in_specs=specs,
        out_specs=jax.tree.map(lambda _: VMEM, out_shape),
        out_shape=out_shape,
        compiler_params=pltpu.CompilerParams(vmem_limit_bytes=24 << 20),
    )(*args)


def shards(grad_out, routes, slots, gates, w_down, saved_gate, saved_up):
    shape = jax.ShapeDtypeStruct
    groups, shard_count, parts = (lax.axis_size(a) for a in ("group", "y", "xc"))
    capacity, lane_count = saved_gate.shape[1:]
    group = lax.axis_index("group").astype(jnp.int32)
    shard = lax.axis_index("y").astype(jnp.int32)
    column = shape((capacity, lane_count), F32)

    send = call(
        dispatch_kernel,
        [VMEM] * 4,
        shape((groups * parts, SLOTS, lane_count), BF16),
        grad_out.T,
        routes.T,
        slots.T,
        gates.T,
    )
    send, gate_pre, up_pre = lax.optimization_barrier((send, saved_gate[0], saved_up[0]))
    expert_rows = lax.all_to_all(send, ("group", "xc"), 0, 0, tiled=True)

    hidden = call(hidden_kernel, [VMEM] * 2, column, gate_pre, up_pre)
    same = lax.all_gather(
        hidden, "y", axis_index_groups=[list(range(p, shard_count, 2)) for p in (0, 1)]
    )
    other = lax.ppermute(same, "y", [(i, i ^ 1) for i in range(shard_count)])
    give, k0, k1, k2, k3, terms, gate_rows = call(
        matmul_kernel,
        [SMEM] + [VMEM] * 4,
        (
            shape((shard_count // 2, capacity, lane_count), F32),
            *[column] * 4,
            shape((groups, 1, lane_count), F32),
            column,
        ),
        jnp.stack([group, shard]),
        expert_rows.reshape(groups, parts, SLOTS, lane_count),
        w_down[0],
        same,
        other,
    )

    got = lax.ppermute(give, "y", [(i, i ^ 1) for i in range(shard_count)])
    home = lax.all_to_all(terms, "group", 0, 0, tiled=True)
    sums = [k + got[d] for d, k in enumerate((k0, k1, k2, k3))]
    for d in (2, 1, 3):
        sums[d] = lax.ppermute(
            sums[d], "y", [(i, (i + 2 * d) % shard_count) for i in range(shard_count)]
        )
    spread = call(
        spread_kernel, [VMEM], shape((shard_count * parts, 2, lane_count), F32), home
    )
    every_term = lax.all_to_all(spread, ("y", "xc"), 0, 0, tiled=True)
    out = shape((capacity, lane_count), BF16)
    grad_gate, grad_up = call(
        output_kernel, [VMEM] * 7, (out, out), *sums, gate_rows, saved_gate[0], saved_up[0]
    )
    grad_gates = call(
        collect_kernel,
        [VMEM] * 3,
        shape(routes.shape[::-1], F32),
        every_term.reshape(shard_count, parts, 2, lane_count),
        routes.T,
        slots.T,
    )
    return (grad_gate[None], grad_up[None], grad_gates.T)


def solution(mesh):
    fine = Mesh(mesh.devices.reshape(mesh.shape["group"], -1, EXP_GRP), ("group", "y", "xc"))
    local, device = ("y", "xc"), ("group", "y", "xc")
    return jax.shard_map(
        shards,
        mesh=fine,
        in_specs=(
            P("group", local),
            P("group", None),
            P("group", None),
            P("group", None),
            P(device, None, None),
            P(device, None, None),
            P(device, None, None),
        ),
        out_specs=(P(device, None, None), P(device, None, None), P("group", None)),
        check_vma=False,
    )
```

time: 141 us -> 120 us (0.85)
  starting transfers between devices: 70 us -> 54.4 us
  waiting for transfers between devices: 26 us -> 10.8 us
  blocking collectives: 32.4 us -> 37.2 us
  local copies, waits for them, and re-layouts: 4.63 us -> 7.87 us
    all_gather x0 -> x1, blocking collectives: none -> 16 us  [shards(): lax.all_gather(hidden, 'y', axis_index_groups=[list(range(p, shard_count,...]
    all_to_all x1, waiting for transfers between devices: 14 us -> 0.01 us  [shards(): home = lax.all_to_all(terms, 'group', 0, 0, tiled=True)]
    all_to_all x1, blocking collectives: 32.4 us -> 21.2 us  [shards(): every_term = lax.all_to_all(spread, ('y', 'xc'), 0, 0, tiled=True)]
    ppermute x7 -> x5, starting transfers between devices: 28.4 us -> 19.3 us  [the longest x3 13.7 us: shards(): lax.ppermute(sums[d], 'y', [(i, (i + 2 * d) % shard_count) for i in range...]
    all_to_all x1, starting transfers between devices: 17.6 us -> 11.1 us  [shards(): home = lax.all_to_all(terms, 'group', 0, 0, tiled=True)]
    ppermute x7 -> x5, waiting for transfers between devices: 12 us -> 8.4 us  [the longest x1 8.39 us: shards(): other = lax.ppermute(same, 'y', [(i, i ^ 1) for i in range(shard_count)])]
    unnamed x24 -> x34, local copies, waits for them, and re-layouts: 4.63 us -> 7.87 us
    all_to_all x1, waiting for transfers between devices: 0.01 us -> 2.38 us  [shards(): expert_rows = lax.all_to_all(send, ('group', 'xc'), 0, 0, tiled=True)]
  transfers between devices with their start and end apart: 9 -> 7, of which waited for: 4 -> 2; matrix products, arithmetic and copies ran while one was open for 0% -> 1% of each run, Pallas kernels for 1% -> 1%
where the time goes in v3:
time: 120 us; the launch traced here: 119 us
  starting transfers between devices  54.4 us (45%)
  blocking collectives  37.2 us (31%)
  waiting for transfers between devices  10.8 us (9%)
  local copies, waits for them, and re-layouts  7.87 us (7%)
  Pallas kernels  6.87 us (6%)
  other arithmetic  1.23 us (1%)
    all_to_all x1, starting transfers between devices, shards(): expert_rows = lax.all_to_all(send, ('group', 'xc'), 0, 0, tiled=True)  24.1 us
    all_to_all x1, blocking collectives, shards(): every_term = lax.all_to_all(spread, ('y', 'xc'), 0, 0, tiled=True)  21.2 us
    all_gather x1, blocking collectives, shards(): lax.all_gather(hidden, 'y', axis_index_groups=[list(range(p, shard_count,...  16 us
    ppermute x3, starting transfers between devices, shards(): lax.ppermute(sums[d], 'y', [(i, (i + 2 * d) % shard_count) for i in range...  13.7 us
    all_to_all x1, starting transfers between devices, shards(): home = lax.all_to_all(terms, 'group', 0, 0, tiled=True)  11.1 us
    ppermute x1, waiting for transfers between devices, shards(): other = lax.ppermute(same, 'y', [(i, i ^ 1) for i in range(shard_count)])  8.39 us
    unnamed x34, local copies, waits for them, and re-layouts  7.87 us
    pallas_call x6, Pallas kernels, call(): pl.pallas_call(kernel, in_specs=specs, out_specs=jax.tree.map(lambda _: V...  6.87 us
  transfers between devices with their start and end apart: 7, of which 2 were waited for; matrix products, arithmetic and copies ran while one was open for 1% of the time, Pallas kernels for 1%

profile of v3, /device:TPU:1, one launch (start us, length us, event | category | flops | bytes accessed | tf_op | source)
XLA Modules:
  0.0 119.1 jit_solution(16919758403053027421)
XLA Ops:
  0.7 0.9 copy-done.11
  1.5 0.7 copy-done.12
  2.2 0.7 copy-done.14
  2.9 0.7 copy-done.16
  3.6 2.0 %shard_map.94 = bf16[128,16,128]{2,1,0:T(8,128)(2,1)} custom-call(bf16[112,128]{1,0:T(8,128)(2,1)S(1)} %bitcast.40, s32[8,128]{1,0:T(8,128)S(1)} %bitcast.41, s32[8,128]{1,0:T(8,128)S(1)} %bitcast.43, bf16[8,128]{1,0:T(8,128)(2,1)S(1)} %bitcast.45), custom_call_target="tpu_custom_call" | custom-call | tf_op jit(solution)/shard_map/pallas_call | solution.py:135
  5.6 24.1 %all-to-all-start = ((bf16[128,16,128]{2,1,0:T(8,128)(2,1)}), bf16[128,16,128]{2,1,0:T(8,128)(2,1)S(1)}, u32[]{:S(2)}, u32[]{:S(2)}) async-start(bf16[128,16,128]{2,1,0:T(8,128)(2,1)} %shard_map.94), calls=%async_computation | async-start | bytes 1048576 | tf_op jit(solution)/shard_map/all_to_all | solution.py:162
  29.7 0.0 copy-start.1
  29.7 0.8 copy-done.1
  30.5 0.8 copy-done.3
  31.4 16.0 %all-gather = f32[1024,128]{1,0:T(8,128)S(1)} all-gather(f32[256,128]{1,0:T(8,128)S(1)} %shard_map.95), channel_id=2, replica_groups={{0,16,32,48},{8,24,40,56},{1,17,33,49},{9,25,41,57},{2,18,34,50},{10,26..., dimensions={0}, use_global_device_ids=true | all-gather | bytes 655360 | tf_op jit(solution)/shard_map/all_gather | solution.py:165
  47.3 2.3 %collective-permute-start = (f32[4,256,128]{2,1,0:T(8,128)S(1)}, f32[4,256,128]{2,1,0:T(8,128)S(1)}, u32[]{:S(2)}, u32[]{:S(2)}) collective-permute-start(f32[4,256,128]{2,1,0:T(8,128)S(1)} %bitcast.31), channel_id=1, source_target_pairs={{0,8},{8,0},{16,24},{24,16},{32,40},{40,32},{48,56},{56,48},{1,9},... | collective-permute-start | bytes 1572872 | tf_op jit(solution)/shard_map/ppermute | solution.py:168
  49.6 0.1 pad_add_fusion.where_ref
  49.7 8.4 %collective-permute-done.other_ref = f32[4,256,128]{2,1,0:T(8,128)S(1)} collective-permute-done((f32[4,256,128]{2,1,0:T(8,128)S(1)}, f32[4,256,128]{2,1,0:T(8,128)S(1)}, u32[]{:S(2)}, u32[]{:S(2)}) %collective-permute-start) | collective-permute-done | bytes 524320 | tf_op jit(solution)/shard_map/ppermute | solution.py:168
  58.1 2.4 %all-to-all-done = bf16[128,16,128]{2,1,0:T(8,128)(2,1)S(1)} async-done(((bf16[128,16,128]{2,1,0:T(8,128)(2,1)}), bf16[128,16,128]{2,1,0:T(8,128)(2,1)S(1)}, u32[]{:S(2)}, u32[]{:S(2)}) %all-to-all-start) | async-done | bytes 524320 | tf_op jit(solution)/shard_map/all_to_all | solution.py:162
  60.5 0.0 copy-start.4
  60.5 2.5 %shard_map.96 = (f32[4,256,128]{2,1,0:T(8,128)}, f32[256,128]{1,0:T(8,128)S(1)}, f32[256,128]{1,0:T(8,128)S(1)}, f32[256,128]{1,0:T(8,128)S(1)}, f32[256,128]{1,...) custom-call(s32[2]{0:T(128)S(1)} %pad_add_fusion.where_ref, bf16[16,8,16,128]{3,2,1,0:T(8,128)(2,1)S(1)} %bitcast.33, ...), custom_call_target="tpu_custom_call" | custom-call | tf_op jit(solution)/shard_map/pallas_call | solution.py:135
  63.0 0.7 copy-done.5
  63.7 0.6 copy-done.6
  64.3 0.6 copy-done.7
  65.0 0.7 copy-done.8
  65.6 0.6 copy-done.9
  66.3 3.3 %collective-permute-start.1 = (f32[4,256,128]{2,1,0:T(8,128)}, f32[4,256,128]{2,1,0:T(8,128)S(1)}, u32[]{:S(2)}, u32[]{:S(2)}) collective-permute-start(f32[4,256,128]{2,1,0:T(8,128)} %get-tuple-element.19), channel_id=1, source_target_pairs={{0,8},{8,0},{16,24},{24,16},{32,40},{40,32},{48,56},{56,48},{1,9},... | collective-permute-start | bytes 1572872 | tf_op jit(solution)/shard_map/ppermute | solution.py:185
  69.6 11.1 %all-to-all-start.1 = ((f32[16,1,128]{2,1,0:T(1,128)}), f32[16,1,128]{2,1,0:T(1,128)S(1)}, u32[]{:S(2)}, u32[]{:S(2)}) async-start(f32[16,1,128]{2,1,0:T(1,128)} %get-tuple-element.26), calls=%async_computation.1 | async-start | bytes 16384 | tf_op jit(solution)/shard_map/all_to_all | solution.py:186
  80.7 0.0 collective-permute-done.1
  80.7 1.2 fusion
  81.8 5.7 %collective-permute-start.4 = (f32[256,128]{1,0:T(8,128)S(1)}, f32[256,128]{1,0:T(8,128)S(1)}, u32[]{:S(2)}, u32[]{:S(2)}) collective-permute-start(f32[256,128]{1,0:T(8,128)S(1)} %get-tuple-element.27), channel_id=1, source_target_pairs={{0,48},{8,56},{16,0},{24,8},{32,16},{40,24},{48,32},{56,40},{1,49}... | collective-permute-start | bytes 393224 | tf_op jit(solution)/shard_map/ppermute | solution.py:189
  87.5 5.5 %collective-permute-start.3 = (f32[256,128]{1,0:T(8,128)S(1)}, f32[256,128]{1,0:T(8,128)S(1)}, u32[]{:S(2)}, u32[]{:S(2)}) collective-permute-start(f32[256,128]{1,0:T(8,128)S(1)} %get-tuple-element.28), channel_id=1, source_target_pairs={{0,32},{8,40},{16,48},{24,56},{32,0},{40,8},{48,16},{56,24},{1,33}... | collective-permute-start | bytes 393224 | tf_op jit(solution)/shard_map/ppermute | solution.py:189
  93.1 2.5 %collective-permute-start.2 = (f32[256,128]{1,0:T(8,128)S(1)}, f32[256,128]{1,0:T(8,128)S(1)}, u32[]{:S(2)}, u32[]{:S(2)}) collective-permute-start(f32[256,128]{1,0:T(8,128)S(1)} %get-tuple-element.29), channel_id=1, source_target_pairs={{0,16},{8,24},{16,32},{24,40},{32,48},{40,56},{48,0},{56,8},{1,17}... | collective-permute-start | bytes 393224 | tf_op jit(solution)/shard_map/ppermute | solution.py:189
  95.5 0.0 all-to-all-done.1.home_ref
  95.6 21.2 %all_to_all.15 = f32[64,2,128]{2,1,0:T(2,128)S(1)} all-to-all(f32[64,2,128]{2,1,0:T(2,128)S(1)} %shard_map.98), channel_id=1, replica_groups=mesh['group'=16,'y'=8,'xc'=8] {'y','xc'}, dimensions={0} | all-to-all | bytes 131072 | tf_op jit(solution)/shard_map/all_to_all | solution.py:195
  116.8 1.6 %shard_map.99 = f32[8,128]{1,0:T(8,128)} custom-call(f32[8,8,2,128]{3,2,1,0:T(2,128)S(1)} %bitcast.39, s32[8,128]{1,0:T(8,128)S(1)} %bitcast.42, s32[8,128]{1,0:T(8,128)S(1)} %bitcast.44), custom_call_target="tpu_custom_call" | custom-call | tf_op jit(solution)/shard_map/pallas_call | solution.py:135
  118.4 0.7 shard_map.97
  (26 shorter events, 0.1 us)
Async XLA Ops:
  0.6 59.8 %copy-start = (bf16[1,1024,896]{2,1,0:T(8,128)(2,1)S(1)}, bf16[1,1024,896]{2,1,0:T(8,128)(2,1)}, u32[]{:S(2)}) copy-start(bf16[1,1024,896]{2,1,0:T(8,128)(2,1)} %param.11) | copy-start | bytes 5505028
  0.6 0.9 copy-start.11
  1.5 0.7 copy-start.12
  2.2 0.7 copy-start.14
  2.9 0.7 copy-start.16
  5.6 54.9 %all-to-all-start = ((bf16[128,16,128]{2,1,0:T(8,128)(2,1)}), bf16[128,16,128]{2,1,0:T(8,128)(2,1)S(1)}, u32[]{:S(2)}, u32[]{:S(2)}) async-start(bf16[128,16,128]{2,1,0:T(8,128)(2,1)} %shard_map.94), calls=%async_computation | async-start | bytes 1048576 | tf_op jit(solution)/shard_map/all_to_all | solution.py:162
  29.7 0.8 copy-start.1
  30.5 0.8 copy-start.3
  47.3 10.8 %collective-permute-start = (f32[4,256,128]{2,1,0:T(8,128)S(1)}, f32[4,256,128]{2,1,0:T(8,128)S(1)}, u32[]{:S(2)}, u32[]{:S(2)}) collective-permute-start(f32[4,256,128]{2,1,0:T(8,128)S(1)} %bitcast.31), channel_id=1, source_target_pairs={{0,8},{8,0},{16,24},{24,16},{32,40},{40,32},{48,56},{56,48},{1,9},... | collective-permute-start | bytes 1572872 | tf_op jit(solution)/shard_map/ppermute | solution.py:168
  60.5 56.3 %copy-start.13 = (s32[128,8]{0,1:T(8,128)S(1)}, s32[128,8]{0,1:T(8,128)}, u32[]{:S(2)}) copy-start(s32[128,8]{0,1:T(8,128)} %param.8) | copy-start | bytes 12292
  60.5 56.3 %copy-start.15 = (s32[128,8]{0,1:T(8,128)S(1)}, s32[128,8]{0,1:T(8,128)}, u32[]{:S(2)}) copy-start(s32[128,8]{0,1:T(8,128)} %param.9) | copy-start | bytes 12292
  60.5 57.9 %copy-start.2 = (bf16[1,256,128]{2,1,0:T(8,128)(2,1)S(1)}, bf16[1,256,128]{2,1,0:T(8,128)(2,1)}, u32[]{:S(2)}) copy-start(bf16[1,256,128]{2,1,0:T(8,128)(2,1)} %param.12) | copy-start | bytes 196612
  60.5 57.9 %copy-start.4 = (bf16[1,256,128]{2,1,0:T(8,128)(2,1)S(1)}, bf16[1,256,128]{2,1,0:T(8,128)(2,1)}, u32[]{:S(2)}) copy-start(bf16[1,256,128]{2,1,0:T(8,128)(2,1)} %param.13) | copy-start | bytes 196612
  63.0 0.7 copy-start.5
  63.7 0.6 copy-start.6
  64.3 0.6 copy-start.7
  65.0 0.7 copy-start.8
  65.6 0.6 copy-start.9
  66.3 52.1 %copy-start.10 = (f32[256,128]{1,0:T(8,128)S(1)}, f32[256,128]{1,0:T(8,128)}, u32[]{:S(2)}) copy-start(f32[256,128]{1,0:T(8,128)} %copy-done.9) | copy-start | bytes 393220
  66.3 14.4 %collective-permute-start.1 = (f32[4,256,128]{2,1,0:T(8,128)}, f32[4,256,128]{2,1,0:T(8,128)S(1)}, u32[]{:S(2)}, u32[]{:S(2)}) collective-permute-start(f32[4,256,128]{2,1,0:T(8,128)} %get-tuple-element.19), channel_id=1, source_target_pairs={{0,8},{8,0},{16,24},{24,16},{32,40},{40,32},{48,56},{56,48},{1,9},... | collective-permute-start | bytes 1572872 | tf_op jit(solution)/shard_map/ppermute | solution.py:185
  69.6 25.9 %all-to-all-start.1 = ((f32[16,1,128]{2,1,0:T(1,128)}), f32[16,1,128]{2,1,0:T(1,128)S(1)}, u32[]{:S(2)}, u32[]{:S(2)}) async-start(f32[16,1,128]{2,1,0:T(1,128)} %get-tuple-element.26), calls=%async_computation.1 | async-start | bytes 16384 | tf_op jit(solution)/shard_map/all_to_all | solution.py:186
  81.8 36.5 %collective-permute-start.4 = (f32[256,128]{1,0:T(8,128)S(1)}, f32[256,128]{1,0:T(8,128)S(1)}, u32[]{:S(2)}, u32[]{:S(2)}) collective-permute-start(f32[256,128]{1,0:T(8,128)S(1)} %get-tuple-element.27), channel_id=1, source_target_pairs={{0,48},{8,56},{16,0},{24,8},{32,16},{40,24},{48,32},{56,40},{1,49}... | collective-permute-start | bytes 393224 | tf_op jit(solution)/shard_map/ppermute | solution.py:189
  87.5 30.8 %collective-permute-start.3 = (f32[256,128]{1,0:T(8,128)S(1)}, f32[256,128]{1,0:T(8,128)S(1)}, u32[]{:S(2)}, u32[]{:S(2)}) collective-permute-start(f32[256,128]{1,0:T(8,128)S(1)} %get-tuple-element.28), channel_id=1, source_target_pairs={{0,32},{8,40},{16,48},{24,56},{32,0},{40,8},{48,16},{56,24},{1,33}... | collective-permute-start | bytes 393224 | tf_op jit(solution)/shard_map/ppermute | solution.py:189
  93.1 25.3 %collective-permute-start.2 = (f32[256,128]{1,0:T(8,128)S(1)}, f32[256,128]{1,0:T(8,128)S(1)}, u32[]{:S(2)}, u32[]{:S(2)}) collective-permute-start(f32[256,128]{1,0:T(8,128)S(1)} %get-tuple-element.29), channel_id=1, source_target_pairs={{0,16},{8,24},{16,32},{24,40},{32,48},{40,56},{48,0},{56,8},{1,17}... | collective-permute-start | bytes 393224 | tf_op jit(solution)/shard_map/ppermute | solution.py:189

commit v4 on v3

--- a/solution.py
+++ b/solution.py
@@ -50,40 +50,81 @@
     out_ref[...] = gate_pre * jax.nn.sigmoid(gate_pre) * up_ref[...].astype(F32)
 
 
-def matmul_kernel(where_ref, rows_ref, w_ref, same_ref, other_ref, give_ref, *outs):
-    keep_refs, (term_ref, gate_ref) = outs[:-2], outs[-2:]
+def matmul_kernel(where_ref, rows_in, w_in, same_in, other_in, *refs):
+    right_out, left_out, keep_out, gate_out, term_ref = refs[:5]
+    rows_ref, w_ref, same_ref, other_ref, part_ref, gate_ref, in_sems, out_sems = refs[5:]
     groups, parts, _, lane_count = rows_ref.shape
     capacity = groups * SLOTS
     col_width = w_ref.shape[1] // parts
+    count = part_ref.shape[0]
     group, shard = where_ref[0], where_ref[1]
-    own, quad = shard % 2, shard // 2
-    quads = give_ref.shape[0]
+    half = capacity // 2
+    low, high = slice(0, half), slice(half, capacity)
+    every = slice(0, capacity)
+    routes = (
+        (1, ((every, right_out, 0),)),
+        (count - 1, ((every, left_out, 0),)),
+        (count - 2, ((every, right_out, capacity),)),
+        (2, ((every, left_out, capacity),)),
+        (4, ((high, right_out, 2 * capacity), (low, left_out, 2 * capacity))),
+        (0, ((every, keep_out, 0),)),
+        (count - 3, ((every, keep_out, capacity),)),
+        (3, ((every, keep_out, 2 * capacity),)),
+    )
+    units = [(shard + offset) % count for offset, _ in routes]
+    arrivals = [pltpu.make_async_copy(rows_in, rows_ref, in_sems.at[0])]
+    for i, unit in enumerate(units):
+        span = pl.ds(pl.multiple_of(unit * lane_count, lane_count), lane_count)
+        arrivals.append(pltpu.make_async_copy(w_in.at[span], w_ref.at[span], in_sems.at[i + 1]))
+    arrivals.append(pltpu.make_async_copy(same_in, same_ref, in_sems.at[count + 1]))
+    arrivals.append(pltpu.make_async_copy(other_in, other_ref, in_sems.at[count + 2]))
+    for copy in arrivals:
+        copy.start()
+    arrivals[0].wait()
+    departures = []
+
+    def leave(source, target):
+        departures.append(pltpu.make_async_copy(source, target, out_sems.at[len(departures)]))
+        departures[-1].start()
+
     blocks = [rows_ref[:, e].reshape(capacity, lane_count) for e in range(parts)]
     x = jnp.concatenate([b[:, :col_width] for b in blocks], axis=1)
+    row_ids, lane_ids = rows((capacity, lane_count)), lanes((capacity, lane_count))
+    gate = jnp.where(lane_ids == col_width, blocks[0].astype(F32), 0.0)
+    gate_ref[...] = jnp.broadcast_to(
+        jnp.sum(gate, axis=1, keepdims=True), (capacity, lane_count)
+    )
+    leave(gate_ref, gate_out)
+    for i, (_, targets) in enumerate(routes):
+        arrivals[i + 1].wait()
+        span = pl.ds(pl.multiple_of(units[i] * lane_count, lane_count), lane_count)
+        part_ref[i] = lax.dot_general(x, w_ref[span, :], NT, preferred_element_type=F32)
+        for span, out, first in targets:
+            size = span.stop - span.start
+            leave(part_ref.at[i, span], out.at[first : first + size])
+    for copy in arrivals[count + 1 :]:
+        copy.wait()
     terms = jnp.zeros((capacity, lane_count), F32)
-    for d in range(quads):
-        target = (quad + d) % quads
-        for mine, hidden_ref in ((0, other_ref), (1, same_ref)):
-            unit = target * 2 + (own if mine else 1 - own)
-            first = pl.multiple_of(unit * lane_count, lane_count)
-            part = lax.dot_general(
-                x, w_ref[pl.ds(first, lane_count), :], NT, preferred_element_type=F32
-            )
-            terms += part * hidden_ref[target]
-            if mine:
-                keep_refs[d][...] = part
-            else:
-                give_ref[d] = part
+    for i, (offset, _) in enumerate(routes):
+        hidden_ref = other_ref if offset % 2 else same_ref
+        terms += part_ref[i] * hidden_ref[units[i] // 2]
     total = jnp.sum(terms, axis=1, keepdims=True)
-    row_ids, lane_ids = rows((capacity, lane_count)), lanes((capacity, lane_count))
     hit = lane_ids == group % (lane_count // SLOTS) * SLOTS + row_ids % SLOTS
     term_ref[...] = jnp.sum(
         jnp.where(hit, total, 0.0).reshape(groups, SLOTS, lane_count), axis=1, keepdims=True
     )
-    gate = jnp.where(lane_ids == col_width, blocks[0].astype(F32), 0.0)
-    gate_ref[...] = jnp.broadcast_to(
-        jnp.sum(gate, axis=1, keepdims=True), (capacity, lane_count)
-    )
+    for copy in departures:
+        copy.wait()
+
+
+def middle_kernel(left_ref, right_ref, keep_ref, down_ref, up_ref):
+    capacity = down_ref.shape[0]
+    half = capacity // 2
+    near = slice(capacity, 2 * capacity)
+    down_ref[...] = keep_ref[near] + left_ref[near]
+    down_ref[:half] += right_ref[2 * capacity :]
+    up_ref[...] = keep_ref[2 * capacity :] + right_ref[near]
+    up_ref[half:] += left_ref[2 * capacity :]
 
 
 def spread_kernel(home_ref, out_ref):
@@ -93,8 +134,11 @@
     out_ref[...] = jnp.broadcast_to(home[None], out_ref.shape)
 
 
-def output_kernel(h0, h1, h2, h3, gate_ref, gate_pre_ref, up_pre_ref, grad_gate_ref, grad_up_ref):
-    hidden_grad = h0[...] + h1[...] + h2[...] + h3[...]
+def output_kernel(
+    left_ref, right_ref, keep_ref, down_ref, up_ref, gate_ref, gate_pre_ref, up_pre_ref, *outs
+):
+    grad_gate_ref, grad_up_ref = outs
+    hidden_grad = keep_ref[...] + left_ref[...] + right_ref[...] + down_ref[...] + up_ref[...]
     gate_pre = gate_pre_ref[...].astype(F32)
     up_pre = up_pre_ref[...].astype(F32)
     sigmoid_gate = jax.nn.sigmoid(gate_pre)
@@ -129,15 +173,16 @@
 
 VMEM = pl.BlockSpec(memory_space=pltpu.VMEM)
 SMEM = pl.BlockSpec(memory_space=pltpu.SMEM)
-
-
-def call(kernel, specs, out_shape, *args):
+HBM = pl.BlockSpec(memory_space=pltpu.HBM)
+
+
+def call(kernel, specs, out_shape, *args, limit=24 << 20):
     return pl.pallas_call(
         kernel,
         in_specs=specs,
         out_specs=jax.tree.map(lambda _: VMEM, out_shape),
         out_shape=out_shape,
-        compiler_params=pltpu.CompilerParams(vmem_limit_bytes=24 << 20),
+        compiler_params=pltpu.CompilerParams(vmem_limit_bytes=limit),
     )(*args)
 
 
@@ -157,6 +202,7 @@
         routes.T,
         slots.T,
         gates.T,
+        limit=56 << 20,
     )
     send, gate_pre, up_pre = lax.optimization_barrier((send, saved_gate[0], saved_up[0]))
     expert_rows = lax.all_to_all(send, ("group", "xc"), 0, 0, tiled=True)
@@ -166,15 +212,31 @@
         hidden, "y", axis_index_groups=[list(range(p, shard_count, 2)) for p in (0, 1)]
     )
     other = lax.ppermute(same, "y", [(i, i ^ 1) for i in range(shard_count)])
-    give, k0, k1, k2, k3, terms, gate_rows = call(
+    send = shape((2 * capacity + capacity // 2, lane_count), F32)
+    held = (shard_count // 2, capacity, lane_count)
+    right, left, keep, gate_rows, terms = pl.pallas_call(
         matmul_kernel,
-        [SMEM] + [VMEM] * 4,
-        (
-            shape((shard_count // 2, capacity, lane_count), F32),
-            *[column] * 4,
+        in_specs=[SMEM] + [HBM] * 4,
+        out_specs=[HBM] * 4 + [VMEM],
+        out_shape=[
+            send,
+            send,
+            shape((3 * capacity, lane_count), F32),
+            column,
             shape((groups, 1, lane_count), F32),
-            column,
-        ),
+        ],
+        scratch_shapes=[
+            pltpu.VMEM((groups, parts, SLOTS, lane_count), BF16),
+            pltpu.VMEM(w_down.shape[1:], BF16),
+            pltpu.VMEM(held, F32),
+            pltpu.VMEM(held, F32),
+            pltpu.VMEM((shard_count, capacity, lane_count), F32),
+            pltpu.VMEM(column.shape, F32),
+            pltpu.SemaphoreType.DMA((shard_count + 3,)),
+            pltpu.SemaphoreType.DMA((shard_count + 2,)),
+        ],
+        compiler_params=pltpu.CompilerParams(vmem_limit_bytes=56 << 20),
+    )(
         jnp.stack([group, shard]),
         expert_rows.reshape(groups, parts, SLOTS, lane_count),
         w_down[0],
@@ -182,21 +244,30 @@
         other,
     )
 
-    got = lax.ppermute(give, "y", [(i, i ^ 1) for i in range(shard_count)])
+    def moved(array, by):
+        return lax.ppermute(
+            array, "y", [(i, (i + by) % shard_count) for i in range(shard_count)]
+        )
+
     home = lax.all_to_all(terms, "group", 0, 0, tiled=True)
-    sums = [k + got[d] for d, k in enumerate((k0, k1, k2, k3))]
-    for d in (2, 1, 3):
-        sums[d] = lax.ppermute(
-            sums[d], "y", [(i, (i + 2 * d) % shard_count) for i in range(shard_count)]
-        )
+    from_left, from_right = moved(right, 1), moved(left, -1)
+    down, up = call(
+        middle_kernel, [VMEM] * 3, (column, column), from_left, from_right, keep
+    )
+    from_above, from_below = moved(down, -3), moved(up, 3)
     spread = call(
         spread_kernel, [VMEM], shape((shard_count * parts, 2, lane_count), F32), home
     )
     every_term = lax.all_to_all(spread, ("y", "xc"), 0, 0, tiled=True)
     out = shape((capacity, lane_count), BF16)
-    grad_gate, grad_up = call(
-        output_kernel, [VMEM] * 7, (out, out), *sums, gate_rows, saved_gate[0], saved_up[0]
-    )
+    block = pl.BlockSpec((capacity, lane_count), lambda i: (0, 0))
+    grad_gate, grad_up = pl.pallas_call(
+        output_kernel,
+        grid=(1,),
+        in_specs=[block] * 8,
+        out_specs=[block] * 2,
+        out_shape=[out, out],
+    )(from_left, from_right, keep, from_above, from_below, gate_rows, saved_gate[0], saved_up[0])
     grad_gates = call(
         collect_kernel,
         [VMEM] * 3,

time: 120 us -> 123 us (1.025)
  Pallas kernels: 6.87 us -> 12.8 us
  local copies, waits for them, and re-layouts: 7.87 us -> 4.37 us
  starting transfers between devices: 54.4 us -> 51.8 us
  blocking collectives: 37.2 us -> 39.5 us
  waiting for transfers between devices: 10.8 us -> 12.4 us
    pallas_call x0 -> x2, Pallas kernels: none -> 8.32 us  [the longest x1 6.39 us: shards(): pl.pallas_call(matmul_kernel, in_specs=[SMEM] + [HBM] * 4, out_specs=[HBM...]
    unnamed x34 -> x24, local copies, waits for them, and re-layouts: 7.87 us -> 4.37 us
    pallas_call x6 -> x5, Pallas kernels: 6.87 us -> 4.43 us  [call(): pl.pallas_call(kernel, in_specs=specs, out_specs=jax.tree.map(lambda _: V...]
    all_to_all x1, blocking collectives: 21.2 us -> 23.5 us  [shards(): every_term = lax.all_to_all(spread, ('y', 'xc'), 0, 0, tiled=True)]
    ppermute x4, starting transfers between devices: 17 us -> 14.8 us  [moved(): lax.ppermute(array, 'y', [(i, (i + by) % shard_count) for i in range(shar...]
    all_to_all x1, waiting for transfers between devices: 0.01 us -> 2.15 us  [shards(): home = lax.all_to_all(terms, 'group', 0, 0, tiled=True)]
  transfers between devices with their start and end apart: 7 -> 7, of which waited for: 2 -> 3; matrix products, arithmetic and copies ran while one was open for 1% -> 0% of each run, Pallas kernels for 1% -> 1%
where the time goes in v4:
time: 123 us; the launch traced here: 122 us
  starting transfers between devices  51.8 us (42%)
  blocking collectives  39.5 us (32%)
  Pallas kernels  12.8 us (10%)
  waiting for transfers between devices  12.4 us (10%)
  local copies, waits for them, and re-layouts  4.37 us (4%)
    all_to_all x1, starting transfers between devices, shards(): expert_rows = lax.all_to_all(send, ('group', 'xc'), 0, 0, tiled=True)  24.1 us
    all_to_all x1, blocking collectives, shards(): every_term = lax.all_to_all(spread, ('y', 'xc'), 0, 0, tiled=True)  23.5 us
    all_gather x1, blocking collectives, shards(): lax.all_gather(hidden, 'y', axis_index_groups=[list(range(p, shard_count,...  16 us
    ppermute x4, starting transfers between devices, moved(): lax.ppermute(array, 'y', [(i, (i + by) % shard_count) for i in range(shar...  14.8 us
    all_to_all x1, starting transfers between devices, shards(): home = lax.all_to_all(terms, 'group', 0, 0, tiled=True)  10.7 us
    ppermute x1, waiting for transfers between devices, shards(): other = lax.ppermute(same, 'y', [(i, i ^ 1) for i in range(shard_count)])  7.88 us
    pallas_call x1, Pallas kernels, shards(): pl.pallas_call(matmul_kernel, in_specs=[SMEM] + [HBM] * 4, out_specs=[HBM...  6.39 us
    pallas_call x5, Pallas kernels, call(): pl.pallas_call(kernel, in_specs=specs, out_specs=jax.tree.map(lambda _: V...  4.43 us
  transfers between devices with their start and end apart: 7, of which 3 were waited for; matrix products, arithmetic and copies ran while one was open for 0% of the time, Pallas kernels for 1%

profile of v4, /device:TPU:1, one launch (start us, length us, event | category | flops | bytes accessed | tf_op | source)
XLA Modules:
  0.0 122.2 jit_solution(17341659713799603969)
XLA Ops:
  0.6 2.8 %shard_map.94 = bf16[128,16,128]{2,1,0:T(8,128)(2,1)} custom-call(bf16[112,128]{1,0:T(8,128)(2,1)} %bitcast.28, s32[8,128]{1,0:T(8,128)} %bitcast.20, s32[8,128]{1,0:T(8,128)} %bitcast.22, bf16[8,128]{1,0:T(8,128)(2,1)} %bitcast.30), custom_call_target="tpu_custom_call" | custom-call | tf_op jit(solution)/shard_map/pallas_call | solution.py:180
  3.4 24.1 %all-to-all-start = ((bf16[128,16,128]{2,1,0:T(8,128)(2,1)}), bf16[128,16,128]{2,1,0:T(8,128)(2,1)S(1)}, u32[]{:S(2)}, u32[]{:S(2)}) async-start(bf16[128,16,128]{2,1,0:T(8,128)(2,1)} %shard_map.94), calls=%async_computation | async-start | bytes 1048576 | tf_op jit(solution)/shard_map/all_to_all | solution.py:208
  27.5 0.0 copy-start.3
  27.5 0.8 copy-done.3
  28.3 0.8 copy-done.4
  29.2 16.0 %all-gather = f32[1024,128]{1,0:T(8,128)S(1)} all-gather(f32[256,128]{1,0:T(8,128)S(1)} %shard_map.95), channel_id=2, replica_groups={{0,16,32,48},{8,24,40,56},{1,17,33,49},{9,25,41,57},{2,18,34,50},{10,26..., dimensions={0}, use_global_device_ids=true | all-gather | bytes 655360 | tf_op jit(solution)/shard_map/all_gather | solution.py:211
  45.2 2.3 %collective-permute-start = (f32[4,256,128]{2,1,0:T(8,128)S(1)}, f32[4,256,128]{2,1,0:T(8,128)S(1)}, u32[]{:S(2)}, u32[]{:S(2)}) collective-permute-start(f32[4,256,128]{2,1,0:T(8,128)S(1)} %bitcast.24), channel_id=1, source_target_pairs={{0,8},{8,0},{16,24},{24,16},{32,40},{40,32},{48,56},{56,48},{1,9},... | collective-permute-start | bytes 1572872 | tf_op jit(solution)/shard_map/ppermute | solution.py:214
  47.4 0.6 pad_add_fusion.where_ref
  48.0 7.9 %collective-permute-done.other_in = f32[4,256,128]{2,1,0:T(8,128)S(1)} collective-permute-done((f32[4,256,128]{2,1,0:T(8,128)S(1)}, f32[4,256,128]{2,1,0:T(8,128)S(1)}, u32[]{:S(2)}, u32[]{:S(2)}) %collective-permute-start) | collective-permute-done | bytes 524320 | tf_op jit(solution)/shard_map/ppermute | solution.py:214
  55.9 2.4 %all-to-all-done = bf16[128,16,128]{2,1,0:T(8,128)(2,1)S(1)} async-done(((bf16[128,16,128]{2,1,0:T(8,128)(2,1)}), bf16[128,16,128]{2,1,0:T(8,128)(2,1)S(1)}, u32[]{:S(2)}, u32[]{:S(2)}) %all-to-all-start) | async-done | bytes 524320 | tf_op jit(solution)/shard_map/all_to_all | solution.py:208
  58.3 0.0 copy-done.7
  58.3 0.0 copy-done.9
  58.3 0.8 copy-done.8
  59.1 6.4 %shard_map.96 = (f32[640,128]{1,0:T(8,128)}, f32[640,128]{1,0:T(8,128)}, f32[768,128]{1,0:T(8,128)}, f32[256,128]{1,0:T(8,128)}, f32[16,1,128]{2,1,0:T(1,128)}) custom-call(s32[2]{0:T(128)} %pad_add_fusion.where_ref, bf16[16,8,16,128]{3,2,1,0:T(8,128)(2,1)} %bitcast.26, bf16[1024,896]{1,0:T(8,128)(2,1)} %bitcast.27, f32[4,256,128]{2,1,0:T(8,128)} %bitcast.25, ...), custom_call_target="tpu_custom_call" | custom-call | tf_op jit(solution)/shard_map/pallas_call | solution.py:217
  65.5 3.2 %collective-permute-start.1 = (f32[640,128]{1,0:T(8,128)}, f32[640,128]{1,0:T(8,128)S(1)}, u32[]{:S(2)}, u32[]{:S(2)}) collective-permute-start(f32[640,128]{1,0:T(8,128)} %get-tuple-element.18), channel_id=1, source_target_pairs={{0,8},{8,16},{16,24},{24,32},{32,40},{40,48},{48,56},{56,0},{1,9},... | collective-permute-start | bytes 983048 | tf_op jit(solution)/shard_map/ppermute | solution.py:248
  68.7 3.8 %collective-permute-start.2 = (f32[640,128]{1,0:T(8,128)}, f32[640,128]{1,0:T(8,128)S(1)}, u32[]{:S(2)}, u32[]{:S(2)}) collective-permute-start(f32[640,128]{1,0:T(8,128)} %get-tuple-element.19), channel_id=1, source_target_pairs={{0,56},{8,0},{16,8},{24,16},{32,24},{40,32},{48,40},{56,48},{1,57}... | collective-permute-start | bytes 983048 | tf_op jit(solution)/shard_map/ppermute | solution.py:248
  72.5 10.7 %all-to-all-start.1 = ((f32[16,1,128]{2,1,0:T(1,128)}), f32[16,1,128]{2,1,0:T(1,128)S(1)}, u32[]{:S(2)}, u32[]{:S(2)}) async-start(f32[16,1,128]{2,1,0:T(1,128)} %get-tuple-element.26), calls=%async_computation.1 | async-start | bytes 16384 | tf_op jit(solution)/shard_map/all_to_all | solution.py:252
  83.2 0.0 collective-permute-done.1.left_ref
  83.2 0.0 copy-start.1
  83.2 0.0 collective-permute-done.2.right_ref
  83.3 1.2 copy-done
  84.5 4.0 %collective-permute-start.3 = (f32[256,128]{1,0:T(8,128)S(1)}, f32[256,128]{1,0:T(8,128)S(1)}, u32[]{:S(2)}, u32[]{:S(2)}) collective-permute-start(f32[256,128]{1,0:T(8,128)S(1)} %get-tuple-element.21), channel_id=1, source_target_pairs={{0,40},{8,48},{16,56},{24,0},{32,8},{40,16},{48,24},{56,32},{1,41}... | collective-permute-start | bytes 393224 | tf_op jit(solution)/shard_map/ppermute | solution.py:248
  88.5 3.8 %collective-permute-start.4 = (f32[256,128]{1,0:T(8,128)S(1)}, f32[256,128]{1,0:T(8,128)S(1)}, u32[]{:S(2)}, u32[]{:S(2)}) collective-permute-start(f32[256,128]{1,0:T(8,128)S(1)} %get-tuple-element.22), channel_id=1, source_target_pairs={{0,24},{8,32},{16,40},{24,48},{32,56},{40,0},{48,8},{56,16},{1,25}... | collective-permute-start | bytes 393224 | tf_op jit(solution)/shard_map/ppermute | solution.py:248
  92.3 2.2 %all-to-all-done.1.home_ref = f32[16,1,128]{2,1,0:T(1,128)S(1)} async-done(((f32[16,1,128]{2,1,0:T(1,128)}), f32[16,1,128]{2,1,0:T(1,128)S(1)}, u32[]{:S(2)}, u32[]{:S(2)}) %all-to-all-start.1) | async-done | bytes 8224 | tf_op jit(solution)/shard_map/all_to_all | solution.py:252
  94.5 23.5 %all_to_all.15 = f32[64,2,128]{2,1,0:T(2,128)S(1)} all-to-all(f32[64,2,128]{2,1,0:T(2,128)S(1)} %shard_map.99), channel_id=1, replica_groups=mesh['group'=16,'y'=8,'xc'=8] {'y','xc'}, dimensions={0} | all-to-all | bytes 131072 | tf_op jit(solution)/shard_map/all_to_all | solution.py:261
  118.0 0.0 copy-done.5
  118.0 1.6 %shard_map.100 = f32[8,128]{1,0:T(8,128)} custom-call(f32[8,8,2,128]{3,2,1,0:T(2,128)S(1)} %bitcast.19, s32[8,128]{1,0:T(8,128)S(1)} %bitcast.21, s32[8,128]{1,0:T(8,128)S(1)} %bitcast.23), custom_call_target="tpu_custom_call" | custom-call | tf_op jit(solution)/shard_map/pallas_call | solution.py:180
  119.6 0.0 collective-permute-done.3.down_ref
  119.6 0.0 collective-permute-done.4.up_ref
  119.6 0.6 copy-done.10
  120.2 0.1 copy-done.11
  120.3 1.9 %shard_map.98 = (bf16[256,128]{1,0:T(8,128)(2,1)}, bf16[256,128]{1,0:T(8,128)(2,1)}) custom-call(f32[640,128]{1,0:T(8,128)} %copy-done.1, f32[640,128]{1,0:T(8,128)} %copy-done.2, f32[768,128]{1,0:T(8,128)} %get-tuple-element.20.keep_ref, f32[256,128]{1,0:T(8,128)} %copy-done.10, f32[256,128]{1,0:T(8,128)} %copy-done.11, ...), custom_call_target="tpu_custom_call" | custom-call | tf_op jit(solution)/shard_map/pallas_call | solution.py:264
  (16 shorter events, 0.1 us)
Async XLA Ops:
  3.4 54.9 %all-to-all-start = ((bf16[128,16,128]{2,1,0:T(8,128)(2,1)}), bf16[128,16,128]{2,1,0:T(8,128)(2,1)S(1)}, u32[]{:S(2)}, u32[]{:S(2)}) async-start(bf16[128,16,128]{2,1,0:T(8,128)(2,1)} %shard_map.94), calls=%async_computation | async-start | bytes 1048576 | tf_op jit(solution)/shard_map/all_to_all | solution.py:208
  27.5 0.8 copy-start.3
  28.3 0.8 copy-start.4
  45.2 13.1 %copy-start.7 = (f32[1024,128]{1,0:T(8,128)}, f32[1024,128]{1,0:T(8,128)S(1)}, u32[]{:S(2)}) copy-start(f32[1024,128]{1,0:T(8,128)S(1)} %all-gather) | copy-start | bytes 1572868
  45.2 10.8 %collective-permute-start = (f32[4,256,128]{2,1,0:T(8,128)S(1)}, f32[4,256,128]{2,1,0:T(8,128)S(1)}, u32[]{:S(2)}, u32[]{:S(2)}) collective-permute-start(f32[4,256,128]{2,1,0:T(8,128)S(1)} %bitcast.24), channel_id=1, source_target_pairs={{0,8},{8,0},{16,24},{24,16},{32,40},{40,32},{48,56},{56,48},{1,9},... | collective-permute-start | bytes 1572872 | tf_op jit(solution)/shard_map/ppermute | solution.py:214
  55.9 2.4 %copy-start.9 = (f32[4,256,128]{2,1,0:T(8,128)}, f32[4,256,128]{2,1,0:T(8,128)S(1)}, u32[]{:S(2)}) copy-start(f32[4,256,128]{2,1,0:T(8,128)S(1)} %collective-permute-done.other_in) | copy-start | bytes 1572868
  58.3 0.8 copy-start.8
  59.1 58.9 %copy-start.5 = (s32[128,8]{0,1:T(8,128)S(1)}, s32[128,8]{0,1:T(8,128)}, u32[]{:S(2)}) copy-start(s32[128,8]{0,1:T(8,128)} %param.8) | copy-start | bytes 12292
  59.1 58.9 %copy-start.6 = (s32[128,8]{0,1:T(8,128)S(1)}, s32[128,8]{0,1:T(8,128)}, u32[]{:S(2)}) copy-start(s32[128,8]{0,1:T(8,128)} %param.9) | copy-start | bytes 12292
  65.5 17.7 %collective-permute-start.1 = (f32[640,128]{1,0:T(8,128)}, f32[640,128]{1,0:T(8,128)S(1)}, u32[]{:S(2)}, u32[]{:S(2)}) collective-permute-start(f32[640,128]{1,0:T(8,128)} %get-tuple-element.18), channel_id=1, source_target_pairs={{0,8},{8,16},{16,24},{24,32},{32,40},{40,48},{48,56},{56,0},{1,9},... | collective-permute-start | bytes 983048 | tf_op jit(solution)/shard_map/ppermute | solution.py:248
  68.7 14.5 %collective-permute-start.2 = (f32[640,128]{1,0:T(8,128)}, f32[640,128]{1,0:T(8,128)S(1)}, u32[]{:S(2)}, u32[]{:S(2)}) collective-permute-start(f32[640,128]{1,0:T(8,128)} %get-tuple-element.19), channel_id=1, source_target_pairs={{0,56},{8,0},{16,8},{24,16},{32,24},{40,32},{48,40},{56,48},{1,57}... | collective-permute-start | bytes 983048 | tf_op jit(solution)/shard_map/ppermute | solution.py:248
  72.5 21.9 %all-to-all-start.1 = ((f32[16,1,128]{2,1,0:T(1,128)}), f32[16,1,128]{2,1,0:T(1,128)S(1)}, u32[]{:S(2)}, u32[]{:S(2)}) async-start(f32[16,1,128]{2,1,0:T(1,128)} %get-tuple-element.26), calls=%async_computation.1 | async-start | bytes 16384 | tf_op jit(solution)/shard_map/all_to_all | solution.py:252
  83.2 36.4 %copy-start.1 = (f32[640,128]{1,0:T(8,128)}, f32[640,128]{1,0:T(8,128)S(1)}, u32[]{:S(2)}) copy-start(f32[640,128]{1,0:T(8,128)S(1)} %collective-permute-done.1.left_ref) | copy-start | bytes 983044
  83.3 36.4 %copy-start.2 = (f32[640,128]{1,0:T(8,128)}, f32[640,128]{1,0:T(8,128)S(1)}, u32[]{:S(2)}) copy-start(f32[640,128]{1,0:T(8,128)S(1)} %collective-permute-done.2.right_ref) | copy-start | bytes 983044
  83.3 1.2 %copy-start = (f32[768,128]{1,0:T(8,128)S(1)}, f32[768,128]{1,0:T(8,128)}, u32[]{:S(2)}) copy-start(f32[768,128]{1,0:T(8,128)} %get-tuple-element.20.keep_ref) | copy-start | bytes 1179652
  84.5 35.1 %collective-permute-start.3 = (f32[256,128]{1,0:T(8,128)S(1)}, f32[256,128]{1,0:T(8,128)S(1)}, u32[]{:S(2)}, u32[]{:S(2)}) collective-permute-start(f32[256,128]{1,0:T(8,128)S(1)} %get-tuple-element.21), channel_id=1, source_target_pairs={{0,40},{8,48},{16,56},{24,0},{32,8},{40,16},{48,24},{56,32},{1,41}... | collective-permute-start | bytes 393224 | tf_op jit(solution)/shard_map/ppermute | solution.py:248
  88.5 31.1 %collective-permute-start.4 = (f32[256,128]{1,0:T(8,128)S(1)}, f32[256,128]{1,0:T(8,128)S(1)}, u32[]{:S(2)}, u32[]{:S(2)}) collective-permute-start(f32[256,128]{1,0:T(8,128)S(1)} %get-tuple-element.22), channel_id=1, source_target_pairs={{0,24},{8,32},{16,40},{24,48},{32,56},{40,0},{48,8},{56,16},{1,25}... | collective-permute-start | bytes 393224 | tf_op jit(solution)/shard_map/ppermute | solution.py:248
  119.6 0.6 copy-start.10
  119.6 0.7 copy-start.11

commit v5 on v3

v5 whole, which is shorter than its diff:
```python
import jax
import jax.numpy as jnp
from jax import lax
from jax.experimental import pallas as pl
from jax.experimental.pallas import tpu as pltpu
from jax.sharding import Mesh, PartitionSpec as P

EXP_GRP = 8
SLOTS = 16
NT = (((1,), (1,)), ((), ()))
TN = (((0,), (0,)), ((), ()))
F32 = jnp.float32
BF16 = jnp.bfloat16


def lanes(shape):
    return lax.broadcasted_iota(jnp.int32, shape, len(shape) - 1)


def rows(shape):
    return lax.broadcasted_iota(jnp.int32, shape, 0)


def dispatch_kernel(tokens_ref, routes_ref, slots_ref, gates_ref, out_ref):
    col_width, tok_count = tokens_ref.shape
    lane_count = out_ref.shape[2]
    place = routes_ref[...] * SLOTS + slots_ref[...]
    gates = gates_ref[...].astype(F32)
    spare = (lane_count - col_width, tok_count)
    features = jnp.concatenate([tokens_ref[...], jnp.zeros(spare, BF16)], axis=0)
    marks = jnp.where(rows((lane_count, tok_count)) == col_width, 1.0, 0.0).astype(BF16)
    source = jnp.concatenate([features, marks], axis=1)
    chunk = 256
    for start in range(0, out_ref.shape[0] * SLOTS, chunk):
        row_ids = rows((chunk, tok_count)) + start
        pick = jnp.zeros((chunk, tok_count), F32)
        gate = jnp.zeros((chunk, tok_count), F32)
        for k in range(place.shape[0]):
            hit = row_ids == place[k : k + 1, :]
            pick = jnp.where(hit, 1.0, pick)
            gate = jnp.where(hit, gates[k : k + 1, :], gate)
        both = jnp.concatenate([pick.astype(BF16), gate.astype(BF16)], axis=1)
        block = lax.dot_general(both, source, NT, preferred_element_type=F32)
        out_ref[start // SLOTS : (start + chunk) // SLOTS] = block.astype(BF16).reshape(
            chunk // SLOTS, SLOTS, lane_count
        )


def hidden_kernel(gate_ref, up_ref, out_ref):
    gate_pre = gate_ref[...].astype(F32)
    out_ref[...] = gate_pre * jax.nn.sigmoid(gate_pre) * up_ref[...].astype(F32)


def matmul_kernel(shard_ref, rows_ref, w_ref, same_ref, other_ref, *outs):
    right_ref, left_ref, keep_ref, gate_ref, term_ref = outs
    groups, parts, _, lane_count = rows_ref.shape
    capacity = groups * SLOTS
    col_width = w_ref.shape[1] // parts
    count = w_ref.shape[0] // lane_count
    shard = shard_ref[0]
    half = capacity // 2
    low, high = slice(0, half), slice(half, capacity)
    every, near = slice(0, capacity), slice(capacity, 2 * capacity)
    last, spare = slice(2 * capacity, 3 * capacity), slice(2 * capacity, 2 * capacity + half)
    pairs = (
        ((1, ((every, right_ref, every),)), (count - 1, ((every, left_ref, every),))),
        ((count - 2, ((every, right_ref, near),)), (2, ((every, left_ref, near),))),
        (
            (4, ((high, right_ref, spare), (low, left_ref, spare))),
            (0, ((every, keep_ref, every),)),
        ),
        ((count - 3, ((every, keep_ref, near),)), (3, ((every, keep_ref, last),))),
    )
    blocks = [rows_ref[:, e].reshape(capacity, lane_count) for e in range(parts)]
    x = jnp.concatenate([b[:, :col_width] for b in blocks], axis=1)
    terms = jnp.zeros((capacity, lane_count), F32)
    for pair in pairs:
        units = [(shard + offset) % count for offset, _ in pair]
        firsts = [pl.multiple_of(unit * lane_count, lane_count) for unit in units]
        w = jnp.concatenate([w_ref[pl.ds(first, lane_count), :] for first in firsts], axis=0)
        both = lax.dot_general(x, w, NT, preferred_element_type=F32)
        for i, (offset, targets) in enumerate(pair):
            part = both[:, i * lane_count : (i + 1) * lane_count]
            for span, target_ref, to in targets:
                target_ref[to] = part[span]
            terms += part * (other_ref if offset % 2 else same_ref)[units[i] // 2]
    total = jnp.sum(terms, axis=1, keepdims=True)
    row_ids, lane_ids = rows((capacity, lane_count)), lanes((capacity, lane_count))
    hit = lane_ids == row_ids % lane_count
    line = jnp.sum(
        jnp.where(hit, total, 0.0).reshape(capacity // lane_count, lane_count, lane_count), axis=1
    )
    term_ref[...] = jnp.broadcast_to(line[None], term_ref.shape)
    gate = jnp.where(lane_ids == col_width, blocks[0].astype(F32), 0.0)
    gate_ref[...] = jnp.broadcast_to(
        jnp.sum(gate, axis=1, keepdims=True), (capacity, lane_count)
    )


def middle_kernel(left_ref, right_ref, keep_ref, own_ref, down_ref, up_ref):
    capacity = down_ref.shape[0]
    half = capacity // 2
    near = slice(capacity, 2 * capacity)
    own_ref[...] = keep_ref[:capacity] + left_ref[:capacity] + right_ref[:capacity]
    down_ref[...] = keep_ref[near] + left_ref[near]
    down_ref[:half] += right_ref[2 * capacity :]
    up_ref[...] = keep_ref[2 * capacity :] + right_ref[near]
    up_ref[half:] += left_ref[2 * capacity :]


def spread_kernel(terms_ref, out_ref):
    total = terms_ref[0]
    for s in range(1, terms_ref.shape[0]):
        total += terms_ref[s]
    half = out_ref.shape[0] // 2
    for h in range(2):
        out_ref[h * half : (h + 1) * half] = jnp.broadcast_to(
            total[:, h, :][None], (half, *out_ref.shape[1:])
        )


def output_kernel(own_ref, down_ref, up_ref, gate_ref, gate_pre_ref, up_pre_ref, *outs):
    grad_gate_ref, grad_up_ref = outs
    hidden_grad = own_ref[...] + down_ref[...] + up_ref[...]
    gate_pre = gate_pre_ref[...].astype(F32)
    up_pre = up_pre_ref[...].astype(F32)
    sigmoid_gate = jax.nn.sigmoid(gate_pre)
    scaled = gate_ref[...] * hidden_grad
    grad_up_ref[...] = (scaled * gate_pre * sigmoid_gate).astype(BF16)
    grad_gate_ref[...] = (
        scaled * up_pre * sigmoid_gate * (1.0 + gate_pre * (1.0 - sigmoid_gate))
    ).astype(BF16)


def collect_kernel(group_ref, terms_ref, routes_ref, slots_ref, out_ref):
    groups, parts, lane_count = terms_ref.shape
    route_count, tok_count = routes_ref.shape
    table = terms_ref[...].reshape(groups * parts, lane_count)
    offset = group_ref[0] % (lane_count // SLOTS) * SLOTS
    for k in range(route_count):
        hit = rows((groups * parts, tok_count)) == routes_ref[k : k + 1, :]
        picked = lax.dot_general(
            table,
            jnp.where(hit, 1.0, 0.0),
            TN,
            preferred_element_type=F32,
            precision=lax.Precision.HIGHEST,
        )
        own = rows((lane_count, tok_count)) == slots_ref[k : k + 1, :] + offset
        out_ref[k : k + 1, :] = jnp.sum(jnp.where(own, picked, 0.0), axis=0, keepdims=True)


VMEM = pl.BlockSpec(memory_space=pltpu.VMEM)
SMEM = pl.BlockSpec(memory_space=pltpu.SMEM)


def call(kernel, specs, out_shape, *args, limit=24 << 20):
    return pl.pallas_call(
        kernel,
        in_specs=specs,
        out_specs=jax.tree.map(lambda _: VMEM, out_shape),
        out_shape=out_shape,
        compiler_params=pltpu.CompilerParams(vmem_limit_bytes=limit),
    )(*args)


def shards(grad_out, routes, slots, gates, w_down, saved_gate, saved_up):
    shape = jax.ShapeDtypeStruct
    groups, shard_count, parts = (lax.axis_size(a) for a in ("group", "y", "xc"))
    capacity, lane_count = saved_gate.shape[1:]
    group = lax.axis_index("group").astype(jnp.int32)
    shard = lax.axis_index("y").astype(jnp.int32)
    column = shape((capacity, lane_count), F32)

    send = call(
        dispatch_kernel,
        [VMEM] * 4,
        shape((groups * parts, SLOTS, lane_count), BF16),
        grad_out.T,
        routes.T,
        slots.T,
        gates.T,
        limit=56 << 20,
    )
    send, gate_pre, up_pre = lax.optimization_barrier((send, saved_gate[0], saved_up[0]))
    expert_rows = lax.all_to_all(send, ("group", "xc"), 0, 0, tiled=True)

    hidden = call(hidden_kernel, [VMEM] * 2, column, gate_pre, up_pre)
    same = lax.all_gather(
        hidden, "y", axis_index_groups=[list(range(p, shard_count, 2)) for p in (0, 1)]
    )
    other = lax.ppermute(same, "y", [(i, i ^ 1) for i in range(shard_count)])
    send = shape((2 * capacity + capacity // 2, lane_count), F32)
    right, left, keep, gate_rows, terms = call(
        matmul_kernel,
        [SMEM] + [VMEM] * 4,
        (
            send,
            send,
            shape((3 * capacity, lane_count), F32),
            column,
            shape((shard_count * parts, 2, lane_count), F32),
        ),
        shard[None],
        expert_rows.reshape(groups, parts, SLOTS, lane_count),
        w_down[0],
        same,
        other,
        limit=56 << 20,
    )

    def moved(array, by):
        return lax.ppermute(
            array, "y", [(i, (i + by) % shard_count) for i in range(shard_count)]
        )

    every_term = lax.all_to_all(terms, ("y", "xc"), 0, 0, tiled=True)
    from_left, from_right = moved(right, 1), moved(left, -1)
    own, down, up = call(
        middle_kernel, [VMEM] * 3, (column,) * 3, from_left, from_right, keep
    )
    from_above, from_below = moved(down, -3), moved(up, 3)
    spread = call(
        spread_kernel,
        [VMEM],
        shape((groups, parts, lane_count), F32),
        every_term.reshape(shard_count, parts, 2, lane_count),
    )
    home_terms = lax.all_to_all(spread, "group", 0, 0, tiled=True)
    column_out = shape((capacity, lane_count), BF16)
    grad_gate, grad_up = call(
        output_kernel,
        [VMEM] * 6,
        (column_out, column_out),
        own,
        from_above,
        from_below,
        gate_rows,
        saved_gate[0],
        saved_up[0],
    )
    grad_gates = call(
        collect_kernel,
        [SMEM] + [VMEM] * 3,
        shape(routes.shape[::-1], F32),
        group[None],
        home_terms,
        routes.T,
        slots.T,
    )
    return (grad_gate[None], grad_up[None], grad_gates.T)


def solution(mesh):
    fine = Mesh(mesh.devices.reshape(mesh.shape["group"], -1, EXP_GRP), ("group", "y", "xc"))
    local, device = ("y", "xc"), ("group", "y", "xc")
    return jax.shard_map(
        shards,
        mesh=fine,
        in_specs=(
            P("group", local),
            P("group", None),
            P("group", None),
            P("group", None),
            P(device, None, None),
            P(device, None, None),
            P(device, None, None),
        ),
        out_specs=(P(device, None, None), P(device, None, None), P("group", None)),
        check_vma=False,
    )
```

time: 120 us -> 124 us (1.033)
  waiting for transfers between devices: 10.8 us -> 19.1 us
  starting transfers between devices: 54.4 us -> 50.8 us
  local copies, waits for them, and re-layouts: 7.87 us -> 4.38 us
  Pallas kernels: 6.87 us -> 9.2 us
  blocking collectives: 37.2 us -> 38.6 us
    ppermute x4, waiting for transfers between devices: 0.01 us -> 4.83 us  [moved(): lax.ppermute(array, 'y', [(i, (i + by) % shard_count) for i in range(shar...]
    unnamed x34 -> x22, local copies, waits for them, and re-layouts: 7.87 us -> 4.38 us
    all_to_all x1, waiting for transfers between devices: 0.01 us -> 3.42 us  [shards(): home_terms = lax.all_to_all(spread, 'group', 0, 0, tiled=True)]
    ppermute x4, starting transfers between devices: 17 us -> 14.1 us  [moved(): lax.ppermute(array, 'y', [(i, (i + by) % shard_count) for i in range(shar...]
    pallas_call x6 -> x7, Pallas kernels: 6.87 us -> 9.2 us  [call(): pl.pallas_call(kernel, in_specs=specs, out_specs=jax.tree.map(lambda _: V...]
    all_to_all x1, blocking collectives: 21.2 us -> 22.6 us  [shards(): every_term = lax.all_to_all(terms, ('y', 'xc'), 0, 0, tiled=True)]
  transfers between devices with their start and end apart: 7 -> 7, of which waited for: 2 -> 4; matrix products, arithmetic and copies ran while one was open for 1% -> 0% of each run, Pallas kernels for 1% -> 2%
where the time goes in v5:
time: 124 us; the launch traced here: 123 us
  starting transfers between devices  50.8 us (41%)
  blocking collectives  38.6 us (31%)
  waiting for transfers between devices  19.1 us (15%)
  Pallas kernels  9.2 us (7%)
  local copies, waits for them, and re-layouts  4.38 us (4%)
    all_to_all x1, starting transfers between devices, shards(): expert_rows = lax.all_to_all(send, ('group', 'xc'), 0, 0, tiled=True)  24.1 us
    all_to_all x1, blocking collectives, shards(): every_term = lax.all_to_all(terms, ('y', 'xc'), 0, 0, tiled=True)  22.6 us
    all_gather x1, blocking collectives, shards(): lax.all_gather(hidden, 'y', axis_index_groups=[list(range(p, shard_count,...  16 us
    ppermute x4, starting transfers between devices, moved(): lax.ppermute(array, 'y', [(i, (i + by) % shard_count) for i in range(shar...  14.1 us
    all_to_all x1, starting transfers between devices, shards(): home_terms = lax.all_to_all(spread, 'group', 0, 0, tiled=True)  10.4 us
    pallas_call x7, Pallas kernels, call(): pl.pallas_call(kernel, in_specs=specs, out_specs=jax.tree.map(lambda _: V...  9.2 us
    ppermute x1, waiting for transfers between devices, shards(): other = lax.ppermute(same, 'y', [(i, i ^ 1) for i in range(shard_count)])  8.47 us
    ppermute x4, waiting for transfers between devices, moved(): lax.ppermute(array, 'y', [(i, (i + by) % shard_count) for i in range(shar...  4.83 us
  transfers between devices with their start and end apart: 7, of which 4 were waited for; matrix products, arithmetic and copies ran while one was open for 0% of the time, Pallas kernels for 2%

profile of v5, /device:TPU:1, one launch (start us, length us, event | category | flops | bytes accessed | tf_op | source)
XLA Modules:
  0.0 122.8 jit_solution(4672006327409326416)
XLA Ops:
  0.6 2.8 %shard_map.94 = bf16[128,16,128]{2,1,0:T(8,128)(2,1)} custom-call(bf16[112,128]{1,0:T(8,128)(2,1)} %bitcast.28, s32[8,128]{1,0:T(8,128)} %bitcast.20, s32[8,128]{1,0:T(8,128)} %bitcast.22, bf16[8,128]{1,0:T(8,128)(2,1)} %bitcast.30), custom_call_target="tpu_custom_call" | custom-call | tf_op jit(solution)/shard_map/pallas_call | solution.py:158
  3.4 24.1 %all-to-all-start = ((bf16[128,16,128]{2,1,0:T(8,128)(2,1)}), bf16[128,16,128]{2,1,0:T(8,128)(2,1)S(1)}, u32[]{:S(2)}, u32[]{:S(2)}) async-start(bf16[128,16,128]{2,1,0:T(8,128)(2,1)} %shard_map.94), calls=%async_computation | async-start | bytes 1048576 | tf_op jit(solution)/shard_map/all_to_all | solution.py:186
  27.5 0.0 copy-start.1
  27.5 0.8 copy-done.1
  28.3 0.8 copy-done.3
  29.2 16.0 %all-gather = f32[1024,128]{1,0:T(8,128)S(1)} all-gather(f32[256,128]{1,0:T(8,128)S(1)} %shard_map.95), channel_id=2, replica_groups={{0,16,32,48},{8,24,40,56},{1,17,33,49},{9,25,41,57},{2,18,34,50},{10,26..., dimensions={0}, use_global_device_ids=true | all-gather | bytes 655360 | tf_op jit(solution)/shard_map/all_gather | solution.py:189
  45.2 2.3 %collective-permute-start = (f32[4,256,128]{2,1,0:T(8,128)S(1)}, f32[4,256,128]{2,1,0:T(8,128)S(1)}, u32[]{:S(2)}, u32[]{:S(2)}) collective-permute-start(f32[4,256,128]{2,1,0:T(8,128)S(1)} %bitcast.24), channel_id=1, source_target_pairs={{0,8},{8,0},{16,24},{24,16},{32,40},{40,32},{48,56},{56,48},{1,9},... | collective-permute-start | bytes 1572872 | tf_op jit(solution)/shard_map/ppermute | solution.py:192
  47.4 8.5 %collective-permute-done.other_ref = f32[4,256,128]{2,1,0:T(8,128)S(1)} collective-permute-done((f32[4,256,128]{2,1,0:T(8,128)S(1)}, f32[4,256,128]{2,1,0:T(8,128)S(1)}, u32[]{:S(2)}, u32[]{:S(2)}) %collective-permute-start) | collective-permute-done | bytes 524320 | tf_op jit(solution)/shard_map/ppermute | solution.py:192
  55.9 2.4 %all-to-all-done = bf16[128,16,128]{2,1,0:T(8,128)(2,1)S(1)} async-done(((bf16[128,16,128]{2,1,0:T(8,128)(2,1)}), bf16[128,16,128]{2,1,0:T(8,128)(2,1)S(1)}, u32[]{:S(2)}, u32[]{:S(2)}) %all-to-all-start) | async-done | bytes 524320 | tf_op jit(solution)/shard_map/all_to_all | solution.py:186
  58.3 0.0 copy-done.8
  58.3 0.0 copy-done.10
  58.3 0.8 copy-done.9
  59.1 3.7 %shard_map.96 = (f32[640,128]{1,0:T(8,128)}, f32[640,128]{1,0:T(8,128)}, f32[768,128]{1,0:T(8,128)}, f32[256,128]{1,0:T(8,128)}, f32[64,2,128]{2,1,0:T(2,128)}) custom-call(s32[1]{0:T(128)} %bitcast.shard_ref, bf16[16,8,16,128]{3,2,1,0:T(8,128)(2,1)} %bitcast.26, bf16[1024,896]{1,0:T(8,128)(2,1)} %bitcast.27, f32[4,256,128]{2,1,0:T(8,128)} %bitcast.25, ...), custom_call_target="tpu_custom_call" | custom-call | tf_op jit(solution)/shard_map/pallas_call | solution.py:158
  62.8 3.2 %collective-permute-start.1 = (f32[640,128]{1,0:T(8,128)}, f32[640,128]{1,0:T(8,128)S(1)}, u32[]{:S(2)}, u32[]{:S(2)}) collective-permute-start(f32[640,128]{1,0:T(8,128)} %get-tuple-element.19), channel_id=1, source_target_pairs={{0,8},{8,16},{16,24},{24,32},{32,40},{40,48},{48,56},{56,0},{1,9},... | collective-permute-start | bytes 983048 | tf_op jit(solution)/shard_map/ppermute | solution.py:213
  66.0 3.8 %collective-permute-start.2 = (f32[640,128]{1,0:T(8,128)}, f32[640,128]{1,0:T(8,128)S(1)}, u32[]{:S(2)}, u32[]{:S(2)}) collective-permute-start(f32[640,128]{1,0:T(8,128)} %get-tuple-element.20), channel_id=1, source_target_pairs={{0,56},{8,0},{16,8},{24,16},{32,24},{40,32},{48,40},{56,48},{1,57}... | collective-permute-start | bytes 983048 | tf_op jit(solution)/shard_map/ppermute | solution.py:213
  69.8 22.6 %all_to_all.15 = f32[64,2,128]{2,1,0:T(2,128)S(1)} all-to-all(f32[64,2,128]{2,1,0:T(2,128)} %get-tuple-element.28), channel_id=1, replica_groups=mesh['group'=16,'y'=8,'xc'=8] {'y','xc'}, dimensions={0} | all-to-all | bytes 131072 | tf_op jit(solution)/shard_map/all_to_all | solution.py:217
  92.4 0.7 shard_map.99
  93.1 10.4 %all-to-all-start.2 = ((f32[16,8,128]{2,1,0:T(8,128)}), f32[16,8,128]{2,1,0:T(8,128)S(1)}, u32[]{:S(2)}, u32[]{:S(2)}) async-start(f32[16,8,128]{2,1,0:T(8,128)} %shard_map.99), calls=%async_computation.2 | async-start | bytes 131072 | tf_op jit(solution)/shard_map/all_to_all | solution.py:229
  103.5 0.0 collective-permute-done.1.left_ref
  103.5 0.0 collective-permute-done.2.right_ref
  103.5 0.0 copy-start
  103.5 1.0 copy-done
  104.5 0.1 shard_map.97
  104.6 2.3 %collective-permute-start.3 = (f32[256,128]{1,0:T(8,128)S(1)}, f32[256,128]{1,0:T(8,128)S(1)}, u32[]{:S(2)}, u32[]{:S(2)}) collective-permute-start(f32[256,128]{1,0:T(8,128)S(1)} %get-tuple-element.23), channel_id=1, source_target_pairs={{0,40},{8,48},{16,56},{24,0},{32,8},{40,16},{48,24},{56,32},{1,41}... | collective-permute-start | bytes 393224 | tf_op jit(solution)/shard_map/ppermute | solution.py:213
  106.8 4.8 %collective-permute-start.4 = (f32[256,128]{1,0:T(8,128)S(1)}, f32[256,128]{1,0:T(8,128)S(1)}, u32[]{:S(2)}, u32[]{:S(2)}) collective-permute-start(f32[256,128]{1,0:T(8,128)S(1)} %get-tuple-element.24), channel_id=1, source_target_pairs={{0,24},{8,32},{16,40},{24,48},{32,56},{40,0},{48,8},{56,16},{1,25}... | collective-permute-start | bytes 393224 | tf_op jit(solution)/shard_map/ppermute | solution.py:213
  111.7 3.4 %all-to-all-done.2.terms_ref = f32[16,8,128]{2,1,0:T(8,128)S(1)} async-done(((f32[16,8,128]{2,1,0:T(8,128)}), f32[16,8,128]{2,1,0:T(8,128)S(1)}, u32[]{:S(2)}, u32[]{:S(2)}) %all-to-all-start.2) | async-done | bytes 65568 | tf_op jit(solution)/shard_map/all_to_all | solution.py:229
  115.1 1.3 %shard_map.100 = f32[8,128]{1,0:T(8,128)} custom-call(s32[1]{0:T(128)} %bitcast.12.group_ref, f32[16,8,128]{2,1,0:T(8,128)S(1)} %all-to-all-done.2.terms_ref, s32[8,128]{1,0:T(8,128)S(1)} %bitcast.21, s32[8,128]{1,0:T(8,128)S(1)} %bitcast.23), custom_call_target="tpu_custom_call" | custom-call | tf_op jit(solution)/shard_map/pallas_call | solution.py:158
  116.3 0.0 collective-permute-done.3.down_ref
  116.3 4.8 %collective-permute-done.4.up_ref = f32[256,128]{1,0:T(8,128)S(1)} collective-permute-done((f32[256,128]{1,0:T(8,128)S(1)}, f32[256,128]{1,0:T(8,128)S(1)}, u32[]{:S(2)}, u32[]{:S(2)}) %collective-permute-start.4) | collective-permute-done | bytes 131104 | tf_op jit(solution)/shard_map/ppermute | solution.py:213
  121.2 0.0 copy-done.4
  121.2 0.9 copy-done.5
  122.1 0.7 shard_map.98
  (13 shorter events, 0.1 us)
Async XLA Ops:
  3.4 54.9 %all-to-all-start = ((bf16[128,16,128]{2,1,0:T(8,128)(2,1)}), bf16[128,16,128]{2,1,0:T(8,128)(2,1)S(1)}, u32[]{:S(2)}, u32[]{:S(2)}) async-start(bf16[128,16,128]{2,1,0:T(8,128)(2,1)} %shard_map.94), calls=%async_computation | async-start | bytes 1048576 | tf_op jit(solution)/shard_map/all_to_all | solution.py:186
  27.5 0.8 copy-start.1
  28.3 0.8 copy-start.3
  45.2 13.1 %copy-start.8 = (f32[1024,128]{1,0:T(8,128)}, f32[1024,128]{1,0:T(8,128)S(1)}, u32[]{:S(2)}) copy-start(f32[1024,128]{1,0:T(8,128)S(1)} %all-gather) | copy-start | bytes 1572868
  45.2 10.8 %collective-permute-start = (f32[4,256,128]{2,1,0:T(8,128)S(1)}, f32[4,256,128]{2,1,0:T(8,128)S(1)}, u32[]{:S(2)}, u32[]{:S(2)}) collective-permute-start(f32[4,256,128]{2,1,0:T(8,128)S(1)} %bitcast.24), channel_id=1, source_target_pairs={{0,8},{8,0},{16,24},{24,16},{32,40},{40,32},{48,56},{56,48},{1,9},... | collective-permute-start | bytes 1572872 | tf_op jit(solution)/shard_map/ppermute | solution.py:192
  55.9 2.4 %copy-start.10 = (f32[4,256,128]{2,1,0:T(8,128)}, f32[4,256,128]{2,1,0:T(8,128)S(1)}, u32[]{:S(2)}) copy-start(f32[4,256,128]{2,1,0:T(8,128)S(1)} %collective-permute-done.other_ref) | copy-start | bytes 1572868
  58.3 0.8 copy-start.9
  59.1 56.0 %copy-start.6 = (s32[128,8]{0,1:T(8,128)S(1)}, s32[128,8]{0,1:T(8,128)}, u32[]{:S(2)}) copy-start(s32[128,8]{0,1:T(8,128)} %param.8) | copy-start | bytes 12292
  59.1 56.0 %copy-start.7 = (s32[128,8]{0,1:T(8,128)S(1)}, s32[128,8]{0,1:T(8,128)}, u32[]{:S(2)}) copy-start(s32[128,8]{0,1:T(8,128)} %param.9) | copy-start | bytes 12292
  59.1 62.1 %copy-start.2 = (bf16[1,256,128]{2,1,0:T(8,128)(2,1)S(1)}, bf16[1,256,128]{2,1,0:T(8,128)(2,1)}, u32[]{:S(2)}) copy-start(bf16[1,256,128]{2,1,0:T(8,128)(2,1)} %param.12) | copy-start | bytes 196612
  59.1 62.1 %copy-start.4 = (bf16[1,256,128]{2,1,0:T(8,128)(2,1)S(1)}, bf16[1,256,128]{2,1,0:T(8,128)(2,1)}, u32[]{:S(2)}) copy-start(bf16[1,256,128]{2,1,0:T(8,128)(2,1)} %param.13) | copy-start | bytes 196612
  62.8 40.7 %collective-permute-start.1 = (f32[640,128]{1,0:T(8,128)}, f32[640,128]{1,0:T(8,128)S(1)}, u32[]{:S(2)}, u32[]{:S(2)}) collective-permute-start(f32[640,128]{1,0:T(8,128)} %get-tuple-element.19), channel_id=1, source_target_pairs={{0,8},{8,16},{16,24},{24,32},{32,40},{40,48},{48,56},{56,0},{1,9},... | collective-permute-start | bytes 983048 | tf_op jit(solution)/shard_map/ppermute | solution.py:213
  66.0 37.5 %collective-permute-start.2 = (f32[640,128]{1,0:T(8,128)}, f32[640,128]{1,0:T(8,128)S(1)}, u32[]{:S(2)}, u32[]{:S(2)}) collective-permute-start(f32[640,128]{1,0:T(8,128)} %get-tuple-element.20), channel_id=1, source_target_pairs={{0,56},{8,0},{16,8},{24,16},{32,24},{40,32},{48,40},{56,48},{1,57}... | collective-permute-start | bytes 983048 | tf_op jit(solution)/shard_map/ppermute | solution.py:213
  93.1 22.0 %all-to-all-start.2 = ((f32[16,8,128]{2,1,0:T(8,128)}), f32[16,8,128]{2,1,0:T(8,128)S(1)}, u32[]{:S(2)}, u32[]{:S(2)}) async-start(f32[16,8,128]{2,1,0:T(8,128)} %shard_map.99), calls=%async_computation.2 | async-start | bytes 131072 | tf_op jit(solution)/shard_map/all_to_all | solution.py:229
  103.5 1.0 copy-start
  104.6 11.8 %collective-permute-start.3 = (f32[256,128]{1,0:T(8,128)S(1)}, f32[256,128]{1,0:T(8,128)S(1)}, u32[]{:S(2)}, u32[]{:S(2)}) collective-permute-start(f32[256,128]{1,0:T(8,128)S(1)} %get-tuple-element.23), channel_id=1, source_target_pairs={{0,40},{8,48},{16,56},{24,0},{32,8},{40,16},{48,24},{56,32},{1,41}... | collective-permute-start | bytes 393224 | tf_op jit(solution)/shard_map/ppermute | solution.py:213
  106.8 14.4 %collective-permute-start.4 = (f32[256,128]{1,0:T(8,128)S(1)}, f32[256,128]{1,0:T(8,128)S(1)}, u32[]{:S(2)}, u32[]{:S(2)}) collective-permute-start(f32[256,128]{1,0:T(8,128)S(1)} %get-tuple-element.24), channel_id=1, source_target_pairs={{0,24},{8,32},{16,40},{24,48},{32,56},{40,0},{48,8},{56,16},{1,25}... | collective-permute-start | bytes 393224 | tf_op jit(solution)/shard_map/ppermute | solution.py:213
  121.2 0.9 copy-start.5

commit v6 on v3

--- a/solution.py
+++ b/solution.py
@@ -9,6 +9,7 @@
 SLOTS = 16
 NT = (((1,), (1,)), ((), ()))
 F32 = jnp.float32
+LARGE = 56 << 20
 BF16 = jnp.bfloat16
 
 
@@ -50,8 +51,8 @@
     out_ref[...] = gate_pre * jax.nn.sigmoid(gate_pre) * up_ref[...].astype(F32)
 
 
-def matmul_kernel(where_ref, rows_ref, w_ref, same_ref, other_ref, give_ref, *outs):
-    keep_refs, (term_ref, gate_ref) = outs[:-2], outs[-2:]
+def matmul_kernel(where_ref, rows_ref, w_ref, same_ref, other_ref, *outs):
+    give_ref, keep_ref, gate_ref, term_ref = outs
     groups, parts, _, lane_count = rows_ref.shape
     capacity = groups * SLOTS
     col_width = w_ref.shape[1] // parts
@@ -63,17 +64,16 @@
     terms = jnp.zeros((capacity, lane_count), F32)
     for d in range(quads):
         target = (quad + d) % quads
-        for mine, hidden_ref in ((0, other_ref), (1, same_ref)):
-            unit = target * 2 + (own if mine else 1 - own)
-            first = pl.multiple_of(unit * lane_count, lane_count)
-            part = lax.dot_general(
-                x, w_ref[pl.ds(first, lane_count), :], NT, preferred_element_type=F32
-            )
-            terms += part * hidden_ref[target]
-            if mine:
-                keep_refs[d][...] = part
-            else:
-                give_ref[d] = part
+        firsts = [
+            pl.multiple_of((target * 2 + parity) * lane_count, lane_count)
+            for parity in (1 - own, own)
+        ]
+        w = jnp.concatenate([w_ref[pl.ds(first, lane_count), :] for first in firsts], axis=0)
+        both = lax.dot_general(x, w, NT, preferred_element_type=F32)
+        give, keep = both[:, :lane_count], both[:, lane_count:]
+        give_ref[d] = give
+        keep_ref[d] = keep
+        terms += give * other_ref[target] + keep * same_ref[target]
     total = jnp.sum(terms, axis=1, keepdims=True)
     row_ids, lane_ids = rows((capacity, lane_count)), lanes((capacity, lane_count))
     hit = lane_ids == group % (lane_count // SLOTS) * SLOTS + row_ids % SLOTS
@@ -131,13 +131,13 @@
 SMEM = pl.BlockSpec(memory_space=pltpu.SMEM)
 
 
-def call(kernel, specs, out_shape, *args):
+def call(kernel, specs, out_shape, *args, limit=24 << 20):
     return pl.pallas_call(
         kernel,
         in_specs=specs,
         out_specs=jax.tree.map(lambda _: VMEM, out_shape),
         out_shape=out_shape,
-        compiler_params=pltpu.CompilerParams(vmem_limit_bytes=24 << 20),
+        compiler_params=pltpu.CompilerParams(vmem_limit_bytes=limit),
     )(*args)
 
 
@@ -157,34 +157,37 @@
         routes.T,
         slots.T,
         gates.T,
+        limit=LARGE,
     )
     send, gate_pre, up_pre = lax.optimization_barrier((send, saved_gate[0], saved_up[0]))
     expert_rows = lax.all_to_all(send, ("group", "xc"), 0, 0, tiled=True)
 
-    hidden = call(hidden_kernel, [VMEM] * 2, column, gate_pre, up_pre)
+    hidden = call(hidden_kernel, [VMEM] * 2, column, gate_pre, up_pre, limit=LARGE)
     same = lax.all_gather(
         hidden, "y", axis_index_groups=[list(range(p, shard_count, 2)) for p in (0, 1)]
     )
+    quads = shard_count // 2
     other = lax.ppermute(same, "y", [(i, i ^ 1) for i in range(shard_count)])
-    give, k0, k1, k2, k3, terms, gate_rows = call(
+    give, keep, gate_rows, terms = call(
         matmul_kernel,
         [SMEM] + [VMEM] * 4,
         (
-            shape((shard_count // 2, capacity, lane_count), F32),
-            *[column] * 4,
+            shape((quads, capacity, lane_count), F32),
+            shape((quads, capacity, lane_count), F32),
+            column,
             shape((groups, 1, lane_count), F32),
-            column,
         ),
         jnp.stack([group, shard]),
         expert_rows.reshape(groups, parts, SLOTS, lane_count),
         w_down[0],
         same,
         other,
+        limit=LARGE,
     )
 
     got = lax.ppermute(give, "y", [(i, i ^ 1) for i in range(shard_count)])
     home = lax.all_to_all(terms, "group", 0, 0, tiled=True)
-    sums = [k + got[d] for d, k in enumerate((k0, k1, k2, k3))]
+    sums = [keep[d] + got[d] for d in range(quads)]
     for d in (2, 1, 3):
         sums[d] = lax.ppermute(
             sums[d], "y", [(i, (i + 2 * d) % shard_count) for i in range(shard_count)]
@@ -197,6 +200,7 @@
     grad_gate, grad_up = call(
         output_kernel, [VMEM] * 7, (out, out), *sums, gate_rows, saved_gate[0], saved_up[0]
     )
+    every_term, grad_gate, grad_up = lax.optimization_barrier((every_term, grad_gate, grad_up))
     grad_gates = call(
         collect_kernel,
         [VMEM] * 3,

time: 120 us -> 116 us (0.967)
  blocking collectives: 37.2 us -> 16.2 us
  starting transfers between devices: 54.4 us -> 65.7 us
  waiting for transfers between devices: 10.8 us -> 19.5 us
  local copies, waits for them, and re-layouts: 7.87 us -> 0.82 us
  Pallas kernels: 6.87 us -> 11 us
    all_to_all x1 -> x0, blocking collectives: 21.2 us -> none  [shards(): every_term = lax.all_to_all(spread, ('y', 'xc'), 0, 0, tiled=True)]
    all_to_all x0 -> x1, starting transfers between devices: none -> 11.3 us  [shards(): every_term = lax.all_to_all(spread, ('y', 'xc'), 0, 0, tiled=True)]
    all_to_all x0 -> x1, waiting for transfers between devices: none -> 9.31 us  [shards(): every_term = lax.all_to_all(spread, ('y', 'xc'), 0, 0, tiled=True)]
    unnamed x34 -> x16, local copies, waits for them, and re-layouts: 7.87 us -> 0.82 us
    pallas_call x6, Pallas kernels: 6.87 us -> 11 us  [call(): pl.pallas_call(kernel, in_specs=specs, out_specs=jax.tree.map(lambda _: V...]
  transfers between devices with their start and end apart: 7 -> 8, of which waited for: 2 -> 3; matrix products, arithmetic and copies ran while one was open for 1% -> 2% of each run, Pallas kernels for 1% -> 3%
where the time goes in v6:
time: 116 us
  starting transfers between devices  65.7 us (57%)
  waiting for transfers between devices  19.5 us (17%)
  blocking collectives  16.2 us (14%)
  Pallas kernels  11 us (9%)
  other arithmetic  1.74 us (2%)
    all_to_all x1, starting transfers between devices, shards(): expert_rows = lax.all_to_all(send, ('group', 'xc'), 0, 0, tiled=True)  24.1 us
    all_gather x1, blocking collectives, shards(): lax.all_gather(hidden, 'y', axis_index_groups=[list(range(p, shard_count,...  16.2 us
    ppermute x3, starting transfers between devices, shards(): lax.ppermute(sums[d], 'y', [(i, (i + 2 * d) % shard_count) for i in range...  13.5 us
    all_to_all x1, starting transfers between devices, shards(): every_term = lax.all_to_all(spread, ('y', 'xc'), 0, 0, tiled=True)  11.3 us
    all_to_all x1, starting transfers between devices, shards(): home = lax.all_to_all(terms, 'group', 0, 0, tiled=True)  11.3 us
    pallas_call x6, Pallas kernels, call(): pl.pallas_call(kernel, in_specs=specs, out_specs=jax.tree.map(lambda _: V...  11 us
    all_to_all x1, waiting for transfers between devices, shards(): every_term = lax.all_to_all(spread, ('y', 'xc'), 0, 0, tiled=True)  9.31 us
    ppermute x1, waiting for transfers between devices, shards(): other = lax.ppermute(same, 'y', [(i, i ^ 1) for i in range(shard_count)])  7.88 us
  transfers between devices with their start and end apart: 8, of which 3 were waited for; matrix products, arithmetic and copies ran while one was open for 2% of the time, Pallas kernels for 3%

profile of v6, /device:TPU:1, one launch (start us, length us, event | category | flops | bytes accessed | tf_op | source)
XLA Modules:
  0.0 115.8 jit_solution(14130207896648913014)
XLA Ops:
  0.6 2.8 %shard_map.94 = bf16[128,16,128]{2,1,0:T(8,128)(2,1)} custom-call(bf16[112,128]{1,0:T(8,128)(2,1)} %bitcast.36, s32[8,128]{1,0:T(8,128)} %bitcast.28, s32[8,128]{1,0:T(8,128)} %bitcast.30, bf16[8,128]{1,0:T(8,128)(2,1)} %bitcast.38), custom_call_target="tpu_custom_call" | custom-call | tf_op jit(solution)/shard_map/pallas_call | solution.py:135
  3.4 24.1 %all-to-all-start = ((bf16[128,16,128]{2,1,0:T(8,128)(2,1)}), bf16[128,16,128]{2,1,0:T(8,128)(2,1)S(1)}, u32[]{:S(2)}, u32[]{:S(2)}) async-start(bf16[128,16,128]{2,1,0:T(8,128)(2,1)} %shard_map.94), calls=%async_computation | async-start | bytes 1048576 | tf_op jit(solution)/shard_map/all_to_all | solution.py:163
  27.5 1.6 %shard_map.95 = f32[256,128]{1,0:T(8,128)} custom-call(bf16[256,128]{1,0:T(8,128)(2,1)} %bitcast.23, bf16[256,128]{1,0:T(8,128)(2,1)} %bitcast.25), custom_call_target="tpu_custom_call" | custom-call | tf_op jit(solution)/shard_map/pallas_call | solution.py:135
  29.0 16.2 %all-gather = f32[1024,128]{1,0:T(8,128)S(1)} all-gather(f32[256,128]{1,0:T(8,128)} %shard_map.95), channel_id=2, replica_groups={{0,16,32,48},{8,24,40,56},{1,17,33,49},{9,25,41,57},{2,18,34,50},{10,26..., dimensions={0}, use_global_device_ids=true | all-gather | bytes 655360 | tf_op jit(solution)/shard_map/all_gather | solution.py:166
  45.2 2.3 %collective-permute-start = (f32[4,256,128]{2,1,0:T(8,128)S(1)}, f32[4,256,128]{2,1,0:T(8,128)S(1)}, u32[]{:S(2)}, u32[]{:S(2)}) collective-permute-start(f32[4,256,128]{2,1,0:T(8,128)S(1)} %bitcast.32), channel_id=1, source_target_pairs={{0,8},{8,0},{16,24},{24,16},{32,40},{40,32},{48,56},{56,48},{1,9},... | collective-permute-start | bytes 1572872 | tf_op jit(solution)/shard_map/ppermute | solution.py:170
  47.5 0.6 pad_add_fusion.where_ref
  48.1 7.9 %collective-permute-done.other_ref = f32[4,256,128]{2,1,0:T(8,128)S(1)} collective-permute-done((f32[4,256,128]{2,1,0:T(8,128)S(1)}, f32[4,256,128]{2,1,0:T(8,128)S(1)}, u32[]{:S(2)}, u32[]{:S(2)}) %collective-permute-start) | collective-permute-done | bytes 524320 | tf_op jit(solution)/shard_map/ppermute | solution.py:170
  55.9 2.3 %all-to-all-done = bf16[128,16,128]{2,1,0:T(8,128)(2,1)S(1)} async-done(((bf16[128,16,128]{2,1,0:T(8,128)(2,1)}), bf16[128,16,128]{2,1,0:T(8,128)(2,1)S(1)}, u32[]{:S(2)}, u32[]{:S(2)}) %all-to-all-start) | async-done | bytes 524320 | tf_op jit(solution)/shard_map/all_to_all | solution.py:163
  58.3 0.0 copy-done.5
  58.3 0.0 copy-done.7
  58.3 0.8 copy-done.6
  59.1 3.7 %shard_map.96 = (f32[4,256,128]{2,1,0:T(8,128)}, f32[4,256,128]{2,1,0:T(8,128)}, f32[256,128]{1,0:T(8,128)}, f32[16,1,128]{2,1,0:T(1,128)}) custom-call(s32[2]{0:T(128)} %pad_add_fusion.where_ref, bf16[16,8,16,128]{3,2,1,0:T(8,128)(2,1)} %bitcast.34, bf16[1024,896]{1,0:T(8,128)(2,1)} %bitcast.35, f32[4,256,128]{2,1,0:T(8,128)} %bitcast.33, ...), custom_call_target="tpu_custom_call" | custom-call | tf_op jit(solution)/shard_map/pallas_call | solution.py:135
  62.8 0.0 copy-start.4
  62.8 3.3 %collective-permute-start.1 = (f32[4,256,128]{2,1,0:T(8,128)}, f32[4,256,128]{2,1,0:T(8,128)S(1)}, u32[]{:S(2)}, u32[]{:S(2)}) collective-permute-start(f32[4,256,128]{2,1,0:T(8,128)} %get-tuple-element.20), channel_id=1, source_target_pairs={{0,8},{8,0},{16,24},{24,16},{32,40},{40,32},{48,56},{56,48},{1,9},... | collective-permute-start | bytes 1572872 | tf_op jit(solution)/shard_map/ppermute | solution.py:188
  66.2 11.3 %all-to-all-start.1 = ((f32[16,1,128]{2,1,0:T(1,128)}), f32[16,1,128]{2,1,0:T(1,128)S(1)}, u32[]{:S(2)}, u32[]{:S(2)}) async-start(f32[16,1,128]{2,1,0:T(1,128)} %get-tuple-element.18), calls=%async_computation.1 | async-start | bytes 16384 | tf_op jit(solution)/shard_map/all_to_all | solution.py:189
  77.5 0.0 collective-permute-done.1
  77.5 1.2 fusion
  78.6 5.3 %collective-permute-start.4 = (f32[256,128]{1,0:T(8,128)S(1)}, f32[256,128]{1,0:T(8,128)S(1)}, u32[]{:S(2)}, u32[]{:S(2)}) collective-permute-start(f32[256,128]{1,0:T(8,128)S(1)} %get-tuple-element.27), channel_id=1, source_target_pairs={{0,48},{8,56},{16,0},{24,8},{32,16},{40,24},{48,32},{56,40},{1,49}... | collective-permute-start | bytes 393224 | tf_op jit(solution)/shard_map/ppermute | solution.py:192
  83.9 5.9 %collective-permute-start.3 = (f32[256,128]{1,0:T(8,128)S(1)}, f32[256,128]{1,0:T(8,128)S(1)}, u32[]{:S(2)}, u32[]{:S(2)}) collective-permute-start(f32[256,128]{1,0:T(8,128)S(1)} %get-tuple-element.28), channel_id=1, source_target_pairs={{0,32},{8,40},{16,48},{24,56},{32,0},{40,8},{48,16},{56,24},{1,33}... | collective-permute-start | bytes 393224 | tf_op jit(solution)/shard_map/ppermute | solution.py:192
  89.8 2.3 %collective-permute-start.2 = (f32[256,128]{1,0:T(8,128)S(1)}, f32[256,128]{1,0:T(8,128)S(1)}, u32[]{:S(2)}, u32[]{:S(2)}) collective-permute-start(f32[256,128]{1,0:T(8,128)S(1)} %get-tuple-element.29), channel_id=1, source_target_pairs={{0,16},{8,24},{16,32},{24,40},{32,48},{40,56},{48,0},{56,8},{1,17}... | collective-permute-start | bytes 393224 | tf_op jit(solution)/shard_map/ppermute | solution.py:192
  92.1 0.0 all-to-all-done.1.home_ref
  92.1 0.7 shard_map.97
  92.8 11.3 %all-to-all-start.2 = ((f32[64,2,128]{2,1,0:T(2,128)}), f32[64,2,128]{2,1,0:T(2,128)S(1)}, u32[]{:S(2)}, u32[]{:S(2)}) async-start(f32[64,2,128]{2,1,0:T(2,128)} %shard_map.97), calls=%async_computation.2 | async-start | bytes 131072 | tf_op jit(solution)/shard_map/all_to_all | solution.py:198
  104.1 0.0 collective-permute-done.4.h3
  104.1 0.0 collective-permute-done.3.h2
  104.1 0.0 collective-permute-done.2.h1
  104.1 0.0 copy-done
  104.1 0.0 copy-done.1
  104.2 0.7 shard_map.98
  104.9 9.3 %all-to-all-done.2 = f32[64,2,128]{2,1,0:T(2,128)S(1)} async-done(((f32[64,2,128]{2,1,0:T(2,128)}), f32[64,2,128]{2,1,0:T(2,128)S(1)}, u32[]{:S(2)}, u32[]{:S(2)}) %all-to-all-start.2) | async-done | bytes 65568 | tf_op jit(solution)/shard_map/all_to_all | solution.py:198
  114.2 0.0 copy-done.3
  114.2 1.6 %shard_map.99 = f32[8,128]{1,0:T(8,128)} custom-call(f32[8,8,2,128]{3,2,1,0:T(2,128)S(1)} %bitcast.27, s32[8,128]{1,0:T(8,128)S(1)} %bitcast.29, s32[8,128]{1,0:T(8,128)S(1)} %bitcast.31), custom_call_target="tpu_custom_call" | custom-call | tf_op jit(solution)/shard_map/pallas_call | solution.py:135
  (9 shorter events, 0.0 us)
Async XLA Ops:
  3.4 54.9 %all-to-all-start = ((bf16[128,16,128]{2,1,0:T(8,128)(2,1)}), bf16[128,16,128]{2,1,0:T(8,128)(2,1)S(1)}, u32[]{:S(2)}, u32[]{:S(2)}) async-start(bf16[128,16,128]{2,1,0:T(8,128)(2,1)} %shard_map.94), calls=%async_computation | async-start | bytes 1048576 | tf_op jit(solution)/shard_map/all_to_all | solution.py:163
  45.2 13.1 %copy-start.5 = (f32[1024,128]{1,0:T(8,128)}, f32[1024,128]{1,0:T(8,128)S(1)}, u32[]{:S(2)}) copy-start(f32[1024,128]{1,0:T(8,128)S(1)} %all-gather) | copy-start | bytes 1572868
  45.2 10.8 %collective-permute-start = (f32[4,256,128]{2,1,0:T(8,128)S(1)}, f32[4,256,128]{2,1,0:T(8,128)S(1)}, u32[]{:S(2)}, u32[]{:S(2)}) collective-permute-start(f32[4,256,128]{2,1,0:T(8,128)S(1)} %bitcast.32), channel_id=1, source_target_pairs={{0,8},{8,0},{16,24},{24,16},{32,40},{40,32},{48,56},{56,48},{1,9},... | collective-permute-start | bytes 1572872 | tf_op jit(solution)/shard_map/ppermute | solution.py:170
  55.9 2.4 %copy-start.7 = (f32[4,256,128]{2,1,0:T(8,128)}, f32[4,256,128]{2,1,0:T(8,128)S(1)}, u32[]{:S(2)}) copy-start(f32[4,256,128]{2,1,0:T(8,128)S(1)} %collective-permute-done.other_ref) | copy-start | bytes 1572868
  58.3 0.8 copy-start.6
  59.1 45.0 %copy-start = (bf16[1,256,128]{2,1,0:T(8,128)(2,1)S(1)}, bf16[1,256,128]{2,1,0:T(8,128)(2,1)}, u32[]{:S(2)}) copy-start(bf16[1,256,128]{2,1,0:T(8,128)(2,1)} %param.12) | copy-start | bytes 196612
  59.1 45.0 %copy-start.1 = (bf16[1,256,128]{2,1,0:T(8,128)(2,1)S(1)}, bf16[1,256,128]{2,1,0:T(8,128)(2,1)}, u32[]{:S(2)}) copy-start(bf16[1,256,128]{2,1,0:T(8,128)(2,1)} %param.13) | copy-start | bytes 196612
  62.8 41.3 %copy-start.2 = (f32[256,128]{1,0:T(8,128)S(1)}, f32[256,128]{1,0:T(8,128)}, u32[]{:S(2)}) copy-start(f32[256,128]{1,0:T(8,128)} %get-tuple-element.21.gate_ref) | copy-start | bytes 393220
  62.8 51.4 %copy-start.3 = (s32[128,8]{0,1:T(8,128)S(1)}, s32[128,8]{0,1:T(8,128)}, u32[]{:S(2)}) copy-start(s32[128,8]{0,1:T(8,128)} %param.8) | copy-start | bytes 12292
  62.8 51.4 %copy-start.4 = (s32[128,8]{0,1:T(8,128)S(1)}, s32[128,8]{0,1:T(8,128)}, u32[]{:S(2)}) copy-start(s32[128,8]{0,1:T(8,128)} %param.9) | copy-start | bytes 12292
  62.8 14.6 %collective-permute-start.1 = (f32[4,256,128]{2,1,0:T(8,128)}, f32[4,256,128]{2,1,0:T(8,128)S(1)}, u32[]{:S(2)}, u32[]{:S(2)}) collective-permute-start(f32[4,256,128]{2,1,0:T(8,128)} %get-tuple-element.20), channel_id=1, source_target_pairs={{0,8},{8,0},{16,24},{24,16},{32,40},{40,32},{48,56},{56,48},{1,9},... | collective-permute-start | bytes 1572872 | tf_op jit(solution)/shard_map/ppermute | solution.py:188
  66.2 25.9 %all-to-all-start.1 = ((f32[16,1,128]{2,1,0:T(1,128)}), f32[16,1,128]{2,1,0:T(1,128)S(1)}, u32[]{:S(2)}, u32[]{:S(2)}) async-start(f32[16,1,128]{2,1,0:T(1,128)} %get-tuple-element.18), calls=%async_computation.1 | async-start | bytes 16384 | tf_op jit(solution)/shard_map/all_to_all | solution.py:189
  78.6 25.5 %collective-permute-start.4 = (f32[256,128]{1,0:T(8,128)S(1)}, f32[256,128]{1,0:T(8,128)S(1)}, u32[]{:S(2)}, u32[]{:S(2)}) collective-permute-start(f32[256,128]{1,0:T(8,128)S(1)} %get-tuple-element.27), channel_id=1, source_target_pairs={{0,48},{8,56},{16,0},{24,8},{32,16},{40,24},{48,32},{56,40},{1,49}... | collective-permute-start | bytes 393224 | tf_op jit(solution)/shard_map/ppermute | solution.py:192
  83.9 20.2 %collective-permute-start.3 = (f32[256,128]{1,0:T(8,128)S(1)}, f32[256,128]{1,0:T(8,128)S(1)}, u32[]{:S(2)}, u32[]{:S(2)}) collective-permute-start(f32[256,128]{1,0:T(8,128)S(1)} %get-tuple-element.28), channel_id=1, source_target_pairs={{0,32},{8,40},{16,48},{24,56},{32,0},{40,8},{48,16},{56,24},{1,33}... | collective-permute-start | bytes 393224 | tf_op jit(solution)/shard_map/ppermute | solution.py:192
  89.8 14.3 %collective-permute-start.2 = (f32[256,128]{1,0:T(8,128)S(1)}, f32[256,128]{1,0:T(8,128)S(1)}, u32[]{:S(2)}, u32[]{:S(2)}) collective-permute-start(f32[256,128]{1,0:T(8,128)S(1)} %get-tuple-element.29), channel_id=1, source_target_pairs={{0,16},{8,24},{16,32},{24,40},{32,48},{40,56},{48,0},{56,8},{1,17}... | collective-permute-start | bytes 393224 | tf_op jit(solution)/shard_map/ppermute | solution.py:192
  92.8 21.4 %all-to-all-start.2 = ((f32[64,2,128]{2,1,0:T(2,128)}), f32[64,2,128]{2,1,0:T(2,128)S(1)}, u32[]{:S(2)}, u32[]{:S(2)}) async-start(f32[64,2,128]{2,1,0:T(2,128)} %shard_map.97), calls=%async_computation.2 | async-start | bytes 131072 | tf_op jit(solution)/shard_map/all_to_all | solution.py:198

commit v7 on v6

--- a/solution.py
+++ b/solution.py
@@ -21,7 +21,9 @@
     return lax.broadcasted_iota(jnp.int32, shape, 0)
 
 
-def dispatch_kernel(tokens_ref, routes_ref, slots_ref, gates_ref, out_ref):
+def dispatch_kernel(
+    tokens_ref, routes_ref, slots_ref, gates_ref, gate_pre_ref, up_pre_ref, out_ref, hidden_ref
+):
     col_width, tok_count = tokens_ref.shape
     lane_count = out_ref.shape[2]
     place = routes_ref[...] * SLOTS + slots_ref[...]
@@ -33,31 +35,24 @@
     chunk = 256
     for start in range(0, out_ref.shape[0] * SLOTS, chunk):
         row_ids = rows((chunk, tok_count)) + start
-        pick = jnp.zeros((chunk, tok_count), F32)
         gate = jnp.zeros((chunk, tok_count), F32)
         for k in range(place.shape[0]):
-            hit = row_ids == place[k : k + 1, :]
-            pick = jnp.where(hit, 1.0, pick)
-            gate = jnp.where(hit, gates[k : k + 1, :], gate)
+            gate = jnp.where(row_ids == place[k : k + 1, :], gates[k : k + 1, :], gate)
+        pick = jnp.where(gate > 0.0, 1.0, 0.0)
         both = jnp.concatenate([pick.astype(BF16), gate.astype(BF16)], axis=1)
         block = lax.dot_general(both, source, NT, preferred_element_type=F32)
         out_ref[start // SLOTS : (start + chunk) // SLOTS] = block.astype(BF16).reshape(
             chunk // SLOTS, SLOTS, lane_count
         )
-
-
-def hidden_kernel(gate_ref, up_ref, out_ref):
-    gate_pre = gate_ref[...].astype(F32)
-    out_ref[...] = gate_pre * jax.nn.sigmoid(gate_pre) * up_ref[...].astype(F32)
-
-
-def matmul_kernel(where_ref, rows_ref, w_ref, same_ref, other_ref, *outs):
-    give_ref, keep_ref, gate_ref, term_ref = outs
+    gate_pre = gate_pre_ref[...].astype(F32)
+    hidden_ref[...] = gate_pre * jax.nn.sigmoid(gate_pre) * up_pre_ref[...].astype(F32)
+
+
+def matmul_kernel(shard_ref, rows_ref, w_ref, same_ref, give_ref, keep_ref, gate_ref, base_ref):
     groups, parts, _, lane_count = rows_ref.shape
     capacity = groups * SLOTS
     col_width = w_ref.shape[1] // parts
-    group, shard = where_ref[0], where_ref[1]
-    own, quad = shard % 2, shard // 2
+    own, quad = shard_ref[0] % 2, shard_ref[0] // 2
     quads = give_ref.shape[0]
     blocks = [rows_ref[:, e].reshape(capacity, lane_count) for e in range(parts)]
     x = jnp.concatenate([b[:, :col_width] for b in blocks], axis=1)
@@ -70,19 +65,28 @@
         ]
         w = jnp.concatenate([w_ref[pl.ds(first, lane_count), :] for first in firsts], axis=0)
         both = lax.dot_general(x, w, NT, preferred_element_type=F32)
-        give, keep = both[:, :lane_count], both[:, lane_count:]
-        give_ref[d] = give
-        keep_ref[d] = keep
-        terms += give * other_ref[target] + keep * same_ref[target]
+        give_ref[d] = both[:, :lane_count]
+        keep_ref[d] = both[:, lane_count:]
+        terms += both[:, lane_count:] * same_ref[target]
+    base_ref[...] = terms
+    gate = jnp.where(lanes((capacity, lane_count)) == col_width, blocks[0].astype(F32), 0.0)
+    gate_ref[...] = jnp.broadcast_to(
+        jnp.sum(gate, axis=1, keepdims=True), (capacity, lane_count)
+    )
+
+
+def terms_kernel(group_ref, shard_ref, give_ref, other_ref, base_ref, term_ref):
+    quads, capacity, lane_count = give_ref.shape
+    groups = term_ref.shape[0]
+    group, quad = group_ref[0], shard_ref[0] // 2
+    terms = base_ref[...]
+    for d in range(quads):
+        terms += give_ref[d] * other_ref[(quad + d) % quads]
     total = jnp.sum(terms, axis=1, keepdims=True)
     row_ids, lane_ids = rows((capacity, lane_count)), lanes((capacity, lane_count))
     hit = lane_ids == group % (lane_count // SLOTS) * SLOTS + row_ids % SLOTS
     term_ref[...] = jnp.sum(
         jnp.where(hit, total, 0.0).reshape(groups, SLOTS, lane_count), axis=1, keepdims=True
-    )
-    gate = jnp.where(lane_ids == col_width, blocks[0].astype(F32), 0.0)
-    gate_ref[...] = jnp.broadcast_to(
-        jnp.sum(gate, axis=1, keepdims=True), (capacity, lane_count)
     )
 
 
@@ -113,18 +117,27 @@
         table += terms_ref[s]
     routes = routes_ref[...]
     place = routes // EXP_GRP * SLOTS + slots_ref[...]
+    places = jnp.concatenate([place[k : k + 1, :] for k in range(route_count)], axis=1)
+    picked = jnp.zeros((experts, route_count * tok_count), F32)
+    for h in range(halves):
+        rest = table[:, h, :]
+        parts = []
+        for _ in range(3):
+            part = rest.astype(BF16)
+            parts.append(part)
+            rest = rest - part.astype(F32)
+        hit = rows((lane_count, route_count * tok_count)) + h * lane_count == places
+        every = jnp.dot(
+            jnp.concatenate(parts, axis=0),
+            jnp.where(hit, 1.0, 0.0).astype(BF16),
+            preferred_element_type=F32,
+        )
+        for i in range(3):
+            picked += every[i * experts : (i + 1) * experts]
     for k in range(route_count):
-        picked = jnp.zeros((experts, tok_count), F32)
-        for h in range(halves):
-            hit = rows((lane_count, tok_count)) + h * lane_count == place[k : k + 1, :]
-            picked += jnp.dot(
-                table[:, h, :],
-                jnp.where(hit, 1.0, 0.0),
-                preferred_element_type=F32,
-                precision=lax.Precision.HIGHEST,
-            )
         own = rows((experts, tok_count)) == routes[k : k + 1, :] % EXP_GRP
-        out_ref[k : k + 1, :] = jnp.sum(jnp.where(own, picked, 0.0), axis=0, keepdims=True)
+        column = picked[:, k * tok_count : (k + 1) * tok_count]
+        out_ref[k : k + 1, :] = jnp.sum(jnp.where(own, column, 0.0), axis=0, keepdims=True)
 
 
 VMEM = pl.BlockSpec(memory_space=pltpu.VMEM)
@@ -149,39 +162,45 @@
     shard = lax.axis_index("y").astype(jnp.int32)
     column = shape((capacity, lane_count), F32)
 
-    send = call(
+    send, hidden = call(
         dispatch_kernel,
-        [VMEM] * 4,
-        shape((groups * parts, SLOTS, lane_count), BF16),
+        [VMEM] * 6,
+        (shape((groups * parts, SLOTS, lane_count), BF16), column),
         grad_out.T,
         routes.T,
         slots.T,
         gates.T,
+        saved_gate[0],
+        saved_up[0],
         limit=LARGE,
     )
-    send, gate_pre, up_pre = lax.optimization_barrier((send, saved_gate[0], saved_up[0]))
     expert_rows = lax.all_to_all(send, ("group", "xc"), 0, 0, tiled=True)
 
-    hidden = call(hidden_kernel, [VMEM] * 2, column, gate_pre, up_pre, limit=LARGE)
     same = lax.all_gather(
         hidden, "y", axis_index_groups=[list(range(p, shard_count, 2)) for p in (0, 1)]
     )
     quads = shard_count // 2
     other = lax.ppermute(same, "y", [(i, i ^ 1) for i in range(shard_count)])
-    give, keep, gate_rows, terms = call(
+    held = shape((quads, capacity, lane_count), F32)
+    give, keep, gate_rows, base = call(
         matmul_kernel,
-        [SMEM] + [VMEM] * 4,
-        (
-            shape((quads, capacity, lane_count), F32),
-            shape((quads, capacity, lane_count), F32),
-            column,
-            shape((groups, 1, lane_count), F32),
-        ),
-        jnp.stack([group, shard]),
+        [SMEM] + [VMEM] * 3,
+        (held, held, column, column),
+        shard[None],
         expert_rows.reshape(groups, parts, SLOTS, lane_count),
         w_down[0],
         same,
+        limit=LARGE,
+    )
+    terms = call(
+        terms_kernel,
+        [SMEM] * 2 + [VMEM] * 3,
+        shape((groups, 1, lane_count), F32),
+        group[None],
+        shard[None],
+        give,
         other,
+        base,
         limit=LARGE,
     )
 

time: 116 us -> 115 us (level)
  starting transfers between devices: 65.7 us -> 60.6 us
  waiting for transfers between devices: 19.5 us -> 23.7 us
    all_to_all x1, waiting for transfers between devices: 2.35 us -> 12.4 us  [shards(): expert_rows = lax.all_to_all(send, ('group', 'xc'), 0, 0, tiled=True)]
    ppermute x1, waiting for transfers between devices: 7.88 us -> 0.01 us  [shards(): other = lax.ppermute(same, 'y', [(i, i ^ 1) for i in range(shard_count)])]
    all_to_all x1, starting transfers between devices: 11.3 us -> 6.26 us  [shards(): home = lax.all_to_all(terms, 'group', 0, 0, tiled=True)]
    ppermute x1, waiting for transfers between devices: 0.01 us -> 2.06 us  [shards(): got = lax.ppermute(give, 'y', [(i, i ^ 1) for i in range(shard_count)])]
    all_to_all x1, starting transfers between devices: 11.3 us -> 9.87 us  [shards(): every_term = lax.all_to_all(spread, ('y', 'xc'), 0, 0, tiled=True)]
    ppermute x3, starting transfers between devices: 13.5 us -> 14.8 us  [shards(): lax.ppermute(sums[d], 'y', [(i, (i + 2 * d) % shard_count) for i in range...]
  transfers between devices with their start and end apart: 8 -> 8, of which waited for: 3 -> 3; matrix products, arithmetic and copies ran while one was open for 2% -> 1% of each run, Pallas kernels for 3% -> 6%
where the time goes in v7:
time: 115 us
  starting transfers between devices  60.6 us (53%)
  waiting for transfers between devices  23.7 us (21%)
  blocking collectives  16.2 us (14%)
  Pallas kernels  10.4 us (9%)
  local copies, waits for them, and re-layouts  1.62 us (1%)
  other arithmetic  1.17 us (1%)
    all_to_all x1, starting transfers between devices, shards(): expert_rows = lax.all_to_all(send, ('group', 'xc'), 0, 0, tiled=True)  24.1 us
    all_gather x1, blocking collectives, shards(): lax.all_gather(hidden, 'y', axis_index_groups=[list(range(p, shard_count,...  16.2 us
    ppermute x3, starting transfers between devices, shards(): lax.ppermute(sums[d], 'y', [(i, (i + 2 * d) % shard_count) for i in range...  14.8 us
    all_to_all x1, waiting for transfers between devices, shards(): expert_rows = lax.all_to_all(send, ('group', 'xc'), 0, 0, tiled=True)  12.4 us
    pallas_call x6, Pallas kernels, call(): pl.pallas_call(kernel, in_specs=specs, out_specs=jax.tree.map(lambda _: V...  10.4 us
    all_to_all x1, starting transfers between devices, shards(): every_term = lax.all_to_all(spread, ('y', 'xc'), 0, 0, tiled=True)  9.87 us
    all_to_all x1, waiting for transfers between devices, shards(): every_term = lax.all_to_all(spread, ('y', 'xc'), 0, 0, tiled=True)  9.3 us
    all_to_all x1, starting transfers between devices, shards(): home = lax.all_to_all(terms, 'group', 0, 0, tiled=True)  6.26 us
  transfers between devices with their start and end apart: 8, of which 3 were waited for; matrix products, arithmetic and copies ran while one was open for 1% of the time, Pallas kernels for 6%

profile of v7, /device:TPU:1, one launch (start us, length us, event | category | flops | bytes accessed | tf_op | source)
XLA Modules:
  0.0 114.5 jit_solution(10084845055692201417)
XLA Ops:
  0.6 2.6 %shard_map.94 = (bf16[128,16,128]{2,1,0:T(8,128)(2,1)}, f32[256,128]{1,0:T(8,128)}) custom-call(bf16[112,128]{1,0:T(8,128)(2,1)} %bitcast.36, s32[8,128]{1,0:T(8,128)} %bitcast.28, s32[8,128]{1,0:T(8,128)} %bitcast.30, bf16[8,128]{1,0:T(8,128)(2,1)} %bitcast.38, bf16[256,128]{1,0:T(8,128)(2,1)} %bitcast.23, bf16[256,128]{1,0:T(8,128)(2,1)} %bitcast.25), custom_call_target="tpu_custom_call" | custom-call | tf_op jit(solution)/shard_map/pallas_call | solution.py:148
  3.2 24.1 %all-to-all-start = ((bf16[128,16,128]{2,1,0:T(8,128)(2,1)}), bf16[128,16,128]{2,1,0:T(8,128)(2,1)S(1)}, u32[]{:S(2)}, u32[]{:S(2)}) async-start(bf16[128,16,128]{2,1,0:T(8,128)(2,1)} %get-tuple-element.14), calls=%async_computation | async-start | bytes 1048576 | tf_op jit(solution)/shard_map/all_to_all | solution.py:177
  27.3 16.2 %all-gather = f32[1024,128]{1,0:T(8,128)S(1)} all-gather(f32[256,128]{1,0:T(8,128)} %get-tuple-element.15), channel_id=2, replica_groups={{0,16,32,48},{8,24,40,56},{1,17,33,49},{9,25,41,57},{2,18,34,50},{10,26..., dimensions={0}, use_global_device_ids=true | all-gather | bytes 655360 | tf_op jit(solution)/shard_map/all_gather | solution.py:179
  43.5 2.3 %collective-permute-start = (f32[4,256,128]{2,1,0:T(8,128)S(1)}, f32[4,256,128]{2,1,0:T(8,128)S(1)}, u32[]{:S(2)}, u32[]{:S(2)}) collective-permute-start(f32[4,256,128]{2,1,0:T(8,128)S(1)} %bitcast.32), channel_id=1, source_target_pairs={{0,8},{8,0},{16,24},{24,16},{32,40},{40,32},{48,56},{56,48},{1,9},... | collective-permute-start | bytes 1572872 | tf_op jit(solution)/shard_map/ppermute | solution.py:183
  45.7 12.4 %all-to-all-done = bf16[128,16,128]{2,1,0:T(8,128)(2,1)S(1)} async-done(((bf16[128,16,128]{2,1,0:T(8,128)(2,1)}), bf16[128,16,128]{2,1,0:T(8,128)(2,1)S(1)}, u32[]{:S(2)}, u32[]{:S(2)}) %all-to-all-start) | async-done | bytes 524320 | tf_op jit(solution)/shard_map/all_to_all | solution.py:177
  58.1 0.0 copy-done.5
  58.1 0.8 copy-done.6
  58.9 3.6 %shard_map.95 = (f32[4,256,128]{2,1,0:T(8,128)}, f32[4,256,128]{2,1,0:T(8,128)}, f32[256,128]{1,0:T(8,128)}, f32[256,128]{1,0:T(8,128)}) custom-call(s32[1]{0:T(128)} %bitcast.1.shard_ref, bf16[16,8,16,128]{3,2,1,0:T(8,128)(2,1)} %bitcast.34, bf16[1024,896]{1,0:T(8,128)(2,1)} %bitcast.35, f32[4,256,128]{2,1,0:T(8,128)} %bitcast.33), custom_call_target="tpu_custom_call" | custom-call | tf_op jit(solution)/shard_map/pallas_call | solution.py:148
  62.5 3.3 %collective-permute-start.1 = (f32[4,256,128]{2,1,0:T(8,128)}, f32[4,256,128]{2,1,0:T(8,128)S(1)}, u32[]{:S(2)}, u32[]{:S(2)}) collective-permute-start(f32[4,256,128]{2,1,0:T(8,128)} %get-tuple-element.16.give_ref), channel_id=1, source_target_pairs={{0,8},{8,0},{16,24},{24,16},{32,40},{40,32},{48,56},{56,48},{1,9},... | collective-permute-start | bytes 1572872 | tf_op jit(solution)/shard_map/ppermute | solution.py:207
  65.9 0.0 collective-permute-done.other_ref
  65.9 0.0 copy-start.7
  65.9 0.8 copy-done.7
  66.7 2.0 %shard_map.96 = f32[16,1,128]{2,1,0:T(1,128)} custom-call(s32[1]{0:T(128)} %bitcast.group_ref, s32[1]{0:T(128)} %bitcast.1.shard_ref, f32[4,256,128]{2,1,0:T(8,128)} %get-tuple-element.16.give_ref, f32[4,256,128]{2,1,0:T(8,128)} %copy-done.7, f32[256,128]{1,0:T(8,128)} %get-tuple-element.17.base_ref), custom_call_target="tpu_custom_call" | custom-call | tf_op jit(solution)/shard_map/pallas_call | solution.py:148
  68.7 6.3 %all-to-all-start.1 = ((f32[16,1,128]{2,1,0:T(1,128)}), f32[16,1,128]{2,1,0:T(1,128)S(1)}, u32[]{:S(2)}, u32[]{:S(2)}) async-start(f32[16,1,128]{2,1,0:T(1,128)} %shard_map.96), calls=%async_computation.1 | async-start | bytes 16384 | tf_op jit(solution)/shard_map/all_to_all | solution.py:208
  74.9 2.1 %collective-permute-done.1 = f32[4,256,128]{2,1,0:T(8,128)S(1)} collective-permute-done((f32[4,256,128]{2,1,0:T(8,128)}, f32[4,256,128]{2,1,0:T(8,128)S(1)}, u32[]{:S(2)}, u32[]{:S(2)}) %collective-permute-start.1) | collective-permute-done | bytes 524320 | tf_op jit(solution)/shard_map/ppermute | solution.py:207
  77.0 1.2 %fusion = (f32[256,128]{1,0:T(8,128)S(1)}, f32[256,128]{1,0:T(8,128)S(1)}, f32[256,128]{1,0:T(8,128)S(1)}, f32[256,128]{1,0:T(8,128)S(1)}) fusion(f32[4,256,128]{2,1,0:T(8,128)S(1)} %collective-permute-done.1, f32[4,256,128]{2,1,0:T(8,128)} %get-tuple-element.18), kind=kLoop, calls=%fused_computation.1 | loop fusion | flops 131072 | bytes 1572864 | tf_op jit(solution)/shard_map/add | solution.py:209
  78.2 4.2 %collective-permute-start.2 = (f32[256,128]{1,0:T(8,128)S(1)}, f32[256,128]{1,0:T(8,128)S(1)}, u32[]{:S(2)}, u32[]{:S(2)}) collective-permute-start(f32[256,128]{1,0:T(8,128)S(1)} %get-tuple-element.27), channel_id=1, source_target_pairs={{0,16},{8,24},{16,32},{24,40},{32,48},{40,56},{48,0},{56,8},{1,17}... | collective-permute-start | bytes 393224 | tf_op jit(solution)/shard_map/ppermute | solution.py:211
  82.4 5.7 %collective-permute-start.3 = (f32[256,128]{1,0:T(8,128)S(1)}, f32[256,128]{1,0:T(8,128)S(1)}, u32[]{:S(2)}, u32[]{:S(2)}) collective-permute-start(f32[256,128]{1,0:T(8,128)S(1)} %get-tuple-element.26), channel_id=1, source_target_pairs={{0,32},{8,40},{16,48},{24,56},{32,0},{40,8},{48,16},{56,24},{1,33}... | collective-permute-start | bytes 393224 | tf_op jit(solution)/shard_map/ppermute | solution.py:211
  88.0 5.0 %collective-permute-start.4 = (f32[256,128]{1,0:T(8,128)S(1)}, f32[256,128]{1,0:T(8,128)S(1)}, u32[]{:S(2)}, u32[]{:S(2)}) collective-permute-start(f32[256,128]{1,0:T(8,128)S(1)} %get-tuple-element.25), channel_id=1, source_target_pairs={{0,48},{8,56},{16,0},{24,8},{32,16},{40,24},{48,32},{56,40},{1,49}... | collective-permute-start | bytes 393224 | tf_op jit(solution)/shard_map/ppermute | solution.py:211
  93.0 0.0 all-to-all-done.1.home_ref
  93.0 0.7 shard_map.97
  93.7 9.9 %all-to-all-start.2 = ((f32[64,2,128]{2,1,0:T(2,128)}), f32[64,2,128]{2,1,0:T(2,128)S(1)}, u32[]{:S(2)}, u32[]{:S(2)}) async-start(f32[64,2,128]{2,1,0:T(2,128)} %shard_map.97), calls=%async_computation.2 | async-start | bytes 131072 | tf_op jit(solution)/shard_map/all_to_all | solution.py:217
  103.6 0.0 collective-permute-done.2.h1
  103.6 0.0 collective-permute-done.3.h2
  103.6 0.0 collective-permute-done.4.h3
  103.6 0.0 copy-done
  103.6 0.0 copy-done.1
  103.6 0.0 copy-done.2
  103.6 0.7 shard_map.98
  104.4 9.3 %all-to-all-done.2 = f32[64,2,128]{2,1,0:T(2,128)S(1)} async-done(((f32[64,2,128]{2,1,0:T(2,128)}), f32[64,2,128]{2,1,0:T(2,128)S(1)}, u32[]{:S(2)}, u32[]{:S(2)}) %all-to-all-start.2) | async-done | bytes 65568 | tf_op jit(solution)/shard_map/all_to_all | solution.py:217
  113.7 0.0 copy-done.3
  113.7 0.8 shard_map.99
  (8 shorter events, 0.0 us)
Async XLA Ops:
  3.2 54.9 %all-to-all-start = ((bf16[128,16,128]{2,1,0:T(8,128)(2,1)}), bf16[128,16,128]{2,1,0:T(8,128)(2,1)S(1)}, u32[]{:S(2)}, u32[]{:S(2)}) async-start(bf16[128,16,128]{2,1,0:T(8,128)(2,1)} %get-tuple-element.14), calls=%async_computation | async-start | bytes 1048576 | tf_op jit(solution)/shard_map/all_to_all | solution.py:177
  43.5 14.6 %copy-start.5 = (f32[1024,128]{1,0:T(8,128)}, f32[1024,128]{1,0:T(8,128)S(1)}, u32[]{:S(2)}) copy-start(f32[1024,128]{1,0:T(8,128)S(1)} %all-gather) | copy-start | bytes 1572868
  43.5 22.4 %collective-permute-start = (f32[4,256,128]{2,1,0:T(8,128)S(1)}, f32[4,256,128]{2,1,0:T(8,128)S(1)}, u32[]{:S(2)}, u32[]{:S(2)}) collective-permute-start(f32[4,256,128]{2,1,0:T(8,128)S(1)} %bitcast.32), channel_id=1, source_target_pairs={{0,8},{8,0},{16,24},{24,16},{32,40},{40,32},{48,56},{56,48},{1,9},... | collective-permute-start | bytes 1572872 | tf_op jit(solution)/shard_map/ppermute | solution.py:183
  58.1 0.8 copy-start.6
  62.5 41.1 %copy-start = (bf16[1,256,128]{2,1,0:T(8,128)(2,1)S(1)}, bf16[1,256,128]{2,1,0:T(8,128)(2,1)}, u32[]{:S(2)}) copy-start(bf16[1,256,128]{2,1,0:T(8,128)(2,1)} %param.12) | copy-start | bytes 196612
  62.5 41.1 %copy-start.1 = (bf16[1,256,128]{2,1,0:T(8,128)(2,1)S(1)}, bf16[1,256,128]{2,1,0:T(8,128)(2,1)}, u32[]{:S(2)}) copy-start(bf16[1,256,128]{2,1,0:T(8,128)(2,1)} %param.13) | copy-start | bytes 196612
  62.5 41.1 %copy-start.2 = (f32[256,128]{1,0:T(8,128)S(1)}, f32[256,128]{1,0:T(8,128)}, u32[]{:S(2)}) copy-start(f32[256,128]{1,0:T(8,128)} %get-tuple-element.19.gate_ref) | copy-start | bytes 393220
  62.5 14.5 %collective-permute-start.1 = (f32[4,256,128]{2,1,0:T(8,128)}, f32[4,256,128]{2,1,0:T(8,128)S(1)}, u32[]{:S(2)}, u32[]{:S(2)}) collective-permute-start(f32[4,256,128]{2,1,0:T(8,128)} %get-tuple-element.16.give_ref), channel_id=1, source_target_pairs={{0,8},{8,0},{16,24},{24,16},{32,40},{40,32},{48,56},{56,48},{1,9},... | collective-permute-start | bytes 1572872 | tf_op jit(solution)/shard_map/ppermute | solution.py:207
  65.9 0.8 copy-start.7
  66.7 47.0 %copy-start.3 = (s32[128,8]{0,1:T(8,128)S(1)}, s32[128,8]{0,1:T(8,128)}, u32[]{:S(2)}) copy-start(s32[128,8]{0,1:T(8,128)} %param.8) | copy-start | bytes 12292
  66.7 47.0 %copy-start.4 = (s32[128,8]{0,1:T(8,128)S(1)}, s32[128,8]{0,1:T(8,128)}, u32[]{:S(2)}) copy-start(s32[128,8]{0,1:T(8,128)} %param.9) | copy-start | bytes 12292
  68.7 24.4 %all-to-all-start.1 = ((f32[16,1,128]{2,1,0:T(1,128)}), f32[16,1,128]{2,1,0:T(1,128)S(1)}, u32[]{:S(2)}, u32[]{:S(2)}) async-start(f32[16,1,128]{2,1,0:T(1,128)} %shard_map.96), calls=%async_computation.1 | async-start | bytes 16384 | tf_op jit(solution)/shard_map/all_to_all | solution.py:208
  78.2 25.4 %collective-permute-start.2 = (f32[256,128]{1,0:T(8,128)S(1)}, f32[256,128]{1,0:T(8,128)S(1)}, u32[]{:S(2)}, u32[]{:S(2)}) collective-permute-start(f32[256,128]{1,0:T(8,128)S(1)} %get-tuple-element.27), channel_id=1, source_target_pairs={{0,16},{8,24},{16,32},{24,40},{32,48},{40,56},{48,0},{56,8},{1,17}... | collective-permute-start | bytes 393224 | tf_op jit(solution)/shard_map/ppermute | solution.py:211
  82.4 21.2 %collective-permute-start.3 = (f32[256,128]{1,0:T(8,128)S(1)}, f32[256,128]{1,0:T(8,128)S(1)}, u32[]{:S(2)}, u32[]{:S(2)}) collective-permute-start(f32[256,128]{1,0:T(8,128)S(1)} %get-tuple-element.26), channel_id=1, source_target_pairs={{0,32},{8,40},{16,48},{24,56},{32,0},{40,8},{48,16},{56,24},{1,33}... | collective-permute-start | bytes 393224 | tf_op jit(solution)/shard_map/ppermute | solution.py:211
  88.0 15.6 %collective-permute-start.4 = (f32[256,128]{1,0:T(8,128)S(1)}, f32[256,128]{1,0:T(8,128)S(1)}, u32[]{:S(2)}, u32[]{:S(2)}) collective-permute-start(f32[256,128]{1,0:T(8,128)S(1)} %get-tuple-element.25), channel_id=1, source_target_pairs={{0,48},{8,56},{16,0},{24,8},{32,16},{40,24},{48,32},{56,40},{1,49}... | collective-permute-start | bytes 393224 | tf_op jit(solution)/shard_map/ppermute | solution.py:211
  93.7 20.0 %all-to-all-start.2 = ((f32[64,2,128]{2,1,0:T(2,128)}), f32[64,2,128]{2,1,0:T(2,128)S(1)}, u32[]{:S(2)}, u32[]{:S(2)}) async-start(f32[64,2,128]{2,1,0:T(2,128)} %shard_map.97), calls=%async_computation.2 | async-start | bytes 131072 | tf_op jit(solution)/shard_map/all_to_all | solution.py:217

commit v8 on v7

--- a/solution.py
+++ b/solution.py
@@ -48,26 +48,41 @@
     hidden_ref[...] = gate_pre * jax.nn.sigmoid(gate_pre) * up_pre_ref[...].astype(F32)
 
 
-def matmul_kernel(shard_ref, rows_ref, w_ref, same_ref, give_ref, keep_ref, gate_ref, base_ref):
+def matmul_kernel(
+    shard_ref, rows_ref, w_ref, same_ref, right_ref, left_ref, keep_ref, gate_ref, base_ref
+):
     groups, parts, _, lane_count = rows_ref.shape
     capacity = groups * SLOTS
     col_width = w_ref.shape[1] // parts
-    own, quad = shard_ref[0] % 2, shard_ref[0] // 2
-    quads = give_ref.shape[0]
+    count = w_ref.shape[0] // lane_count
+    shard = shard_ref[0]
+    half = capacity // 2
+    low, high = slice(0, half), slice(half, capacity)
+    every, near = slice(0, capacity), slice(capacity, 2 * capacity)
+    last, spare = slice(2 * capacity, 3 * capacity), slice(2 * capacity, 2 * capacity + half)
+    pairs = (
+        ((1, ((every, right_ref, every),)), (count - 1, ((every, left_ref, every),))),
+        ((count - 2, ((every, right_ref, near),)), (2, ((every, left_ref, near),))),
+        (
+            (4, ((high, right_ref, spare), (low, left_ref, spare))),
+            (0, ((every, keep_ref, every),)),
+        ),
+        ((count - 3, ((every, keep_ref, near),)), (3, ((every, keep_ref, last),))),
+    )
     blocks = [rows_ref[:, e].reshape(capacity, lane_count) for e in range(parts)]
     x = jnp.concatenate([b[:, :col_width] for b in blocks], axis=1)
     terms = jnp.zeros((capacity, lane_count), F32)
-    for d in range(quads):
-        target = (quad + d) % quads
-        firsts = [
-            pl.multiple_of((target * 2 + parity) * lane_count, lane_count)
-            for parity in (1 - own, own)
-        ]
+    for pair in pairs:
+        units = [(shard + offset) % count for offset, _ in pair]
+        firsts = [pl.multiple_of(unit * lane_count, lane_count) for unit in units]
         w = jnp.concatenate([w_ref[pl.ds(first, lane_count), :] for first in firsts], axis=0)
         both = lax.dot_general(x, w, NT, preferred_element_type=F32)
-        give_ref[d] = both[:, :lane_count]
-        keep_ref[d] = both[:, lane_count:]
-        terms += both[:, lane_count:] * same_ref[target]
+        for i, (offset, targets) in enumerate(pair):
+            part = both[:, i * lane_count : (i + 1) * lane_count]
+            for span, target_ref, to in targets:
+                target_ref[to] = part[span]
+            if offset % 2 == 0:
+                terms += part * same_ref[units[i] // 2]
     base_ref[...] = terms
     gate = jnp.where(lanes((capacity, lane_count)) == col_width, blocks[0].astype(F32), 0.0)
     gate_ref[...] = jnp.broadcast_to(
@@ -75,13 +90,22 @@
     )
 
 
-def terms_kernel(group_ref, shard_ref, give_ref, other_ref, base_ref, term_ref):
-    quads, capacity, lane_count = give_ref.shape
+def terms_kernel(
+    group_ref, shard_ref, right_ref, left_ref, keep_ref, other_ref, base_ref, term_ref
+):
+    capacity, lane_count = base_ref.shape
     groups = term_ref.shape[0]
-    group, quad = group_ref[0], shard_ref[0] // 2
+    count = 2 * other_ref.shape[0]
+    group, shard = group_ref[0], shard_ref[0]
     terms = base_ref[...]
-    for d in range(quads):
-        terms += give_ref[d] * other_ref[(quad + d) % quads]
+    for offset, part_ref, first in (
+        (1, right_ref, 0),
+        (count - 1, left_ref, 0),
+        (count - 3, keep_ref, capacity),
+        (3, keep_ref, 2 * capacity),
+    ):
+        unit = (shard + offset) % count
+        terms += part_ref[first : first + capacity] * other_ref[unit // 2]
     total = jnp.sum(terms, axis=1, keepdims=True)
     row_ids, lane_ids = rows((capacity, lane_count)), lanes((capacity, lane_count))
     hit = lane_ids == group % (lane_count // SLOTS) * SLOTS + row_ids % SLOTS
@@ -90,6 +114,17 @@
     )
 
 
+def middle_kernel(left_ref, right_ref, keep_ref, own_ref, down_ref, up_ref):
+    capacity = down_ref.shape[0]
+    half = capacity // 2
+    near = slice(capacity, 2 * capacity)
+    own_ref[...] = keep_ref[:capacity] + left_ref[:capacity] + right_ref[:capacity]
+    down_ref[...] = keep_ref[near] + left_ref[near]
+    down_ref[:half] += right_ref[2 * capacity :]
+    up_ref[...] = keep_ref[2 * capacity :] + right_ref[near]
+    up_ref[half:] += left_ref[2 * capacity :]
+
+
 def spread_kernel(home_ref, out_ref):
     groups, _, lane_count = home_ref.shape
     half = groups // 2
@@ -97,8 +132,9 @@
     out_ref[...] = jnp.broadcast_to(home[None], out_ref.shape)
 
 
-def output_kernel(h0, h1, h2, h3, gate_ref, gate_pre_ref, up_pre_ref, grad_gate_ref, grad_up_ref):
-    hidden_grad = h0[...] + h1[...] + h2[...] + h3[...]
+def output_kernel(own_ref, down_ref, up_ref, gate_ref, gate_pre_ref, up_pre_ref, *outs):
+    grad_gate_ref, grad_up_ref = outs
+    hidden_grad = own_ref[...] + down_ref[...] + up_ref[...]
     gate_pre = gate_pre_ref[...].astype(F32)
     up_pre = up_pre_ref[...].astype(F32)
     sigmoid_gate = jax.nn.sigmoid(gate_pre)
@@ -181,11 +217,11 @@
     )
     quads = shard_count // 2
     other = lax.ppermute(same, "y", [(i, i ^ 1) for i in range(shard_count)])
-    held = shape((quads, capacity, lane_count), F32)
-    give, keep, gate_rows, base = call(
+    send_shape = shape((2 * capacity + capacity // 2, lane_count), F32)
+    right, left, keep, gate_rows, base = call(
         matmul_kernel,
         [SMEM] + [VMEM] * 3,
-        (held, held, column, column),
+        (send_shape, send_shape, shape((3 * capacity, lane_count), F32), column, column),
         shard[None],
         expert_rows.reshape(groups, parts, SLOTS, lane_count),
         w_down[0],
@@ -194,30 +230,44 @@
     )
     terms = call(
         terms_kernel,
-        [SMEM] * 2 + [VMEM] * 3,
+        [SMEM] * 2 + [VMEM] * 5,
         shape((groups, 1, lane_count), F32),
         group[None],
         shard[None],
-        give,
+        right,
+        left,
+        keep,
         other,
         base,
         limit=LARGE,
     )
 
-    got = lax.ppermute(give, "y", [(i, i ^ 1) for i in range(shard_count)])
+    def moved(array, by):
+        return lax.ppermute(
+            array, "y", [(i, (i + by) % shard_count) for i in range(shard_count)]
+        )
+
+    from_left, from_right = moved(right, 1), moved(left, -1)
     home = lax.all_to_all(terms, "group", 0, 0, tiled=True)
-    sums = [keep[d] + got[d] for d in range(quads)]
-    for d in (2, 1, 3):
-        sums[d] = lax.ppermute(
-            sums[d], "y", [(i, (i + 2 * d) % shard_count) for i in range(shard_count)]
-        )
+    own, down, up = call(
+        middle_kernel, [VMEM] * 3, (column,) * 3, from_left, from_right, keep
+    )
+    from_above, from_below = moved(down, -3), moved(up, 3)
     spread = call(
         spread_kernel, [VMEM], shape((shard_count * parts, 2, lane_count), F32), home
     )
     every_term = lax.all_to_all(spread, ("y", "xc"), 0, 0, tiled=True)
     out = shape((capacity, lane_count), BF16)
     grad_gate, grad_up = call(
-        output_kernel, [VMEM] * 7, (out, out), *sums, gate_rows, saved_gate[0], saved_up[0]
+        output_kernel,
+        [VMEM] * 6,
+        (out, out),
+        own,
+        from_above,
+        from_below,
+        gate_rows,
+        saved_gate[0],
+        saved_up[0],
     )
     every_term, grad_gate, grad_up = lax.optimization_barrier((every_term, grad_gate, grad_up))
     grad_gates = call(

time: 115 us -> 113 us (0.983)
  starting transfers between devices: 60.6 us -> 57.6 us
  waiting for transfers between devices: 23.7 us -> 25.7 us
  other arithmetic: 1.17 us -> 0 us
    all_to_all x1, waiting for transfers between devices: 0.01 us -> 4.03 us  [shards(): home = lax.all_to_all(terms, 'group', 0, 0, tiled=True)]
    ppermute x4, starting transfers between devices: 18.2 us -> 14.2 us  [moved(): lax.ppermute(array, 'y', [(i, (i + by) % shard_count) for i in range(shar...]
    ppermute x4, waiting for transfers between devices: 2.07 us -> 0.01 us  [moved(): lax.ppermute(array, 'y', [(i, (i + by) % shard_count) for i in range(shar...]
    add x1 -> x0, other arithmetic: 1.17 us -> none  [shards(): sums = [keep[d] + got[d] for d in range(quads)]]
    pallas_call x6 -> x7, Pallas kernels: 10.4 us -> 10.5 us  [call(): pl.pallas_call(kernel, in_specs=specs, out_specs=jax.tree.map(lambda _: V...]
  transfers between devices with their start and end apart: 8 -> 8, of which waited for: 3 -> 3; matrix products, arithmetic and copies ran while one was open for 1% -> 0% of each run, Pallas kernels for 6% -> 6%
where the time goes in v8:
time: 113 us; the launch traced here: 112 us
  starting transfers between devices  57.6 us (51%)
  waiting for transfers between devices  25.7 us (23%)
  blocking collectives  16.2 us (14%)
  Pallas kernels  10.5 us (9%)
  local copies, waits for them, and re-layouts  1.62 us (1%)
    all_to_all x1, starting transfers between devices, shards(): expert_rows = lax.all_to_all(send, ('group', 'xc'), 0, 0, tiled=True)  24.1 us
    all_gather x1, blocking collectives, shards(): lax.all_gather(hidden, 'y', axis_index_groups=[list(range(p, shard_count,...  16.2 us
    ppermute x4, starting transfers between devices, moved(): lax.ppermute(array, 'y', [(i, (i + by) % shard_count) for i in range(shar...  14.2 us
    all_to_all x1, waiting for transfers between devices, shards(): expert_rows = lax.all_to_all(send, ('group', 'xc'), 0, 0, tiled=True)  12.4 us
    all_to_all x1, starting transfers between devices, shards(): every_term = lax.all_to_all(spread, ('y', 'xc'), 0, 0, tiled=True)  10.8 us
    pallas_call x7, Pallas kernels, call(): pl.pallas_call(kernel, in_specs=specs, out_specs=jax.tree.map(lambda _: V...  10.5 us
    all_to_all x1, waiting for transfers between devices, shards(): every_term = lax.all_to_all(spread, ('y', 'xc'), 0, 0, tiled=True)  9.32 us
    all_to_all x1, starting transfers between devices, shards(): home = lax.all_to_all(terms, 'group', 0, 0, tiled=True)  6.27 us
  transfers between devices with their start and end apart: 8, of which 3 were waited for; matrix products, arithmetic and copies ran while one was open for 0% of the time, Pallas kernels for 6%

profile of v8, /device:TPU:1, one launch (start us, length us, event | category | flops | bytes accessed | tf_op | source)
XLA Modules:
  0.0 112.4 jit_solution(833641993150451773)
XLA Ops:
  0.6 2.6 %shard_map.94 = (bf16[128,16,128]{2,1,0:T(8,128)(2,1)}, f32[256,128]{1,0:T(8,128)}) custom-call(bf16[112,128]{1,0:T(8,128)(2,1)} %bitcast.28, s32[8,128]{1,0:T(8,128)} %bitcast.20, s32[8,128]{1,0:T(8,128)} %bitcast.22, bf16[8,128]{1,0:T(8,128)(2,1)} %bitcast.30, bf16[256,128]{1,0:T(8,128)(2,1)} %bitcast.15, bf16[256,128]{1,0:T(8,128)(2,1)} %bitcast.17), custom_call_target="tpu_custom_call" | custom-call | tf_op jit(solution)/shard_map/pallas_call | solution.py:184
  3.2 24.1 %all-to-all-start = ((bf16[128,16,128]{2,1,0:T(8,128)(2,1)}), bf16[128,16,128]{2,1,0:T(8,128)(2,1)S(1)}, u32[]{:S(2)}, u32[]{:S(2)}) async-start(bf16[128,16,128]{2,1,0:T(8,128)(2,1)} %get-tuple-element.18), calls=%async_computation | async-start | bytes 1048576 | tf_op jit(solution)/shard_map/all_to_all | solution.py:213
  27.3 16.2 %all-gather = f32[1024,128]{1,0:T(8,128)S(1)} all-gather(f32[256,128]{1,0:T(8,128)} %get-tuple-element.19), channel_id=2, replica_groups={{0,16,32,48},{8,24,40,56},{1,17,33,49},{9,25,41,57},{2,18,34,50},{10,26..., dimensions={0}, use_global_device_ids=true | all-gather | bytes 655360 | tf_op jit(solution)/shard_map/all_gather | solution.py:215
  43.4 2.3 %collective-permute-start = (f32[4,256,128]{2,1,0:T(8,128)S(1)}, f32[4,256,128]{2,1,0:T(8,128)S(1)}, u32[]{:S(2)}, u32[]{:S(2)}) collective-permute-start(f32[4,256,128]{2,1,0:T(8,128)S(1)} %bitcast.24), channel_id=1, source_target_pairs={{0,8},{8,0},{16,24},{24,16},{32,40},{40,32},{48,56},{56,48},{1,9},... | collective-permute-start | bytes 1572872 | tf_op jit(solution)/shard_map/ppermute | solution.py:219
  45.7 12.4 %all-to-all-done = bf16[128,16,128]{2,1,0:T(8,128)(2,1)S(1)} async-done(((bf16[128,16,128]{2,1,0:T(8,128)(2,1)}), bf16[128,16,128]{2,1,0:T(8,128)(2,1)S(1)}, u32[]{:S(2)}, u32[]{:S(2)}) %all-to-all-start) | async-done | bytes 524320 | tf_op jit(solution)/shard_map/all_to_all | solution.py:213
  58.1 0.0 copy-done.6
  58.1 0.8 copy-done.7
  58.9 3.5 %shard_map.95 = (f32[640,128]{1,0:T(8,128)}, f32[640,128]{1,0:T(8,128)}, f32[768,128]{1,0:T(8,128)}, f32[256,128]{1,0:T(8,128)}, f32[256,128]{1,0:T(8,128)}) custom-call(s32[1]{0:T(128)} %bitcast.1.shard_ref, bf16[16,8,16,128]{3,2,1,0:T(8,128)(2,1)} %bitcast.26, bf16[1024,896]{1,0:T(8,128)(2,1)} %bitcast.27, f32[4,256,128]{2,1,0:T(8,128)} %bitcast.25), custom_call_target="tpu_custom_call" | custom-call | tf_op jit(solution)/shard_map/pallas_call | solution.py:184
  62.4 0.0 copy-start.3
  62.4 0.0 copy-start.4
  62.4 0.0 copy-start.5
  62.5 3.3 %collective-permute-start.1 = (f32[640,128]{1,0:T(8,128)}, f32[640,128]{1,0:T(8,128)S(1)}, u32[]{:S(2)}, u32[]{:S(2)}) collective-permute-start(f32[640,128]{1,0:T(8,128)} %get-tuple-element.20.right_ref), channel_id=1, source_target_pairs={{0,8},{8,16},{16,24},{24,32},{32,40},{40,48},{48,56},{56,0},{1,9},... | collective-permute-start | bytes 983048 | tf_op jit(solution)/shard_map/ppermute | solution.py:246
  65.8 3.8 %collective-permute-start.2 = (f32[640,128]{1,0:T(8,128)}, f32[640,128]{1,0:T(8,128)S(1)}, u32[]{:S(2)}, u32[]{:S(2)}) collective-permute-start(f32[640,128]{1,0:T(8,128)} %get-tuple-element.21.left_ref), channel_id=1, source_target_pairs={{0,56},{8,0},{16,8},{24,16},{32,24},{40,32},{48,40},{56,48},{1,57}... | collective-permute-start | bytes 983048 | tf_op jit(solution)/shard_map/ppermute | solution.py:246
  69.6 0.0 collective-permute-done.other_ref
  69.6 0.0 copy-start.8
  69.6 0.8 copy-done.8
  70.4 2.1 %shard_map.96 = f32[16,1,128]{2,1,0:T(1,128)} custom-call(s32[1]{0:T(128)} %bitcast.group_ref, s32[1]{0:T(128)} %bitcast.1.shard_ref, f32[640,128]{1,0:T(8,128)} %get-tuple-element.20.right_ref, f32[640,128]{1,0:T(8,128)} %get-tuple-element.21.left_ref, f32[768,128]{1,0:T(8,128)} %get-tuple-element.22.keep_ref, f32[4,256,128]{2,1,0:T(8,128)} %copy-done.8, ...), custom_call_target="tpu_custom_call" | custom-call | tf_op jit(solution)/shard_map/pallas_call | solution.py:184
  72.6 6.3 %all-to-all-start.1 = ((f32[16,1,128]{2,1,0:T(1,128)}), f32[16,1,128]{2,1,0:T(1,128)S(1)}, u32[]{:S(2)}, u32[]{:S(2)}) async-start(f32[16,1,128]{2,1,0:T(1,128)} %shard_map.96), calls=%async_computation.1 | async-start | bytes 16384 | tf_op jit(solution)/shard_map/all_to_all | solution.py:251
  78.9 0.0 collective-permute-done.1.left_ref
  78.9 0.0 collective-permute-done.2.right_ref
  78.9 0.0 copy-done
  78.9 0.1 shard_map.98
  78.9 4.9 %collective-permute-start.3 = (f32[256,128]{1,0:T(8,128)S(1)}, f32[256,128]{1,0:T(8,128)S(1)}, u32[]{:S(2)}, u32[]{:S(2)}) collective-permute-start(f32[256,128]{1,0:T(8,128)S(1)} %get-tuple-element.25), channel_id=1, source_target_pairs={{0,40},{8,48},{16,56},{24,0},{32,8},{40,16},{48,24},{56,32},{1,41}... | collective-permute-start | bytes 393224 | tf_op jit(solution)/shard_map/ppermute | solution.py:246
  83.9 2.1 %collective-permute-start.4 = (f32[256,128]{1,0:T(8,128)S(1)}, f32[256,128]{1,0:T(8,128)S(1)}, u32[]{:S(2)}, u32[]{:S(2)}) collective-permute-start(f32[256,128]{1,0:T(8,128)S(1)} %get-tuple-element.26), channel_id=1, source_target_pairs={{0,24},{8,32},{16,40},{24,48},{32,56},{40,0},{48,8},{56,16},{1,25}... | collective-permute-start | bytes 393224 | tf_op jit(solution)/shard_map/ppermute | solution.py:246
  86.0 4.0 %all-to-all-done.1.home_ref = f32[16,1,128]{2,1,0:T(1,128)S(1)} async-done(((f32[16,1,128]{2,1,0:T(1,128)}), f32[16,1,128]{2,1,0:T(1,128)S(1)}, u32[]{:S(2)}, u32[]{:S(2)}) %all-to-all-start.1) | async-done | bytes 8224 | tf_op jit(solution)/shard_map/all_to_all | solution.py:251
  90.1 0.7 shard_map.97
  90.7 10.8 %all-to-all-start.2 = ((f32[64,2,128]{2,1,0:T(2,128)}), f32[64,2,128]{2,1,0:T(2,128)S(1)}, u32[]{:S(2)}, u32[]{:S(2)}) async-start(f32[64,2,128]{2,1,0:T(2,128)} %shard_map.97), calls=%async_computation.2 | async-start | bytes 131072 | tf_op jit(solution)/shard_map/all_to_all | solution.py:259
  101.5 0.0 collective-permute-done.3.down_ref
  101.5 0.0 collective-permute-done.4.up_ref
  101.5 0.7 shard_map.99
  102.3 9.3 %all-to-all-done.2 = f32[64,2,128]{2,1,0:T(2,128)S(1)} async-done(((f32[64,2,128]{2,1,0:T(2,128)}), f32[64,2,128]{2,1,0:T(2,128)S(1)}, u32[]{:S(2)}, u32[]{:S(2)}) %all-to-all-start.2) | async-done | bytes 65568 | tf_op jit(solution)/shard_map/all_to_all | solution.py:259
  111.6 0.8 shard_map.100
  (10 shorter events, 0.0 us)
Async XLA Ops:
  3.2 54.9 %all-to-all-start = ((bf16[128,16,128]{2,1,0:T(8,128)(2,1)}), bf16[128,16,128]{2,1,0:T(8,128)(2,1)S(1)}, u32[]{:S(2)}, u32[]{:S(2)}) async-start(bf16[128,16,128]{2,1,0:T(8,128)(2,1)} %get-tuple-element.18), calls=%async_computation | async-start | bytes 1048576 | tf_op jit(solution)/shard_map/all_to_all | solution.py:213
  43.4 14.6 %copy-start.6 = (f32[1024,128]{1,0:T(8,128)}, f32[1024,128]{1,0:T(8,128)S(1)}, u32[]{:S(2)}) copy-start(f32[1024,128]{1,0:T(8,128)S(1)} %all-gather) | copy-start | bytes 1572868
  43.4 26.2 %collective-permute-start = (f32[4,256,128]{2,1,0:T(8,128)S(1)}, f32[4,256,128]{2,1,0:T(8,128)S(1)}, u32[]{:S(2)}, u32[]{:S(2)}) collective-permute-start(f32[4,256,128]{2,1,0:T(8,128)S(1)} %bitcast.24), channel_id=1, source_target_pairs={{0,8},{8,0},{16,24},{24,16},{32,40},{40,32},{48,56},{56,48},{1,9},... | collective-permute-start | bytes 1572872 | tf_op jit(solution)/shard_map/ppermute | solution.py:219
  58.1 0.8 copy-start.7
  62.4 16.5 %copy-start = (f32[768,128]{1,0:T(8,128)S(1)}, f32[768,128]{1,0:T(8,128)}, u32[]{:S(2)}) copy-start(f32[768,128]{1,0:T(8,128)} %get-tuple-element.22.keep_ref) | copy-start | bytes 1179652
  62.4 39.1 %copy-start.1 = (bf16[1,256,128]{2,1,0:T(8,128)(2,1)S(1)}, bf16[1,256,128]{2,1,0:T(8,128)(2,1)}, u32[]{:S(2)}) copy-start(bf16[1,256,128]{2,1,0:T(8,128)(2,1)} %param.12) | copy-start | bytes 196612
  62.4 39.1 %copy-start.2 = (bf16[1,256,128]{2,1,0:T(8,128)(2,1)S(1)}, bf16[1,256,128]{2,1,0:T(8,128)(2,1)}, u32[]{:S(2)}) copy-start(bf16[1,256,128]{2,1,0:T(8,128)(2,1)} %param.13) | copy-start | bytes 196612
  62.4 39.1 %copy-start.3 = (f32[256,128]{1,0:T(8,128)S(1)}, f32[256,128]{1,0:T(8,128)}, u32[]{:S(2)}) copy-start(f32[256,128]{1,0:T(8,128)} %get-tuple-element.27.gate_ref) | copy-start | bytes 393220
  62.4 49.2 %copy-start.4 = (s32[128,8]{0,1:T(8,128)S(1)}, s32[128,8]{0,1:T(8,128)}, u32[]{:S(2)}) copy-start(s32[128,8]{0,1:T(8,128)} %param.8) | copy-start | bytes 12292
  62.4 49.1 %copy-start.5 = (s32[128,8]{0,1:T(8,128)S(1)}, s32[128,8]{0,1:T(8,128)}, u32[]{:S(2)}) copy-start(s32[128,8]{0,1:T(8,128)} %param.9) | copy-start | bytes 12292
  62.5 16.4 %collective-permute-start.1 = (f32[640,128]{1,0:T(8,128)}, f32[640,128]{1,0:T(8,128)S(1)}, u32[]{:S(2)}, u32[]{:S(2)}) collective-permute-start(f32[640,128]{1,0:T(8,128)} %get-tuple-element.20.right_ref), channel_id=1, source_target_pairs={{0,8},{8,16},{16,24},{24,32},{32,40},{40,48},{48,56},{56,0},{1,9},... | collective-permute-start | bytes 983048 | tf_op jit(solution)/shard_map/ppermute | solution.py:246
  65.8 13.1 %collective-permute-start.2 = (f32[640,128]{1,0:T(8,128)}, f32[640,128]{1,0:T(8,128)S(1)}, u32[]{:S(2)}, u32[]{:S(2)}) collective-permute-start(f32[640,128]{1,0:T(8,128)} %get-tuple-element.21.left_ref), channel_id=1, source_target_pairs={{0,56},{8,0},{16,8},{24,16},{32,24},{40,32},{48,40},{56,48},{1,57}... | collective-permute-start | bytes 983048 | tf_op jit(solution)/shard_map/ppermute | solution.py:246
  69.6 0.8 copy-start.8
  72.6 17.5 %all-to-all-start.1 = ((f32[16,1,128]{2,1,0:T(1,128)}), f32[16,1,128]{2,1,0:T(1,128)S(1)}, u32[]{:S(2)}, u32[]{:S(2)}) async-start(f32[16,1,128]{2,1,0:T(1,128)} %shard_map.96), calls=%async_computation.1 | async-start | bytes 16384 | tf_op jit(solution)/shard_map/all_to_all | solution.py:251
  78.9 22.5 %collective-permute-start.3 = (f32[256,128]{1,0:T(8,128)S(1)}, f32[256,128]{1,0:T(8,128)S(1)}, u32[]{:S(2)}, u32[]{:S(2)}) collective-permute-start(f32[256,128]{1,0:T(8,128)S(1)} %get-tuple-element.25), channel_id=1, source_target_pairs={{0,40},{8,48},{16,56},{24,0},{32,8},{40,16},{48,24},{56,32},{1,41}... | collective-permute-start | bytes 393224 | tf_op jit(solution)/shard_map/ppermute | solution.py:246
  83.9 17.6 %collective-permute-start.4 = (f32[256,128]{1,0:T(8,128)S(1)}, f32[256,128]{1,0:T(8,128)S(1)}, u32[]{:S(2)}, u32[]{:S(2)}) collective-permute-start(f32[256,128]{1,0:T(8,128)S(1)} %get-tuple-element.26), channel_id=1, source_target_pairs={{0,24},{8,32},{16,40},{24,48},{32,56},{40,0},{48,8},{56,16},{1,25}... | collective-permute-start | bytes 393224 | tf_op jit(solution)/shard_map/ppermute | solution.py:246
  90.7 20.8 %all-to-all-start.2 = ((f32[64,2,128]{2,1,0:T(2,128)}), f32[64,2,128]{2,1,0:T(2,128)S(1)}, u32[]{:S(2)}, u32[]{:S(2)}) async-start(f32[64,2,128]{2,1,0:T(2,128)} %shard_map.97), calls=%async_computation.2 | async-start | bytes 131072 | tf_op jit(solution)/shard_map/all_to_all | solution.py:259

commit v9 on v8

--- a/solution.py
+++ b/solution.py
@@ -226,7 +226,7 @@
         expert_rows.reshape(groups, parts, SLOTS, lane_count),
         w_down[0],
         same,
-        limit=LARGE,
+        limit=24 << 20,
     )
     terms = call(
         terms_kernel,
@@ -239,7 +239,7 @@
         keep,
         other,
         base,
-        limit=LARGE,
+        limit=24 << 20,
     )
 
     def moved(array, by):

time: 113 us -> 109 us (0.965)
  Pallas kernels: 10.5 us -> 8.54 us
  local copies, waits for them, and re-layouts: 1.62 us -> 0.02 us
    pallas_call x7, Pallas kernels: 10.5 us -> 8.54 us  [call(): pl.pallas_call(kernel, in_specs=specs, out_specs=jax.tree.map(lambda _: V...]
    unnamed x18 -> x10, local copies, waits for them, and re-layouts: 1.62 us -> 0.02 us
  transfers between devices with their start and end apart: 8 -> 8, of which waited for: 3 -> 3; matrix products, arithmetic and copies ran while one was open for 0% -> 0% of each run, Pallas kernels for 6% -> 5%
where the time goes in v9:
time: 109 us
  starting transfers between devices  57.8 us (53%)
  waiting for transfers between devices  25.6 us (23%)
  blocking collectives  16.2 us (15%)
  Pallas kernels  8.54 us (8%)
    all_to_all x1, starting transfers between devices, shards(): expert_rows = lax.all_to_all(send, ('group', 'xc'), 0, 0, tiled=True)  24.1 us
    all_gather x1, blocking collectives, shards(): lax.all_gather(hidden, 'y', axis_index_groups=[list(range(p, shard_count,...  16.2 us
    ppermute x4, starting transfers between devices, moved(): lax.ppermute(array, 'y', [(i, (i + by) % shard_count) for i in range(shar...  14.4 us
    all_to_all x1, waiting for transfers between devices, shards(): expert_rows = lax.all_to_all(send, ('group', 'xc'), 0, 0, tiled=True)  12.4 us
    all_to_all x1, starting transfers between devices, shards(): every_term = lax.all_to_all(spread, ('y', 'xc'), 0, 0, tiled=True)  10.7 us
    all_to_all x1, waiting for transfers between devices, shards(): every_term = lax.all_to_all(spread, ('y', 'xc'), 0, 0, tiled=True)  9.33 us
    pallas_call x7, Pallas kernels, call(): pl.pallas_call(kernel, in_specs=specs, out_specs=jax.tree.map(lambda _: V...  8.54 us
    all_to_all x1, starting transfers between devices, shards(): home = lax.all_to_all(terms, 'group', 0, 0, tiled=True)  6.28 us
  transfers between devices with their start and end apart: 8, of which 3 were waited for; matrix products, arithmetic and copies ran while one was open for 0% of the time, Pallas kernels for 5%

profile of v9, /device:TPU:1, one launch (start us, length us, event | category | flops | bytes accessed | tf_op | source)
XLA Modules:
  0.0 108.9 jit_solution(6128583382433942703)
XLA Ops:
  0.6 0.0 copy-start
  0.6 2.7 %shard_map.94 = (bf16[128,16,128]{2,1,0:T(8,128)(2,1)}, f32[256,128]{1,0:T(8,128)}) custom-call(bf16[112,128]{1,0:T(8,128)(2,1)} %bitcast.28, s32[8,128]{1,0:T(8,128)} %bitcast.24, s32[8,128]{1,0:T(8,128)} %bitcast.26, bf16[8,128]{1,0:T(8,128)(2,1)} %bitcast.30, bf16[256,128]{1,0:T(8,128)(2,1)} %bitcast.19, bf16[256,128]{1,0:T(8,128)(2,1)} %bitcast.21), custom_call_target="tpu_custom_call" | custom-call | tf_op jit(solution)/shard_map/pallas_call | solution.py:184
  3.3 24.1 %all-to-all-start = ((bf16[128,16,128]{2,1,0:T(8,128)(2,1)}), bf16[128,16,128]{2,1,0:T(8,128)(2,1)S(1)}, u32[]{:S(2)}, u32[]{:S(2)}) async-start(bf16[128,16,128]{2,1,0:T(8,128)(2,1)} %get-tuple-element.18), calls=%async_computation | async-start | bytes 1048576 | tf_op jit(solution)/shard_map/all_to_all | solution.py:213
  27.4 16.2 %all-gather = f32[1024,128]{1,0:T(8,128)S(1)} all-gather(f32[256,128]{1,0:T(8,128)} %get-tuple-element.19), channel_id=2, replica_groups={{0,16,32,48},{8,24,40,56},{1,17,33,49},{9,25,41,57},{2,18,34,50},{10,26..., dimensions={0}, use_global_device_ids=true | all-gather | bytes 655360 | tf_op jit(solution)/shard_map/all_gather | solution.py:215
  43.6 2.3 %collective-permute-start = (f32[4,256,128]{2,1,0:T(8,128)S(1)}, f32[4,256,128]{2,1,0:T(8,128)}, u32[]{:S(2)}, u32[]{:S(2)}) collective-permute-start(f32[4,256,128]{2,1,0:T(8,128)S(1)} %bitcast.15), channel_id=1, source_target_pairs={{0,8},{8,0},{16,24},{24,16},{32,40},{40,32},{48,56},{56,48},{1,9},... | collective-permute-start | bytes 1572872 | tf_op jit(solution)/shard_map/ppermute | solution.py:219
  45.9 12.4 %all-to-all-done = bf16[128,16,128]{2,1,0:T(8,128)(2,1)S(1)} async-done(((bf16[128,16,128]{2,1,0:T(8,128)(2,1)}), bf16[128,16,128]{2,1,0:T(8,128)(2,1)S(1)}, u32[]{:S(2)}, u32[]{:S(2)}) %all-to-all-start) | async-done | bytes 524320 | tf_op jit(solution)/shard_map/all_to_all | solution.py:213
  58.2 0.0 copy-done
  58.2 1.6 %shard_map.95 = (f32[640,128]{1,0:T(8,128)}, f32[640,128]{1,0:T(8,128)}, f32[768,128]{1,0:T(8,128)S(1)}, f32[256,128]{1,0:T(8,128)S(1)}, f32[256,128]{1,0:T(8,128)S(1)}) custom-call(s32[1]{0:T(128)} %bitcast.1.shard_ref, bf16[16,8,16,128]{3,2,1,0:T(8,128)(2,1)S(1)} %bitcast.17, bf16[1024,896]{1,0:T(8,128)(2,1)S(1)} %bitcast.18, f32[4,256,128]{2,1,0:T(8,128)S(1)} %bitcast.16), custom_call_target="tpu_custom_call" | custom-call | tf_op jit(solution)/shard_map/pallas_call | solution.py:184
  59.8 0.0 copy-start.1
  59.8 0.0 copy-start.2
  59.8 3.3 %collective-permute-start.1 = (f32[640,128]{1,0:T(8,128)}, f32[640,128]{1,0:T(8,128)S(1)}, u32[]{:S(2)}, u32[]{:S(2)}) collective-permute-start(f32[640,128]{1,0:T(8,128)} %get-tuple-element.20.right_ref), channel_id=1, source_target_pairs={{0,8},{8,16},{16,24},{24,32},{32,40},{40,48},{48,56},{56,0},{1,9},... | collective-permute-start | bytes 983048 | tf_op jit(solution)/shard_map/ppermute | solution.py:246
  63.2 3.8 %collective-permute-start.2 = (f32[640,128]{1,0:T(8,128)}, f32[640,128]{1,0:T(8,128)S(1)}, u32[]{:S(2)}, u32[]{:S(2)}) collective-permute-start(f32[640,128]{1,0:T(8,128)} %get-tuple-element.21.left_ref), channel_id=1, source_target_pairs={{0,56},{8,0},{16,8},{24,16},{32,24},{40,32},{48,40},{56,48},{1,57}... | collective-permute-start | bytes 983048 | tf_op jit(solution)/shard_map/ppermute | solution.py:246
  67.0 0.0 collective-permute-done.other_ref
  67.0 2.0 %shard_map.96 = f32[16,1,128]{2,1,0:T(1,128)} custom-call(s32[1]{0:T(128)} %bitcast.group_ref, s32[1]{0:T(128)} %bitcast.1.shard_ref, f32[640,128]{1,0:T(8,128)} %get-tuple-element.20.right_ref, f32[640,128]{1,0:T(8,128)} %get-tuple-element.21.left_ref, f32[768,128]{1,0:T(8,128)S(1)} %get-tuple-element.22.keep_ref, ...), custom_call_target="tpu_custom_call" | custom-call | tf_op jit(solution)/shard_map/pallas_call | solution.py:184
  69.0 6.3 %all-to-all-start.1 = ((f32[16,1,128]{2,1,0:T(1,128)}), f32[16,1,128]{2,1,0:T(1,128)S(1)}, u32[]{:S(2)}, u32[]{:S(2)}) async-start(f32[16,1,128]{2,1,0:T(1,128)} %shard_map.96), calls=%async_computation.1 | async-start | bytes 16384 | tf_op jit(solution)/shard_map/all_to_all | solution.py:251
  75.3 0.0 collective-permute-done.1.left_ref
  75.3 0.0 collective-permute-done.2.right_ref
  75.3 0.1 shard_map.98
  75.4 4.9 %collective-permute-start.3 = (f32[256,128]{1,0:T(8,128)S(1)}, f32[256,128]{1,0:T(8,128)S(1)}, u32[]{:S(2)}, u32[]{:S(2)}) collective-permute-start(f32[256,128]{1,0:T(8,128)S(1)} %get-tuple-element.25), channel_id=1, source_target_pairs={{0,40},{8,48},{16,56},{24,0},{32,8},{40,16},{48,24},{56,32},{1,41}... | collective-permute-start | bytes 393224 | tf_op jit(solution)/shard_map/ppermute | solution.py:246
  80.3 2.3 %collective-permute-start.4 = (f32[256,128]{1,0:T(8,128)S(1)}, f32[256,128]{1,0:T(8,128)S(1)}, u32[]{:S(2)}, u32[]{:S(2)}) collective-permute-start(f32[256,128]{1,0:T(8,128)S(1)} %get-tuple-element.26), channel_id=1, source_target_pairs={{0,24},{8,32},{16,40},{24,48},{32,56},{40,0},{48,8},{56,16},{1,25}... | collective-permute-start | bytes 393224 | tf_op jit(solution)/shard_map/ppermute | solution.py:246
  82.7 3.9 %all-to-all-done.1.home_ref = f32[16,1,128]{2,1,0:T(1,128)S(1)} async-done(((f32[16,1,128]{2,1,0:T(1,128)}), f32[16,1,128]{2,1,0:T(1,128)S(1)}, u32[]{:S(2)}, u32[]{:S(2)}) %all-to-all-start.1) | async-done | bytes 8224 | tf_op jit(solution)/shard_map/all_to_all | solution.py:251
  86.5 0.7 shard_map.97
  87.2 10.7 %all-to-all-start.2 = ((f32[64,2,128]{2,1,0:T(2,128)}), f32[64,2,128]{2,1,0:T(2,128)S(1)}, u32[]{:S(2)}, u32[]{:S(2)}) async-start(f32[64,2,128]{2,1,0:T(2,128)} %shard_map.97), calls=%async_computation.2 | async-start | bytes 131072 | tf_op jit(solution)/shard_map/all_to_all | solution.py:259
  97.9 0.0 collective-permute-done.3.down_ref
  97.9 0.0 collective-permute-done.4.up_ref
  98.0 0.0 copy-done.1
  98.0 0.0 copy-done.2
  98.0 0.7 shard_map.99
  98.7 9.3 %all-to-all-done.2 = f32[64,2,128]{2,1,0:T(2,128)S(1)} async-done(((f32[64,2,128]{2,1,0:T(2,128)}), f32[64,2,128]{2,1,0:T(2,128)S(1)}, u32[]{:S(2)}, u32[]{:S(2)}) %all-to-all-start.2) | async-done | bytes 65568 | tf_op jit(solution)/shard_map/all_to_all | solution.py:259
  108.0 0.0 copy-done.3
  108.0 0.0 copy-done.4
  108.0 0.8 shard_map.100
  (2 shorter events, 0.0 us)
Async XLA Ops:
  0.6 57.6 %copy-start = (bf16[1,1024,896]{2,1,0:T(8,128)(2,1)S(1)}, bf16[1,1024,896]{2,1,0:T(8,128)(2,1)}, u32[]{:S(2)}) copy-start(bf16[1,1024,896]{2,1,0:T(8,128)(2,1)} %param.11) | copy-start | bytes 5505028
  3.3 54.9 %all-to-all-start = ((bf16[128,16,128]{2,1,0:T(8,128)(2,1)}), bf16[128,16,128]{2,1,0:T(8,128)(2,1)S(1)}, u32[]{:S(2)}, u32[]{:S(2)}) async-start(bf16[128,16,128]{2,1,0:T(8,128)(2,1)} %get-tuple-element.18), calls=%async_computation | async-start | bytes 1048576 | tf_op jit(solution)/shard_map/all_to_all | solution.py:213
  43.6 23.4 %collective-permute-start = (f32[4,256,128]{2,1,0:T(8,128)S(1)}, f32[4,256,128]{2,1,0:T(8,128)}, u32[]{:S(2)}, u32[]{:S(2)}) collective-permute-start(f32[4,256,128]{2,1,0:T(8,128)S(1)} %bitcast.15), channel_id=1, source_target_pairs={{0,8},{8,0},{16,24},{24,16},{32,40},{40,32},{48,56},{56,48},{1,9},... | collective-permute-start | bytes 1572872 | tf_op jit(solution)/shard_map/ppermute | solution.py:219
  59.8 38.1 %copy-start.1 = (bf16[1,256,128]{2,1,0:T(8,128)(2,1)S(1)}, bf16[1,256,128]{2,1,0:T(8,128)(2,1)}, u32[]{:S(2)}) copy-start(bf16[1,256,128]{2,1,0:T(8,128)(2,1)} %param.12) | copy-start | bytes 196612
  59.8 38.1 %copy-start.2 = (bf16[1,256,128]{2,1,0:T(8,128)(2,1)S(1)}, bf16[1,256,128]{2,1,0:T(8,128)(2,1)}, u32[]{:S(2)}) copy-start(bf16[1,256,128]{2,1,0:T(8,128)(2,1)} %param.13) | copy-start | bytes 196612
  59.8 48.2 %copy-start.3 = (s32[128,8]{0,1:T(8,128)S(1)}, s32[128,8]{0,1:T(8,128)}, u32[]{:S(2)}) copy-start(s32[128,8]{0,1:T(8,128)} %param.8) | copy-start | bytes 12292
  59.8 48.2 %copy-start.4 = (s32[128,8]{0,1:T(8,128)S(1)}, s32[128,8]{0,1:T(8,128)}, u32[]{:S(2)}) copy-start(s32[128,8]{0,1:T(8,128)} %param.9) | copy-start | bytes 12292
  59.8 15.5 %collective-permute-start.1 = (f32[640,128]{1,0:T(8,128)}, f32[640,128]{1,0:T(8,128)S(1)}, u32[]{:S(2)}, u32[]{:S(2)}) collective-permute-start(f32[640,128]{1,0:T(8,128)} %get-tuple-element.20.right_ref), channel_id=1, source_target_pairs={{0,8},{8,16},{16,24},{24,32},{32,40},{40,48},{48,56},{56,0},{1,9},... | collective-permute-start | bytes 983048 | tf_op jit(solution)/shard_map/ppermute | solution.py:246
  63.2 12.1 %collective-permute-start.2 = (f32[640,128]{1,0:T(8,128)}, f32[640,128]{1,0:T(8,128)S(1)}, u32[]{:S(2)}, u32[]{:S(2)}) collective-permute-start(f32[640,128]{1,0:T(8,128)} %get-tuple-element.21.left_ref), channel_id=1, source_target_pairs={{0,56},{8,0},{16,8},{24,16},{32,24},{40,32},{48,40},{56,48},{1,57}... | collective-permute-start | bytes 983048 | tf_op jit(solution)/shard_map/ppermute | solution.py:246
  69.0 17.5 %all-to-all-start.1 = ((f32[16,1,128]{2,1,0:T(1,128)}), f32[16,1,128]{2,1,0:T(1,128)S(1)}, u32[]{:S(2)}, u32[]{:S(2)}) async-start(f32[16,1,128]{2,1,0:T(1,128)} %shard_map.96), calls=%async_computation.1 | async-start | bytes 16384 | tf_op jit(solution)/shard_map/all_to_all | solution.py:251
  75.4 22.6 %collective-permute-start.3 = (f32[256,128]{1,0:T(8,128)S(1)}, f32[256,128]{1,0:T(8,128)S(1)}, u32[]{:S(2)}, u32[]{:S(2)}) collective-permute-start(f32[256,128]{1,0:T(8,128)S(1)} %get-tuple-element.25), channel_id=1, source_target_pairs={{0,40},{8,48},{16,56},{24,0},{32,8},{40,16},{48,24},{56,32},{1,41}... | collective-permute-start | bytes 393224 | tf_op jit(solution)/shard_map/ppermute | solution.py:246
  80.3 17.6 %collective-permute-start.4 = (f32[256,128]{1,0:T(8,128)S(1)}, f32[256,128]{1,0:T(8,128)S(1)}, u32[]{:S(2)}, u32[]{:S(2)}) collective-permute-start(f32[256,128]{1,0:T(8,128)S(1)} %get-tuple-element.26), channel_id=1, source_target_pairs={{0,24},{8,32},{16,40},{24,48},{32,56},{40,0},{48,8},{56,16},{1,25}... | collective-permute-start | bytes 393224 | tf_op jit(solution)/shard_map/ppermute | solution.py:246
  87.2 20.8 %all-to-all-start.2 = ((f32[64,2,128]{2,1,0:T(2,128)}), f32[64,2,128]{2,1,0:T(2,128)S(1)}, u32[]{:S(2)}, u32[]{:S(2)}) async-start(f32[64,2,128]{2,1,0:T(2,128)} %shard_map.97), calls=%async_computation.2 | async-start | bytes 131072 | tf_op jit(solution)/shard_map/all_to_all | solution.py:259

commit v10 on v9

--- a/solution.py
+++ b/solution.py
@@ -91,21 +91,29 @@
 
 
 def terms_kernel(
-    group_ref, shard_ref, right_ref, left_ref, keep_ref, other_ref, base_ref, term_ref
+    group_ref, shard_ref, right_in, left_in, keep_ref, other_ref, base_ref, term_ref, odd_ref, sems
 ):
     capacity, lane_count = base_ref.shape
     groups = term_ref.shape[0]
     count = 2 * other_ref.shape[0]
     group, shard = group_ref[0], shard_ref[0]
+    copies = [
+        pltpu.make_async_copy(part.at[:capacity], odd_ref.at[i], sems.at[i])
+        for i, part in enumerate((right_in, left_in))
+    ]
+    for copy in copies:
+        copy.start()
+
+    def product(offset, part):
+        return part * other_ref[(shard + offset) % count // 2]
+
     terms = base_ref[...]
-    for offset, part_ref, first in (
-        (1, right_ref, 0),
-        (count - 1, left_ref, 0),
-        (count - 3, keep_ref, capacity),
-        (3, keep_ref, 2 * capacity),
-    ):
-        unit = (shard + offset) % count
-        terms += part_ref[first : first + capacity] * other_ref[unit // 2]
+    terms += product(count - 3, keep_ref[capacity : 2 * capacity])
+    terms += product(3, keep_ref[2 * capacity :])
+    for copy in copies:
+        copy.wait()
+    terms += product(1, odd_ref[0])
+    terms += product(count - 1, odd_ref[1])
     total = jnp.sum(terms, axis=1, keepdims=True)
     row_ids, lane_ids = rows((capacity, lane_count)), lanes((capacity, lane_count))
     hit = lane_ids == group % (lane_count // SLOTS) * SLOTS + row_ids % SLOTS
@@ -178,6 +186,7 @@
 
 VMEM = pl.BlockSpec(memory_space=pltpu.VMEM)
 SMEM = pl.BlockSpec(memory_space=pltpu.SMEM)
+HBM = pl.BlockSpec(memory_space=pltpu.HBM)
 
 
 def call(kernel, specs, out_shape, *args, limit=24 << 20):
@@ -228,19 +237,17 @@
         same,
         limit=24 << 20,
     )
-    terms = call(
+    terms = pl.pallas_call(
         terms_kernel,
-        [SMEM] * 2 + [VMEM] * 5,
-        shape((groups, 1, lane_count), F32),
-        group[None],
-        shard[None],
-        right,
-        left,
-        keep,
-        other,
-        base,
-        limit=24 << 20,
-    )
+        in_specs=[SMEM] * 2 + [HBM] * 2 + [VMEM] * 3,
+        out_specs=VMEM,
+        out_shape=shape((groups, 1, lane_count), F32),
+        scratch_shapes=[
+            pltpu.VMEM((2, capacity, lane_count), F32),
+            pltpu.SemaphoreType.DMA((2,)),
+        ],
+        compiler_params=pltpu.CompilerParams(vmem_limit_bytes=24 << 20),
+    )(group[None], shard[None], right, left, keep, other, base)
 
     def moved(array, by):
         return lax.ppermute(

time: 109 us -> 110 us (level)
    pallas_call x0 -> x1, Pallas kernels: none -> 2.76 us  [shards(): pl.pallas_call(terms_kernel, in_specs=[SMEM] * 2 + [HBM] * 2 + [VMEM] * 3...]
    pallas_call x7 -> x6, Pallas kernels: 8.54 us -> 6.55 us  [call(): pl.pallas_call(kernel, in_specs=specs, out_specs=jax.tree.map(lambda _: V...]
where the time goes in v10:
time: 110 us
  starting transfers between devices  57.6 us (52%)
  waiting for transfers between devices  25.7 us (23%)
  blocking collectives  16.2 us (15%)
  Pallas kernels  9.31 us (8%)
    all_to_all x1, starting transfers between devices, shards(): expert_rows = lax.all_to_all(send, ('group', 'xc'), 0, 0, tiled=True)  24.1 us
    all_gather x1, blocking collectives, shards(): lax.all_gather(hidden, 'y', axis_index_groups=[list(range(p, shard_count,...  16.2 us
    ppermute x4, starting transfers between devices, moved(): lax.ppermute(array, 'y', [(i, (i + by) % shard_count) for i in range(shar...  14.2 us
    all_to_all x1, waiting for transfers between devices, shards(): expert_rows = lax.all_to_all(send, ('group', 'xc'), 0, 0, tiled=True)  12.4 us
    all_to_all x1, starting transfers between devices, shards(): every_term = lax.all_to_all(spread, ('y', 'xc'), 0, 0, tiled=True)  10.7 us
    all_to_all x1, waiting for transfers between devices, shards(): every_term = lax.all_to_all(spread, ('y', 'xc'), 0, 0, tiled=True)  9.33 us
    pallas_call x6, Pallas kernels, call(): pl.pallas_call(kernel, in_specs=specs, out_specs=jax.tree.map(lambda _: V...  6.55 us
    all_to_all x1, starting transfers between devices, shards(): home = lax.all_to_all(terms, 'group', 0, 0, tiled=True)  6.29 us
  transfers between devices with their start and end apart: 8, of which 3 were waited for; matrix products, arithmetic and copies ran while one was open for 0% of the time, Pallas kernels for 5%

profile of v10, /device:TPU:1, one launch (start us, length us, event | category | flops | bytes accessed | tf_op | source)
XLA Modules:
  0.0 109.6 jit_solution(7846124343915195210)
XLA Ops:
  0.6 0.0 copy-start
  0.6 2.7 %shard_map.94 = (bf16[128,16,128]{2,1,0:T(8,128)(2,1)}, f32[256,128]{1,0:T(8,128)}) custom-call(bf16[112,128]{1,0:T(8,128)(2,1)} %bitcast.28, s32[8,128]{1,0:T(8,128)} %bitcast.24, s32[8,128]{1,0:T(8,128)} %bitcast.26, bf16[8,128]{1,0:T(8,128)(2,1)} %bitcast.30, bf16[256,128]{1,0:T(8,128)(2,1)} %bitcast.19, bf16[256,128]{1,0:T(8,128)(2,1)} %bitcast.21), custom_call_target="tpu_custom_call" | custom-call | tf_op jit(solution)/shard_map/pallas_call | solution.py:193
  3.3 24.1 %all-to-all-start = ((bf16[128,16,128]{2,1,0:T(8,128)(2,1)}), bf16[128,16,128]{2,1,0:T(8,128)(2,1)S(1)}, u32[]{:S(2)}, u32[]{:S(2)}) async-start(bf16[128,16,128]{2,1,0:T(8,128)(2,1)} %get-tuple-element.18), calls=%async_computation | async-start | bytes 1048576 | tf_op jit(solution)/shard_map/all_to_all | solution.py:222
  27.4 16.2 %all-gather = f32[1024,128]{1,0:T(8,128)S(1)} all-gather(f32[256,128]{1,0:T(8,128)} %get-tuple-element.19), channel_id=2, replica_groups={{0,16,32,48},{8,24,40,56},{1,17,33,49},{9,25,41,57},{2,18,34,50},{10,26..., dimensions={0}, use_global_device_ids=true | all-gather | bytes 655360 | tf_op jit(solution)/shard_map/all_gather | solution.py:224
  43.6 2.3 %collective-permute-start = (f32[4,256,128]{2,1,0:T(8,128)S(1)}, f32[4,256,128]{2,1,0:T(8,128)}, u32[]{:S(2)}, u32[]{:S(2)}) collective-permute-start(f32[4,256,128]{2,1,0:T(8,128)S(1)} %bitcast.15), channel_id=1, source_target_pairs={{0,8},{8,0},{16,24},{24,16},{32,40},{40,32},{48,56},{56,48},{1,9},... | collective-permute-start | bytes 1572872 | tf_op jit(solution)/shard_map/ppermute | solution.py:228
  45.9 12.4 %all-to-all-done = bf16[128,16,128]{2,1,0:T(8,128)(2,1)S(1)} async-done(((bf16[128,16,128]{2,1,0:T(8,128)(2,1)}), bf16[128,16,128]{2,1,0:T(8,128)(2,1)S(1)}, u32[]{:S(2)}, u32[]{:S(2)}) %all-to-all-start) | async-done | bytes 524320 | tf_op jit(solution)/shard_map/all_to_all | solution.py:222
  58.2 0.0 copy-done
  58.2 1.6 %shard_map.95 = (f32[640,128]{1,0:T(8,128)}, f32[640,128]{1,0:T(8,128)}, f32[768,128]{1,0:T(8,128)S(1)}, f32[256,128]{1,0:T(8,128)S(1)}, f32[256,128]{1,0:T(8,128)S(1)}) custom-call(s32[1]{0:T(128)} %bitcast.1.shard_ref, bf16[16,8,16,128]{3,2,1,0:T(8,128)(2,1)S(1)} %bitcast.17, bf16[1024,896]{1,0:T(8,128)(2,1)S(1)} %bitcast.18, f32[4,256,128]{2,1,0:T(8,128)S(1)} %bitcast.16), custom_call_target="tpu_custom_call" | custom-call | tf_op jit(solution)/shard_map/pallas_call | solution.py:193
  59.8 0.0 copy-start.1
  59.8 0.0 copy-start.2
  59.8 3.3 %collective-permute-start.1 = (f32[640,128]{1,0:T(8,128)}, f32[640,128]{1,0:T(8,128)S(1)}, u32[]{:S(2)}, u32[]{:S(2)}) collective-permute-start(f32[640,128]{1,0:T(8,128)} %get-tuple-element.20.right_in), channel_id=1, source_target_pairs={{0,8},{8,16},{16,24},{24,32},{32,40},{40,48},{48,56},{56,0},{1,9},... | collective-permute-start | bytes 983048 | tf_op jit(solution)/shard_map/ppermute | solution.py:253
  63.2 3.8 %collective-permute-start.2 = (f32[640,128]{1,0:T(8,128)}, f32[640,128]{1,0:T(8,128)S(1)}, u32[]{:S(2)}, u32[]{:S(2)}) collective-permute-start(f32[640,128]{1,0:T(8,128)} %get-tuple-element.21.left_in), channel_id=1, source_target_pairs={{0,56},{8,0},{16,8},{24,16},{32,24},{40,32},{48,40},{56,48},{1,57}... | collective-permute-start | bytes 983048 | tf_op jit(solution)/shard_map/ppermute | solution.py:253
  67.0 0.0 collective-permute-done.other_ref
  67.0 2.8 %shard_map.96 = f32[16,1,128]{2,1,0:T(1,128)} custom-call(s32[1]{0:T(128)} %bitcast.group_ref, s32[1]{0:T(128)} %bitcast.1.shard_ref, f32[640,128]{1,0:T(8,128)} %get-tuple-element.20.right_in, f32[640,128]{1,0:T(8,128)} %get-tuple-element.21.left_in, f32[768,128]{1,0:T(8,128)S(1)} %get-tuple-element.22.keep_ref, ...), custom_call_target="tpu_custom_call" | custom-call | tf_op jit(solution)/shard_map/pallas_call | solution.py:240
  69.8 6.3 %all-to-all-start.1 = ((f32[16,1,128]{2,1,0:T(1,128)}), f32[16,1,128]{2,1,0:T(1,128)S(1)}, u32[]{:S(2)}, u32[]{:S(2)}) async-start(f32[16,1,128]{2,1,0:T(1,128)} %shard_map.96), calls=%async_computation.1 | async-start | bytes 16384 | tf_op jit(solution)/shard_map/all_to_all | solution.py:258
  76.1 0.0 collective-permute-done.1.left_ref
  76.1 0.0 collective-permute-done.2.right_ref
  76.1 0.1 shard_map.98
  76.2 4.9 %collective-permute-start.3 = (f32[256,128]{1,0:T(8,128)S(1)}, f32[256,128]{1,0:T(8,128)S(1)}, u32[]{:S(2)}, u32[]{:S(2)}) collective-permute-start(f32[256,128]{1,0:T(8,128)S(1)} %get-tuple-element.25), channel_id=1, source_target_pairs={{0,40},{8,48},{16,56},{24,0},{32,8},{40,16},{48,24},{56,32},{1,41}... | collective-permute-start | bytes 393224 | tf_op jit(solution)/shard_map/ppermute | solution.py:253
  81.1 2.2 %collective-permute-start.4 = (f32[256,128]{1,0:T(8,128)S(1)}, f32[256,128]{1,0:T(8,128)S(1)}, u32[]{:S(2)}, u32[]{:S(2)}) collective-permute-start(f32[256,128]{1,0:T(8,128)S(1)} %get-tuple-element.26), channel_id=1, source_target_pairs={{0,24},{8,32},{16,40},{24,48},{32,56},{40,0},{48,8},{56,16},{1,25}... | collective-permute-start | bytes 393224 | tf_op jit(solution)/shard_map/ppermute | solution.py:253
  83.3 4.0 %all-to-all-done.1.home_ref = f32[16,1,128]{2,1,0:T(1,128)S(1)} async-done(((f32[16,1,128]{2,1,0:T(1,128)}), f32[16,1,128]{2,1,0:T(1,128)S(1)}, u32[]{:S(2)}, u32[]{:S(2)}) %all-to-all-start.1) | async-done | bytes 8224 | tf_op jit(solution)/shard_map/all_to_all | solution.py:258
  87.3 0.7 shard_map.97
  88.0 10.7 %all-to-all-start.2 = ((f32[64,2,128]{2,1,0:T(2,128)}), f32[64,2,128]{2,1,0:T(2,128)S(1)}, u32[]{:S(2)}, u32[]{:S(2)}) async-start(f32[64,2,128]{2,1,0:T(2,128)} %shard_map.97), calls=%async_computation.2 | async-start | bytes 131072 | tf_op jit(solution)/shard_map/all_to_all | solution.py:266
  98.7 0.0 collective-permute-done.3.down_ref
  98.7 0.0 collective-permute-done.4.up_ref
  98.7 0.0 copy-done.1
  98.7 0.0 copy-done.2
  98.8 0.7 shard_map.99
  99.5 9.3 %all-to-all-done.2 = f32[64,2,128]{2,1,0:T(2,128)S(1)} async-done(((f32[64,2,128]{2,1,0:T(2,128)}), f32[64,2,128]{2,1,0:T(2,128)S(1)}, u32[]{:S(2)}, u32[]{:S(2)}) %all-to-all-start.2) | async-done | bytes 65568 | tf_op jit(solution)/shard_map/all_to_all | solution.py:266
  108.8 0.0 copy-done.3
  108.8 0.0 copy-done.4
  108.8 0.8 shard_map.100
  (2 shorter events, 0.0 us)
Async XLA Ops:
  0.6 57.6 %copy-start = (bf16[1,1024,896]{2,1,0:T(8,128)(2,1)S(1)}, bf16[1,1024,896]{2,1,0:T(8,128)(2,1)}, u32[]{:S(2)}) copy-start(bf16[1,1024,896]{2,1,0:T(8,128)(2,1)} %param.11) | copy-start | bytes 5505028
  3.3 54.9 %all-to-all-start = ((bf16[128,16,128]{2,1,0:T(8,128)(2,1)}), bf16[128,16,128]{2,1,0:T(8,128)(2,1)S(1)}, u32[]{:S(2)}, u32[]{:S(2)}) async-start(bf16[128,16,128]{2,1,0:T(8,128)(2,1)} %get-tuple-element.18), calls=%async_computation | async-start | bytes 1048576 | tf_op jit(solution)/shard_map/all_to_all | solution.py:222
  43.6 23.4 %collective-permute-start = (f32[4,256,128]{2,1,0:T(8,128)S(1)}, f32[4,256,128]{2,1,0:T(8,128)}, u32[]{:S(2)}, u32[]{:S(2)}) collective-permute-start(f32[4,256,128]{2,1,0:T(8,128)S(1)} %bitcast.15), channel_id=1, source_target_pairs={{0,8},{8,0},{16,24},{24,16},{32,40},{40,32},{48,56},{56,48},{1,9},... | collective-permute-start | bytes 1572872 | tf_op jit(solution)/shard_map/ppermute | solution.py:228
  59.8 38.9 %copy-start.1 = (bf16[1,256,128]{2,1,0:T(8,128)(2,1)S(1)}, bf16[1,256,128]{2,1,0:T(8,128)(2,1)}, u32[]{:S(2)}) copy-start(bf16[1,256,128]{2,1,0:T(8,128)(2,1)} %param.12) | copy-start | bytes 196612
  59.8 38.9 %copy-start.2 = (bf16[1,256,128]{2,1,0:T(8,128)(2,1)S(1)}, bf16[1,256,128]{2,1,0:T(8,128)(2,1)}, u32[]{:S(2)}) copy-start(bf16[1,256,128]{2,1,0:T(8,128)(2,1)} %param.13) | copy-start | bytes 196612
  59.8 49.0 %copy-start.3 = (s32[128,8]{0,1:T(8,128)S(1)}, s32[128,8]{0,1:T(8,128)}, u32[]{:S(2)}) copy-start(s32[128,8]{0,1:T(8,128)} %param.8) | copy-start | bytes 12292
  59.8 49.0 %copy-start.4 = (s32[128,8]{0,1:T(8,128)S(1)}, s32[128,8]{0,1:T(8,128)}, u32[]{:S(2)}) copy-start(s32[128,8]{0,1:T(8,128)} %param.9) | copy-start | bytes 12292
  59.8 16.3 %collective-permute-start.1 = (f32[640,128]{1,0:T(8,128)}, f32[640,128]{1,0:T(8,128)S(1)}, u32[]{:S(2)}, u32[]{:S(2)}) collective-permute-start(f32[640,128]{1,0:T(8,128)} %get-tuple-element.20.right_in), channel_id=1, source_target_pairs={{0,8},{8,16},{16,24},{24,32},{32,40},{40,48},{48,56},{56,0},{1,9},... | collective-permute-start | bytes 983048 | tf_op jit(solution)/shard_map/ppermute | solution.py:253
  63.2 12.9 %collective-permute-start.2 = (f32[640,128]{1,0:T(8,128)}, f32[640,128]{1,0:T(8,128)S(1)}, u32[]{:S(2)}, u32[]{:S(2)}) collective-permute-start(f32[640,128]{1,0:T(8,128)} %get-tuple-element.21.left_in), channel_id=1, source_target_pairs={{0,56},{8,0},{16,8},{24,16},{32,24},{40,32},{48,40},{56,48},{1,57}... | collective-permute-start | bytes 983048 | tf_op jit(solution)/shard_map/ppermute | solution.py:253
  69.8 17.5 %all-to-all-start.1 = ((f32[16,1,128]{2,1,0:T(1,128)}), f32[16,1,128]{2,1,0:T(1,128)S(1)}, u32[]{:S(2)}, u32[]{:S(2)}) async-start(f32[16,1,128]{2,1,0:T(1,128)} %shard_map.96), calls=%async_computation.1 | async-start | bytes 16384 | tf_op jit(solution)/shard_map/all_to_all | solution.py:258
  76.2 22.6 %collective-permute-start.3 = (f32[256,128]{1,0:T(8,128)S(1)}, f32[256,128]{1,0:T(8,128)S(1)}, u32[]{:S(2)}, u32[]{:S(2)}) collective-permute-start(f32[256,128]{1,0:T(8,128)S(1)} %get-tuple-element.25), channel_id=1, source_target_pairs={{0,40},{8,48},{16,56},{24,0},{32,8},{40,16},{48,24},{56,32},{1,41}... | collective-permute-start | bytes 393224 | tf_op jit(solution)/shard_map/ppermute | solution.py:253
  81.1 17.6 %collective-permute-start.4 = (f32[256,128]{1,0:T(8,128)S(1)}, f32[256,128]{1,0:T(8,128)S(1)}, u32[]{:S(2)}, u32[]{:S(2)}) collective-permute-start(f32[256,128]{1,0:T(8,128)S(1)} %get-tuple-element.26), channel_id=1, source_target_pairs={{0,24},{8,32},{16,40},{24,48},{32,56},{40,0},{48,8},{56,16},{1,25}... | collective-permute-start | bytes 393224 | tf_op jit(solution)/shard_map/ppermute | solution.py:253
  88.0 20.8 %all-to-all-start.2 = ((f32[64,2,128]{2,1,0:T(2,128)}), f32[64,2,128]{2,1,0:T(2,128)S(1)}, u32[]{:S(2)}, u32[]{:S(2)}) async-start(f32[64,2,128]{2,1,0:T(2,128)} %shard_map.97), calls=%async_computation.2 | async-start | bytes 131072 | tf_op jit(solution)/shard_map/all_to_all | solution.py:266

commit v11 on v9

--- a/solution.py
+++ b/solution.py
@@ -35,10 +35,12 @@
     chunk = 256
     for start in range(0, out_ref.shape[0] * SLOTS, chunk):
         row_ids = rows((chunk, tok_count)) + start
+        pick = jnp.zeros((chunk, tok_count), F32)
         gate = jnp.zeros((chunk, tok_count), F32)
         for k in range(place.shape[0]):
-            gate = jnp.where(row_ids == place[k : k + 1, :], gates[k : k + 1, :], gate)
-        pick = jnp.where(gate > 0.0, 1.0, 0.0)
+            hit = row_ids == place[k : k + 1, :]
+            pick = jnp.where(hit, 1.0, pick)
+            gate = jnp.where(hit, gates[k : k + 1, :], gate)
         both = jnp.concatenate([pick.astype(BF16), gate.astype(BF16)], axis=1)
         block = lax.dot_general(both, source, NT, preferred_element_type=F32)
         out_ref[start // SLOTS : (start + chunk) // SLOTS] = block.astype(BF16).reshape(

time: 109 us -> 110 us (level)
  no operation moved by 1% of the time
where the time goes in v11:
time: 110 us; the launch traced here: 109 us
  starting transfers between devices  57.8 us (53%)
  waiting for transfers between devices  25.6 us (23%)
  blocking collectives  16.2 us (15%)
  Pallas kernels  8.93 us (8%)
    all_to_all x1, starting transfers between devices, shards(): expert_rows = lax.all_to_all(send, ('group', 'xc'), 0, 0, tiled=True)  24.1 us
    all_gather x1, blocking collectives, shards(): lax.all_gather(hidden, 'y', axis_index_groups=[list(range(p, shard_count,...  16.2 us
    ppermute x4, starting transfers between devices, moved(): lax.ppermute(array, 'y', [(i, (i + by) % shard_count) for i in range(shar...  14.4 us
    all_to_all x1, waiting for transfers between devices, shards(): expert_rows = lax.all_to_all(send, ('group', 'xc'), 0, 0, tiled=True)  12.4 us
    all_to_all x1, starting transfers between devices, shards(): every_term = lax.all_to_all(spread, ('y', 'xc'), 0, 0, tiled=True)  10.8 us
    all_to_all x1, waiting for transfers between devices, shards(): every_term = lax.all_to_all(spread, ('y', 'xc'), 0, 0, tiled=True)  9.33 us
    pallas_call x7, Pallas kernels, call(): pl.pallas_call(kernel, in_specs=specs, out_specs=jax.tree.map(lambda _: V...  8.93 us
    all_to_all x1, starting transfers between devices, shards(): home = lax.all_to_all(terms, 'group', 0, 0, tiled=True)  6.27 us
  transfers between devices with their start and end apart: 8, of which 3 were waited for; matrix products, arithmetic and copies ran while one was open for 0% of the time, Pallas kernels for 5%

profile of v11, /device:TPU:1, one launch (start us, length us, event | category | flops | bytes accessed | tf_op | source)
XLA Modules:
  0.0 109.2 jit_solution(1343329393651049850)
XLA Ops:
  0.6 0.0 copy-start
  0.6 3.1 %shard_map.94 = (bf16[128,16,128]{2,1,0:T(8,128)(2,1)}, f32[256,128]{1,0:T(8,128)}) custom-call(bf16[112,128]{1,0:T(8,128)(2,1)} %bitcast.28, s32[8,128]{1,0:T(8,128)} %bitcast.24, s32[8,128]{1,0:T(8,128)} %bitcast.26, bf16[8,128]{1,0:T(8,128)(2,1)} %bitcast.30, bf16[256,128]{1,0:T(8,128)(2,1)} %bitcast.19, bf16[256,128]{1,0:T(8,128)(2,1)} %bitcast.21), custom_call_target="tpu_custom_call" | custom-call | tf_op jit(solution)/shard_map/pallas_call | solution.py:186
  3.7 24.1 %all-to-all-start = ((bf16[128,16,128]{2,1,0:T(8,128)(2,1)}), bf16[128,16,128]{2,1,0:T(8,128)(2,1)S(1)}, u32[]{:S(2)}, u32[]{:S(2)}) async-start(bf16[128,16,128]{2,1,0:T(8,128)(2,1)} %get-tuple-element.18), calls=%async_computation | async-start | bytes 1048576 | tf_op jit(solution)/shard_map/all_to_all | solution.py:215
  27.8 16.2 %all-gather = f32[1024,128]{1,0:T(8,128)S(1)} all-gather(f32[256,128]{1,0:T(8,128)} %get-tuple-element.19), channel_id=2, replica_groups={{0,16,32,48},{8,24,40,56},{1,17,33,49},{9,25,41,57},{2,18,34,50},{10,26..., dimensions={0}, use_global_device_ids=true | all-gather | bytes 655360 | tf_op jit(solution)/shard_map/all_gather | solution.py:217
  44.0 2.3 %collective-permute-start = (f32[4,256,128]{2,1,0:T(8,128)S(1)}, f32[4,256,128]{2,1,0:T(8,128)}, u32[]{:S(2)}, u32[]{:S(2)}) collective-permute-start(f32[4,256,128]{2,1,0:T(8,128)S(1)} %bitcast.15), channel_id=1, source_target_pairs={{0,8},{8,0},{16,24},{24,16},{32,40},{40,32},{48,56},{56,48},{1,9},... | collective-permute-start | bytes 1572872 | tf_op jit(solution)/shard_map/ppermute | solution.py:221
  46.2 12.4 %all-to-all-done = bf16[128,16,128]{2,1,0:T(8,128)(2,1)S(1)} async-done(((bf16[128,16,128]{2,1,0:T(8,128)(2,1)}), bf16[128,16,128]{2,1,0:T(8,128)(2,1)S(1)}, u32[]{:S(2)}, u32[]{:S(2)}) %all-to-all-start) | async-done | bytes 524320 | tf_op jit(solution)/shard_map/all_to_all | solution.py:215
  58.6 0.0 copy-done
  58.6 1.6 %shard_map.95 = (f32[640,128]{1,0:T(8,128)}, f32[640,128]{1,0:T(8,128)}, f32[768,128]{1,0:T(8,128)S(1)}, f32[256,128]{1,0:T(8,128)S(1)}, f32[256,128]{1,0:T(8,128)S(1)}) custom-call(s32[1]{0:T(128)} %bitcast.1.shard_ref, bf16[16,8,16,128]{3,2,1,0:T(8,128)(2,1)S(1)} %bitcast.17, bf16[1024,896]{1,0:T(8,128)(2,1)S(1)} %bitcast.18, f32[4,256,128]{2,1,0:T(8,128)S(1)} %bitcast.16), custom_call_target="tpu_custom_call" | custom-call | tf_op jit(solution)/shard_map/pallas_call | solution.py:186
  60.2 0.0 copy-start.1
  60.2 0.0 copy-start.2
  60.2 3.3 %collective-permute-start.1 = (f32[640,128]{1,0:T(8,128)}, f32[640,128]{1,0:T(8,128)S(1)}, u32[]{:S(2)}, u32[]{:S(2)}) collective-permute-start(f32[640,128]{1,0:T(8,128)} %get-tuple-element.20.right_ref), channel_id=1, source_target_pairs={{0,8},{8,16},{16,24},{24,32},{32,40},{40,48},{48,56},{56,0},{1,9},... | collective-permute-start | bytes 983048 | tf_op jit(solution)/shard_map/ppermute | solution.py:248
  63.6 3.8 %collective-permute-start.2 = (f32[640,128]{1,0:T(8,128)}, f32[640,128]{1,0:T(8,128)S(1)}, u32[]{:S(2)}, u32[]{:S(2)}) collective-permute-start(f32[640,128]{1,0:T(8,128)} %get-tuple-element.21.left_ref), channel_id=1, source_target_pairs={{0,56},{8,0},{16,8},{24,16},{32,24},{40,32},{48,40},{56,48},{1,57}... | collective-permute-start | bytes 983048 | tf_op jit(solution)/shard_map/ppermute | solution.py:248
  67.4 0.0 collective-permute-done.other_ref
  67.4 2.0 %shard_map.96 = f32[16,1,128]{2,1,0:T(1,128)} custom-call(s32[1]{0:T(128)} %bitcast.group_ref, s32[1]{0:T(128)} %bitcast.1.shard_ref, f32[640,128]{1,0:T(8,128)} %get-tuple-element.20.right_ref, f32[640,128]{1,0:T(8,128)} %get-tuple-element.21.left_ref, f32[768,128]{1,0:T(8,128)S(1)} %get-tuple-element.22.keep_ref, ...), custom_call_target="tpu_custom_call" | custom-call | tf_op jit(solution)/shard_map/pallas_call | solution.py:186
  69.4 6.3 %all-to-all-start.1 = ((f32[16,1,128]{2,1,0:T(1,128)}), f32[16,1,128]{2,1,0:T(1,128)S(1)}, u32[]{:S(2)}, u32[]{:S(2)}) async-start(f32[16,1,128]{2,1,0:T(1,128)} %shard_map.96), calls=%async_computation.1 | async-start | bytes 16384 | tf_op jit(solution)/shard_map/all_to_all | solution.py:253
  75.7 0.0 collective-permute-done.1.left_ref
  75.7 0.0 collective-permute-done.2.right_ref
  75.7 0.1 shard_map.98
  75.7 4.9 %collective-permute-start.3 = (f32[256,128]{1,0:T(8,128)S(1)}, f32[256,128]{1,0:T(8,128)S(1)}, u32[]{:S(2)}, u32[]{:S(2)}) collective-permute-start(f32[256,128]{1,0:T(8,128)S(1)} %get-tuple-element.25), channel_id=1, source_target_pairs={{0,40},{8,48},{16,56},{24,0},{32,8},{40,16},{48,24},{56,32},{1,41}... | collective-permute-start | bytes 393224 | tf_op jit(solution)/shard_map/ppermute | solution.py:248
  80.7 2.3 %collective-permute-start.4 = (f32[256,128]{1,0:T(8,128)S(1)}, f32[256,128]{1,0:T(8,128)S(1)}, u32[]{:S(2)}, u32[]{:S(2)}) collective-permute-start(f32[256,128]{1,0:T(8,128)S(1)} %get-tuple-element.26), channel_id=1, source_target_pairs={{0,24},{8,32},{16,40},{24,48},{32,56},{40,0},{48,8},{56,16},{1,25}... | collective-permute-start | bytes 393224 | tf_op jit(solution)/shard_map/ppermute | solution.py:248
  83.0 3.9 %all-to-all-done.1.home_ref = f32[16,1,128]{2,1,0:T(1,128)S(1)} async-done(((f32[16,1,128]{2,1,0:T(1,128)}), f32[16,1,128]{2,1,0:T(1,128)S(1)}, u32[]{:S(2)}, u32[]{:S(2)}) %all-to-all-start.1) | async-done | bytes 8224 | tf_op jit(solution)/shard_map/all_to_all | solution.py:253
  86.9 0.7 shard_map.97
  87.5 10.8 %all-to-all-start.2 = ((f32[64,2,128]{2,1,0:T(2,128)}), f32[64,2,128]{2,1,0:T(2,128)S(1)}, u32[]{:S(2)}, u32[]{:S(2)}) async-start(f32[64,2,128]{2,1,0:T(2,128)} %shard_map.97), calls=%async_computation.2 | async-start | bytes 131072 | tf_op jit(solution)/shard_map/all_to_all | solution.py:261
  98.3 0.0 collective-permute-done.3.down_ref
  98.3 0.0 collective-permute-done.4.up_ref
  98.3 0.0 copy-done.1
  98.4 0.0 copy-done.2
  98.4 0.7 shard_map.99
  99.1 9.3 %all-to-all-done.2 = f32[64,2,128]{2,1,0:T(2,128)S(1)} async-done(((f32[64,2,128]{2,1,0:T(2,128)}), f32[64,2,128]{2,1,0:T(2,128)S(1)}, u32[]{:S(2)}, u32[]{:S(2)}) %all-to-all-start.2) | async-done | bytes 65568 | tf_op jit(solution)/shard_map/all_to_all | solution.py:261
  108.4 0.0 copy-done.3
  108.4 0.0 copy-done.4
  108.4 0.8 shard_map.100
  (2 shorter events, 0.0 us)
Async XLA Ops:
  0.6 58.0 %copy-start = (bf16[1,1024,896]{2,1,0:T(8,128)(2,1)S(1)}, bf16[1,1024,896]{2,1,0:T(8,128)(2,1)}, u32[]{:S(2)}) copy-start(bf16[1,1024,896]{2,1,0:T(8,128)(2,1)} %param.11) | copy-start | bytes 5505028
  3.7 54.9 %all-to-all-start = ((bf16[128,16,128]{2,1,0:T(8,128)(2,1)}), bf16[128,16,128]{2,1,0:T(8,128)(2,1)S(1)}, u32[]{:S(2)}, u32[]{:S(2)}) async-start(bf16[128,16,128]{2,1,0:T(8,128)(2,1)} %get-tuple-element.18), calls=%async_computation | async-start | bytes 1048576 | tf_op jit(solution)/shard_map/all_to_all | solution.py:215
  44.0 23.4 %collective-permute-start = (f32[4,256,128]{2,1,0:T(8,128)S(1)}, f32[4,256,128]{2,1,0:T(8,128)}, u32[]{:S(2)}, u32[]{:S(2)}) collective-permute-start(f32[4,256,128]{2,1,0:T(8,128)S(1)} %bitcast.15), channel_id=1, source_target_pairs={{0,8},{8,0},{16,24},{24,16},{32,40},{40,32},{48,56},{56,48},{1,9},... | collective-permute-start | bytes 1572872 | tf_op jit(solution)/shard_map/ppermute | solution.py:221
  60.2 38.1 %copy-start.1 = (bf16[1,256,128]{2,1,0:T(8,128)(2,1)S(1)}, bf16[1,256,128]{2,1,0:T(8,128)(2,1)}, u32[]{:S(2)}) copy-start(bf16[1,256,128]{2,1,0:T(8,128)(2,1)} %param.12) | copy-start | bytes 196612
  60.2 38.2 %copy-start.2 = (bf16[1,256,128]{2,1,0:T(8,128)(2,1)S(1)}, bf16[1,256,128]{2,1,0:T(8,128)(2,1)}, u32[]{:S(2)}) copy-start(bf16[1,256,128]{2,1,0:T(8,128)(2,1)} %param.13) | copy-start | bytes 196612
  60.2 48.2 %copy-start.3 = (s32[128,8]{0,1:T(8,128)S(1)}, s32[128,8]{0,1:T(8,128)}, u32[]{:S(2)}) copy-start(s32[128,8]{0,1:T(8,128)} %param.8) | copy-start | bytes 12292
  60.2 48.2 %copy-start.4 = (s32[128,8]{0,1:T(8,128)S(1)}, s32[128,8]{0,1:T(8,128)}, u32[]{:S(2)}) copy-start(s32[128,8]{0,1:T(8,128)} %param.9) | copy-start | bytes 12292
  60.2 15.5 %collective-permute-start.1 = (f32[640,128]{1,0:T(8,128)}, f32[640,128]{1,0:T(8,128)S(1)}, u32[]{:S(2)}, u32[]{:S(2)}) collective-permute-start(f32[640,128]{1,0:T(8,128)} %get-tuple-element.20.right_ref), channel_id=1, source_target_pairs={{0,8},{8,16},{16,24},{24,32},{32,40},{40,48},{48,56},{56,0},{1,9},... | collective-permute-start | bytes 983048 | tf_op jit(solution)/shard_map/ppermute | solution.py:248
  63.6 12.1 %collective-permute-start.2 = (f32[640,128]{1,0:T(8,128)}, f32[640,128]{1,0:T(8,128)S(1)}, u32[]{:S(2)}, u32[]{:S(2)}) collective-permute-start(f32[640,128]{1,0:T(8,128)} %get-tuple-element.21.left_ref), channel_id=1, source_target_pairs={{0,56},{8,0},{16,8},{24,16},{32,24},{40,32},{48,40},{56,48},{1,57}... | collective-permute-start | bytes 983048 | tf_op jit(solution)/shard_map/ppermute | solution.py:248
  69.4 17.5 %all-to-all-start.1 = ((f32[16,1,128]{2,1,0:T(1,128)}), f32[16,1,128]{2,1,0:T(1,128)S(1)}, u32[]{:S(2)}, u32[]{:S(2)}) async-start(f32[16,1,128]{2,1,0:T(1,128)} %shard_map.96), calls=%async_computation.1 | async-start | bytes 16384 | tf_op jit(solution)/shard_map/all_to_all | solution.py:253
  75.7 22.6 %collective-permute-start.3 = (f32[256,128]{1,0:T(8,128)S(1)}, f32[256,128]{1,0:T(8,128)S(1)}, u32[]{:S(2)}, u32[]{:S(2)}) collective-permute-start(f32[256,128]{1,0:T(8,128)S(1)} %get-tuple-element.25), channel_id=1, source_target_pairs={{0,40},{8,48},{16,56},{24,0},{32,8},{40,16},{48,24},{56,32},{1,41}... | collective-permute-start | bytes 393224 | tf_op jit(solution)/shard_map/ppermute | solution.py:248
  80.7 17.6 %collective-permute-start.4 = (f32[256,128]{1,0:T(8,128)S(1)}, f32[256,128]{1,0:T(8,128)S(1)}, u32[]{:S(2)}, u32[]{:S(2)}) collective-permute-start(f32[256,128]{1,0:T(8,128)S(1)} %get-tuple-element.26), channel_id=1, source_target_pairs={{0,24},{8,32},{16,40},{24,48},{32,56},{40,0},{48,8},{56,16},{1,25}... | collective-permute-start | bytes 393224 | tf_op jit(solution)/shard_map/ppermute | solution.py:248
  87.5 20.9 %all-to-all-start.2 = ((f32[64,2,128]{2,1,0:T(2,128)}), f32[64,2,128]{2,1,0:T(2,128)S(1)}, u32[]{:S(2)}, u32[]{:S(2)}) async-start(f32[64,2,128]{2,1,0:T(2,128)} %shard_map.97), calls=%async_computation.2 | async-start | bytes 131072 | tf_op jit(solution)/shard_map/all_to_all | solution.py:261
